TPU v7x, 32 devices: a whole 2x2x4 slice. The times are simulated.
32 devices in a mesh: blk: 4 (over y, x), rows: 8 (over z, core).
Axes of the slice: x: 2, y: 2, z: 4, core: 2. Of those that a mesh axis runs over, the one named last changes fastest.
Arguments:
- tokens: bfloat16 [24, 1024, 768], P('rows', 'blk'), may hold values from -6 to 6
- timesteps: int32 [24], P('rows'), may hold values from 0 to 63
- lengths: int32 [24, 8], P('rows'), may hold values from 1 to 1017, as said below
- time_table: bfloat16 [64, 128], replicated, may hold values from -6 to 6
- w_ada: bfloat16 [128, 4608], replicated, may hold values from -0.5 to 0.5
- b_ada: bfloat16 [4608], replicated, may hold values from -3 to 3
- gain_attn: bfloat16 [768], replicated, may hold values from 0.25 to 1.75
- w_qkv: bfloat16 [768, 2304], replicated, may hold values from -0.21875 to 0.21875
- w_out: bfloat16 [768, 768], replicated, may hold values from -0.875 to 0.875
- gain_mlp: bfloat16 [768], replicated, may hold values from 0.25 to 1.75
- w_up: bfloat16 [768, 3072], replicated, may hold values from -0.21875 to 0.21875
- b_up: bfloat16 [3072], replicated, may hold values from -3 to 3
- w_down: bfloat16 [3072, 768], replicated, may hold values from -0.109375 to 0.109375
- b_down: bfloat16 [768], replicated, may hold values from -2 to 2
- grad_out: bfloat16 [24, 1024, 768], P('rows', 'blk'), may hold values from -6 to 6
Outputs:
- out: bfloat16 [24, 1024, 768], P('rows', 'blk')
- grad_tokens: bfloat16 [24, 1024, 768], P('rows', 'blk')
- grad_time_table: float32 [64, 128], replicated
- grad_w_ada: float32 [128, 4608], P('rows')
- grad_b_ada: float32 [4608], replicated
- grad_gain_attn: float32 [768], replicated
- grad_w_qkv: float32 [768, 2304], P('rows')
- grad_w_out: float32 [768, 768], P('rows')
- grad_gain_mlp: float32 [768], replicated
- grad_w_up: float32 [768, 3072], P('rows')
- grad_b_up: float32 [3072], replicated
- grad_w_down: float32 [3072, 768], P('rows')
- grad_b_down: float32 [768], replicated
Inputs may be any that keep to these rules, and one draw needn't show every extreme that they name: Each row's 8 lengths are positive and sum to 1024.
All inputs are finite; a program needn't handle non-finite values.
Results may differ from a plain program's by a relative error of at most 0.01505.
The roundings to bfloat16 on the way count: a program that leaves them out, or rounds other values in their place, can miss the bound.
Values may be sent and summed in bfloat16 or wider, within the bound.
A program may use at most 256 MiB of HBM per device.

v0:
```python
import math

import jax
import jax.numpy as jnp
from jax import lax
from jax.sharding import PartitionSpec as P

H = 12


epsilon = 1e-05
highest = lax.Precision.HIGHEST


def norm_rows(values):
    centre = jnp.mean(values, axis=-1, keepdims=True)
    centred = values - centre
    spread = jnp.mean(centred * centred, axis=-1, keepdims=True)
    inverse = lax.rsqrt(spread + epsilon)
    return (centred * inverse, inverse)


def norm_back(grad_normed, normed, inverse):
    first = jnp.mean(grad_normed, axis=-1, keepdims=True)
    second = jnp.mean(grad_normed * normed, axis=-1, keepdims=True)
    return inverse * (grad_normed - first - normed * second)


def doc_layout(lengths, slots):
    ends = jnp.cumsum(lengths, axis=-1)
    before = ends[:, None, :] <= slots[None, :, None]
    doc_ids = jnp.sum(before.astype(jnp.int32), axis=-1)
    begins = jnp.max(jnp.where(before, ends[:, None, :], 0), axis=-1)
    return (doc_ids, slots[None, :] - begins)


def turn_tables(place, head_dim):
    freqs = 10000.0 ** (-jnp.arange(head_dim // 2, dtype=jnp.float32) * 2.0 / head_dim)
    angle = place.astype(jnp.float32)[..., None] * freqs
    return (jnp.cos(angle)[:, :, None, :], jnp.sin(angle)[:, :, None, :])


def rotate(values, cosine, sine):
    half = values.shape[-1] // 2
    first = values[..., :half]
    second = values[..., half:]
    return jnp.concatenate(
        [first * cosine - second * sine, second * cosine + first * sine], axis=-1
    )


def rotate_back(grads, cosine, sine):
    half = grads.shape[-1] // 2
    first = grads[..., :half]
    second = grads[..., half:]
    return jnp.concatenate(
        [first * cosine + second * sine, second * cosine - first * sine], axis=-1
    )


def to_blocks(whole, nblocks, block):
    shape = whole.shape
    split = whole.reshape((shape[0], nblocks, block) + shape[2:])
    order = (1, 0) + tuple(range(2, split.ndim))
    return jnp.transpose(split, order)


def per_device(
    tokens,
    timesteps,
    lengths,
    time_table,
    w_ada,
    b_ada,
    gain_attn,
    w_qkv,
    w_out,
    gain_mlp,
    w_up,
    b_up,
    w_down,
    b_down,
    grad_out,
):
    rows_dev, stretch, width = tokens.shape
    heads = H
    head_dim = width // heads
    seq_len = stretch * lax.axis_size("blk")
    tok_count = rows_dev * stretch
    scale = 1.0 / math.sqrt(head_dim)
    my_slots = lax.axis_index("blk") * stretch + jnp.arange(stretch, dtype=jnp.int32)
    query_doc, place = doc_layout(lengths, my_slots)
    cosine, sine = turn_tables(place, head_dim)
    onehot = (
        timesteps[:, None] == jnp.arange(time_table.shape[0], dtype=jnp.int32)[None, :]
    ).astype(jnp.float32)
    cond = jnp.dot(onehot, time_table.astype(jnp.float32), precision=highest)
    cond_act = jax.nn.silu(cond)
    ada_full = w_ada.astype(jnp.float32)
    modulate = jnp.dot(cond_act, ada_full, precision=highest) + b_ada.astype(jnp.float32)
    shift_a, scale_a, gate_a, shift_m, scale_m, gate_m = jnp.split(modulate[:, None, :], 6, axis=-1)
    gain_a = gain_attn.astype(jnp.float32)
    gain_m = gain_mlp.astype(jnp.float32)
    inputs = tokens.astype(jnp.float32)
    normed_a, inverse_a = norm_rows(inputs)
    factor_a = gain_a * (1.0 + scale_a)
    hidden_a = (normed_a * factor_a + shift_a).astype(jnp.bfloat16).reshape(tok_count, width)
    projected = jnp.dot(hidden_a, w_qkv, preferred_element_type=jnp.float32)
    projected = projected.reshape(rows_dev, stretch, 3, heads, head_dim)
    queries = rotate(projected[:, :, 0], cosine, sine).astype(jnp.bfloat16)
    keys_rot = rotate(projected[:, :, 1], cosine, sine).astype(jnp.bfloat16)
    values_b = projected[:, :, 2].astype(jnp.bfloat16)
    key_flat = keys_rot.reshape(rows_dev, stretch, width)
    value_flat = values_b.reshape(rows_dev, stretch, width)
    piece_k = lax.all_gather(key_flat, "blk", axis=1, tiled=True)
    piece_v = lax.all_gather(value_flat, "blk", axis=1, tiled=True)
    count = piece_k.shape[1]
    key_doc, unused = doc_layout(lengths, jnp.arange(count, dtype=jnp.int32))
    top_in = jnp.full((rows_dev, heads, stretch), -1e30, jnp.float32)
    keys4 = piece_k.reshape(rows_dev, count, heads, head_dim)
    vals4 = piece_v.reshape(rows_dev, count, heads, head_dim)
    raw = jnp.einsum("rqhd,rkhd->rhqk", queries, keys4, preferred_element_type=jnp.float32)
    same = (query_doc[:, :, None] == key_doc[:, None, :])[:, None]
    score = jnp.where(same, raw * scale, -1e30)
    new_top = jnp.maximum(top_in, jnp.max(score, axis=-1))
    weight = jnp.where(same, jnp.exp(score - new_top[..., None]), 0.0)
    new_total = jnp.sum(weight, axis=-1)
    mixed = jnp.einsum(
        "rhqk,rkhd->rhqd", weight.astype(jnp.bfloat16), vals4, preferred_element_type=jnp.float32
    )
    log_total = new_top + jnp.log(new_total)
    attended = jnp.transpose(mixed / new_total[..., None], (0, 2, 1, 3))
    attended_b = attended.astype(jnp.bfloat16).reshape(tok_count, width)
    branch_a = jnp.dot(attended_b, w_out, preferred_element_type=jnp.float32).reshape(
        rows_dev, stretch, width
    )
    middle = inputs + gate_a * branch_a
    normed_m, inverse_m = norm_rows(middle)
    factor_m = gain_m * (1.0 + scale_m)
    hidden_m = (normed_m * factor_m + shift_m).astype(jnp.bfloat16).reshape(tok_count, width)
    pre = jnp.dot(hidden_m, w_up, preferred_element_type=jnp.float32) + b_up.astype(jnp.float32)
    gelu_value, gelu_pull = jax.vjp(lambda values: jax.nn.gelu(values, approximate=True), pre)
    active = gelu_value.astype(jnp.bfloat16)
    branch_m = (
        jnp.dot(active, w_down, preferred_element_type=jnp.float32) + b_down.astype(jnp.float32)
    ).reshape(rows_dev, stretch, width)
    result = (middle + gate_m * branch_m).astype(jnp.bfloat16)
    grad = grad_out.astype(jnp.float32)
    grad_branch = (gate_m * grad).astype(jnp.bfloat16).reshape(tok_count, width)
    grad_w_down = jnp.einsum("tf,td->fd", active, grad_branch, preferred_element_type=jnp.float32)
    grad_b_down = jnp.sum(grad_branch.astype(jnp.float32), axis=0)
    dgate_m = jnp.sum(grad * branch_m, axis=1, keepdims=True)
    grad_active = jnp.einsum("td,fd->tf", grad_branch, w_down, preferred_element_type=jnp.float32)
    grad_pre = gelu_pull(grad_active)[0].astype(jnp.bfloat16)
    grad_w_up = jnp.einsum("td,tf->df", hidden_m, grad_pre, preferred_element_type=jnp.float32)
    grad_b_up = jnp.sum(grad_pre.astype(jnp.float32), axis=0)
    grad_hm = jnp.einsum("tf,df->td", grad_pre, w_up, preferred_element_type=jnp.float32).reshape(
        rows_dev, stretch, width
    )
    grad_gain_m = jnp.sum(grad_hm * normed_m * (1.0 + scale_m), axis=(0, 1))
    dshift_m = jnp.sum(grad_hm, axis=1, keepdims=True)
    dscale_m = jnp.sum(grad_hm * normed_m, axis=1, keepdims=True) * gain_m
    grad_mid = grad + norm_back(grad_hm * factor_m, normed_m, inverse_m)
    dgate_a = jnp.sum(grad_mid * branch_a, axis=1, keepdims=True)
    grad_ya = (gate_a * grad_mid).astype(jnp.bfloat16).reshape(tok_count, width)
    grad_w_out = jnp.einsum("td,te->de", attended_b, grad_ya, preferred_element_type=jnp.float32)
    grad_att = jnp.einsum("te,de->td", grad_ya, w_out, preferred_element_type=jnp.float32).astype(
        jnp.bfloat16
    )
    grad_att = grad_att.reshape(rows_dev, stretch, heads, head_dim)
    delta = jnp.transpose(jnp.sum(grad_att.astype(jnp.float32) * attended, axis=-1), (0, 2, 1))
    whole_k, whole_v = (
        lax.all_gather(key_flat, "blk", axis=1, tiled=True),
        lax.all_gather(value_flat, "blk", axis=1, tiled=True),
    )
    block = min(512, seq_len)
    nblocks = seq_len // block
    key_blocks = to_blocks(whole_k.reshape(rows_dev, seq_len, heads, head_dim), nblocks, block)
    value_blocks = to_blocks(whole_v.reshape(rows_dev, seq_len, heads, head_dim), nblocks, block)
    block_starts = jnp.arange(nblocks, dtype=jnp.int32) * block
    zero_grads = jnp.zeros((rows_dev, stretch, heads, head_dim), jnp.float32)

    def back_block(grad_q, inputs_block):
        keys4, vals4, begin = inputs_block
        key_doc, unused = doc_layout(lengths, begin + jnp.arange(block, dtype=jnp.int32))
        raw = jnp.einsum("rqhd,rkhd->rhqk", queries, keys4, preferred_element_type=jnp.float32)
        same = (query_doc[:, :, None] == key_doc[:, None, :])[:, None]
        prob = jnp.where(same, jnp.exp(raw * scale - log_total[..., None]), 0.0)
        grad_v = jnp.einsum(
            "rhqk,rqhd->rkhd",
            prob.astype(jnp.bfloat16),
            grad_att,
            preferred_element_type=jnp.float32,
        )
        grad_p = jnp.einsum("rqhd,rkhd->rhqk", grad_att, vals4, preferred_element_type=jnp.float32)
        grad_s = (prob * (grad_p - delta[..., None]) * scale).astype(jnp.bfloat16)
        added = jnp.einsum("rhqk,rkhd->rqhd", grad_s, keys4, preferred_element_type=jnp.float32)
        grad_k = jnp.einsum("rhqk,rqhd->rkhd", grad_s, queries, preferred_element_type=jnp.float32)
        paired = jnp.concatenate(
            [grad_k.reshape(rows_dev, block, width), grad_v.reshape(rows_dev, block, width)],
            axis=-1,
        )
        return (grad_q + added, paired)

    grad_q, paired_blocks = lax.scan(
        back_block, zero_grads, (key_blocks, value_blocks, block_starts)
    )
    paired_rows = jnp.transpose(paired_blocks, (1, 0, 2, 3)).reshape(rows_dev, seq_len, 2 * width)
    summed = lax.psum_scatter(
        paired_rows.astype(jnp.bfloat16), "blk", scatter_dimension=1, tiled=True
    ).astype(jnp.float32)
    grad_k_rot = summed[..., :width].reshape(rows_dev, stretch, heads, head_dim)
    grad_vals = summed[..., width:].reshape(rows_dev, stretch, heads, head_dim)
    grad_qkv = jnp.stack(
        [rotate_back(grad_q, cosine, sine), rotate_back(grad_k_rot, cosine, sine), grad_vals],
        axis=2,
    )
    grad_qkv = grad_qkv.astype(jnp.bfloat16).reshape(tok_count, 3 * width)
    grad_w_qkv = jnp.einsum("td,te->de", hidden_a, grad_qkv, preferred_element_type=jnp.float32)
    grad_ha = jnp.einsum("te,de->td", grad_qkv, w_qkv, preferred_element_type=jnp.float32).reshape(
        rows_dev, stretch, width
    )
    grad_gain_a = jnp.sum(grad_ha * normed_a * (1.0 + scale_a), axis=(0, 1))
    dshift_a = jnp.sum(grad_ha, axis=1, keepdims=True)
    dscale_a = jnp.sum(grad_ha * normed_a, axis=1, keepdims=True) * gain_a
    grad_in = (grad_mid + norm_back(grad_ha * factor_a, normed_a, inverse_a)).astype(jnp.bfloat16)
    grad_mod = jnp.concatenate([dshift_a, dscale_a, dgate_a, dshift_m, dscale_m, dgate_m], axis=-1)[
        :, 0, :
    ]
    grad_w_ada = jnp.dot(cond_act.T, grad_mod, precision=highest)
    grad_b_ada = jnp.sum(grad_mod, axis=0)
    grad_cond_act = jnp.dot(grad_mod, ada_full.T, precision=highest)
    sigmoid = jax.nn.sigmoid(cond)
    grad_cond = grad_cond_act * sigmoid * (1.0 + cond * (1.0 - sigmoid))
    grad_table = jnp.dot(onehot.T, grad_cond, precision=highest)
    shares = (
        lax.psum_scatter(grad_w_ada, "rows", scatter_dimension=0, tiled=True),
        lax.psum_scatter(grad_w_qkv, "rows", scatter_dimension=0, tiled=True),
        lax.psum_scatter(grad_w_out, "rows", scatter_dimension=0, tiled=True),
        lax.psum_scatter(grad_w_up, "rows", scatter_dimension=0, tiled=True),
        lax.psum_scatter(grad_w_down, "rows", scatter_dimension=0, tiled=True),
    )
    matrices = (
        lax.psum(shares[0].astype(jnp.bfloat16), "blk").astype(jnp.float32),
        lax.psum(shares[1].astype(jnp.bfloat16), "blk").astype(jnp.float32),
        lax.psum(shares[2].astype(jnp.bfloat16), "blk").astype(jnp.float32),
        lax.psum(shares[3].astype(jnp.bfloat16), "blk").astype(jnp.float32),
        lax.psum(shares[4].astype(jnp.bfloat16), "blk").astype(jnp.float32),
    )
    smalls = lax.psum(
        (grad_table, grad_b_ada, grad_gain_a, grad_gain_m, grad_b_up, grad_b_down), ("blk", "rows")
    )
    return (
        result,
        grad_in,
        smalls[0],
        matrices[0],
        smalls[1],
        smalls[2],
        matrices[1],
        matrices[2],
        smalls[3],
        matrices[3],
        smalls[4],
        matrices[4],
        smalls[5],
    )


def solution(mesh):
    placed = (
        P("rows", "blk", None),
        P("rows"),
        P("rows", None),
        P(),
        P(),
        P(),
        P(),
        P(),
        P(),
        P(),
        P(),
        P(),
        P(),
        P(),
        P("rows", "blk", None),
    )
    return jax.shard_map(
        per_device,
        mesh=mesh,
        in_specs=placed,
        out_specs=(
            P("rows", "blk", None),
            P("rows", "blk", None),
            P(),
            P("rows", None),
            P(),
            P(),
            P("rows", None),
            P("rows", None),
            P(),
            P("rows", None),
            P(),
            P("rows", None),
            P(),
        ),
        check_vma=False,
    )
```

profile of v0, /device:TPU:0, one launch (start us, length us, event | category | flops | bytes accessed | tf_op | source)
XLA Modules:
  0.0 1076.1 jit_solution(4651269795503194278)
XLA Ops:
  15.7 5.9 copy.55
  47.5 52.0 %all-gather.3.cloned.1.call-done = bf16[3,1024,768]{1,2,0:T(8,128)(2,1)} async-done(((bf16[3,256,768]{1,2,0:T(8,128)(2,1)}), bf16[3,1024,768]{1,2,0:T(8,128)(2,1)}) %all-gather.3.cloned.1.call-update) | async-done | bytes 4718608 | tf_op jit(solution)/shard_map/all_gather | solution.py:115
  99.5 8.9 reshape_reshape.6
  108.4 6.1 copy.60
  114.4 44.4 %all-gather.5.cloned.1.call-done = bf16[3,1024,768]{1,2,0:T(8,128)(2,1)} async-done(((bf16[3,256,768]{1,2,0:T(8,128)(2,1)}), bf16[3,1024,768]{1,2,0:T(8,128)(2,1)}) %all-gather.5.cloned.1.call-update) | async-done | bytes 4718608 | tf_op jit(solution)/shard_map/all_gather | solution.py:116
  158.9 8.8 reshape_reshape.7
  173.4 17.9 %fusion.24 = (f32[3,12,256]{2,1,0:T(8,128)S(1)}, f32[3,12,256,1024]{3,2,1,0:T(8,128)}) fusion(pred[3,256,1024]{2,1,0:T(8,128)(4,1)S(1)} %copy-done.13, bf16[3,1024,12,64]{1,3,2,0:T(8,128)(2,1)} %bitcast.216, bf16[3,256,12,32]{1,3,2,0:T(8,128)(2,1)} %get-tuple-element.278, bf16[3,256,12,32]{1,3,2,0:T(8,128)(2,1)S(1)} %copy-done.14), kind=kOutput, calls=%fused_computation.31 | convolution fusion | flops 1238621184 | bytes 44470272 | tf_op jit(solution)/shard_map/rqhd,rkhd->rhqk/dot_general | solution.py:122
  191.3 18.3 %fusion.25 = f32[3,12,256]{2,1,0:T(8,128)S(1)} fusion(f32[3,12,256,1024]{3,2,1,0:T(8,128)} %get-tuple-element.300, f32[3,12,256]{2,1,0:T(8,128)S(1)} %broadcast_maximum_fusion, pred[3,256,1024]{2,1,0:T(8,128)(4,1)S(1)} %copy-done.13), kind=kLoop, calls=%fused_computation.32 | loop fusion | flops 47176704 | bytes 38608896 | tf_op jit(solution)/shard_map/reduce_sum | solution.py:127
  210.3 18.2 %fusion.89 = (bf16[3,256,12,64]{1,3,2,0:T(8,128)(2,1)S(1)}, f32[3,256,12,64]{1,3,2,0:T(8,128)}) fusion(f32[3,256,12]{1,2,0:T(8,128)S(1)} %bitcast.242, bf16[3,1024,12,64]{1,3,2,0:T(8,128)(2,1)} %bitcast.226, f32[3,12,256,1024]{3,2,1,0:T(8,128)} %get-tuple-element.300, f32[3,12,256]{2,1,0:T(8,128)S(1)} %broadcast_maximum_fusion, ...), kind=kOutput, calls=%fused_computation.172 | convolution fusion | flops 1256325120 | bytes 46866432 | tf_op jit(solution)/shard_map/rhqk,rkhd->rhqd/dot_general | solution.py:128
  233.7 5.7 fusion.91
  239.6 7.3 convolution_add_fusion.1
  246.8 12.6 %convert_reduce_fusion.1 = (f32[3072]{0:T(1024)}, bf16[768,3072]{1,0:T(8,128)(2,1)S(1)}) fusion(f32[768,3072]{1,0:T(8,128)} %copy-done.78, f32[3072]{0:T(1024)S(1)} %copy-done.68, bf16[768,768]{1,0:T(8,128)(2,1)S(1)} %bitcast.237, bf16[3072,768]{1,0:T(8,128)(2,1)S(1)} %bitcast.249), kind=kOutput, calls=%fused_computation.45 | convolution fusion | flops 3678139392 | bytes 20078592 | tf_op jit(solution)/shard_map/td,fd->tf/dot_general | solution.py:153
  289.0 121.6 %while.15 = (s32[]{:T(128)}, f32[3,256,12,64]{1,3,2,0:T(8,128)}, bf16[2,3,512,1536]{3,2,0,1:T(8,128)(2,1)}, bf16[2,3,512,12,64]{2,4,3,1,0:T(8,128)(2,1)}, s32[3,...) while((s32[]{:T(128)}, f32[3,256,12,64]{1,3,2,0:T(8,128)}, ...), condition=%wide.region_15.16_spmd.clone, body=%wide.region_13.15_spmd.clone.sunk | while | flops 3082849280 | bytes 154664352 | solution.py:205
  290.9 10.7 fusion.150
  301.7 10.2 fusion.152
  311.9 10.8 %fusion.151 = bf16[3,12,256,512]{2,3,1,0:T(8,128)(2,1)S(1)} fusion(f32[3,12,512,256]{3,2,1,0:T(8,128)} %fusion.150, f32[3,12,256]{2,1,0:T(8,128)S(1)} %get-tuple-element.420, f32[3,12,256]{2,1,0:T(8,128)S(1)} %get-tuple-element.417, pred[3,256,512]{1,2,0:T(8,128)(4,1)S(1)} %broadcast_compare_fusion.3, bf16[3,256,12,64]{1,3,2,0:T(8,128)(2,1)} %copy-done.19, ...), kind=kOutput, calls=%fused_computation.2.clone.1 | convolution fusion | flops 637009920 | bytes 32317444 | tf_op jit(solution)/shard_map/while/body/eval_jaxpr/rqhd,rkhd->rhqk/dot_general | solution.py:195
  337.8 6.6 copy.105
  351.2 10.8 fusion.150
  361.9 10.2 fusion.152
  372.2 10.8 %fusion.151 = bf16[3,12,256,512]{2,3,1,0:T(8,128)(2,1)S(1)} fusion(f32[3,12,512,256]{3,2,1,0:T(8,128)} %fusion.150, f32[3,12,256]{2,1,0:T(8,128)S(1)} %get-tuple-element.420, f32[3,12,256]{2,1,0:T(8,128)S(1)} %get-tuple-element.417, pred[3,256,512]{1,2,0:T(8,128)(4,1)S(1)} %broadcast_compare_fusion.3, bf16[3,256,12,64]{1,3,2,0:T(8,128)(2,1)} %copy-done.19, ...), kind=kOutput, calls=%fused_computation.2.clone.1 | convolution fusion | flops 637009920 | bytes 32317444 | tf_op jit(solution)/shard_map/while/body/eval_jaxpr/rqhd,rkhd->rhqk/dot_general | solution.py:195
  398.8 6.6 copy.105
  416.9 13.6 %fusion.85 = f32[3072,768]{1,0:T(8,128)} fusion(bf16[768,768]{1,0:T(8,128)(2,1)S(1)} %bitcast.238, f32[768,3072]{1,0:T(8,128)} %copy-done.78, f32[3072]{0:T(1024)S(1)} %copy-done.69), kind=kOutput, calls=%fused_computation.170 | convolution fusion | flops 3647471616 | bytes 20066304 | tf_op jit(solution)/shard_map/tf,td->fd/dot_general | solution.py:150
  431.8 8.8 fusion.94
  440.7 65.0 %reduce-scatter.7.cloned.1.call-done = bf16[3,256,1536]{2,1,0:T(8,128)(2,1)} async-done(((bf16[3,1024,1536]{2,1,0:T(8,128)(2,1)}), bf16[3,256,1536]{2,1,0:T(8,128)(2,1)}) %reduce-scatter.7.cloned.1.call-update) | async-done | bytes 2359312 | tf_op jit(solution)/shard_map/reduce_scatter | solution.py:209
  518.4 5.7 multiply_reduce_fusion.1
  538.3 5.9 reduce-scatter.13.cloned.1.call-done
  545.8 99.3 %reduce-scatter.17.cloned.1.call-done = f32[384,768]{1,0:T(8,128)} async-done(((f32[3072,768]{1,0:T(8,128)}), f32[384,768]{1,0:T(8,128)}) %reduce-scatter.17.cloned.1.call-update) | async-done | bytes 1179664 | tf_op jit(solution)/shard_map/reduce_scatter | solution.py:241
  647.3 97.9 %reduce-scatter.15.cloned.1.call-done = f32[96,3072]{1,0:T(8,128)} async-done(((f32[768,3072]{1,0:T(8,128)}), f32[96,3072]{1,0:T(8,128)}) %reduce-scatter.15.cloned.1.call-update) | async-done | bytes 1179664 | tf_op jit(solution)/shard_map/reduce_scatter | solution.py:240
  747.3 34.8 %reduce-scatter.9.cloned.1.call-done = f32[16,4608]{1,0:T(8,128)} async-done(((f32[128,4608]{1,0:T(8,128)}), f32[16,4608]{1,0:T(8,128)}) %reduce-scatter.9.cloned.1.call-update) | async-done | bytes 294928 | tf_op jit(solution)/shard_map/reduce_scatter | solution.py:237
  783.8 77.1 %reduce-scatter.11.cloned.1.call-done = f32[96,2304]{1,0:T(8,128)} async-done(((f32[768,2304]{1,0:T(8,128)}), f32[96,2304]{1,0:T(8,128)}) %reduce-scatter.11.cloned.1.call-update) | async-done | bytes 884752 | tf_op jit(solution)/shard_map/reduce_scatter | solution.py:238
  874.0 57.9 %all-reduce.7.cloned.1.call-done = (bf16[16,4608]{1,0:T(8,128)(2,1)}, bf16[96,2304]{1,0:T(8,128)(2,1)}, bf16[96,768]{1,0:T(8,128)(2,1)}, bf16[96,3072]{1,0:T(8,128)(2,1)}, bf16[384,768]{1,0:T(8,128)(2,1)}) async-done(((bf16[16,4608]{1,0:T(8,128)(2,1)}, bf16[96,2304]{1,0:T(8,128)(2,1)}, bf16[96,768]{1,0:T(8,128)(2,1)}, bf16[96,3072]{1,0:T(8,128)(2,1)}, bf16[384,768]{1,0:T(8,128)(2,1)}), ...) | async-done | bytes 1916944 | tf_op jit(solution)/shard_map/psum | solution.py:244
  939.6 121.6 %all-reduce.5.cloned.1.call-done = (f32[64,128]{1,0:T(8,128)}, f32[4608]{0:T(1024)}, f32[768]{0:T(1024)}, f32[768]{0:T(1024)}, f32[3072]{0:T(1024)}, /*index=5*/f32[768]{0:T(1024)}) async-done(((f32[64,128]{1,0:T(8,128)}, f32[4608]{0:T(1024)}, f32[768]{0:T(1024)}, f32[768]{0:T(1024)}, f32[3072]{0:T(1024)}, /*index=5*/f32[768]{0:T(1024)}), (f32[64,128]{1,0:T(8,128)}, f32[4608]{0:T(1024)}, f32[768]{0:T(1024)}, ...) | async-done | bytes 72720 | tf_op jit(solution)/shard_map/psum | solution.py:250
  (306 shorter events, 189.8 us)
Async XLA Ops:
  7.2 221.3 %copy-start = (bf16[768,768]{1,0:T(8,128)(2,1)S(1)}, bf16[768,768]{1,0:T(8,128)(2,1)}, u32[]{:S(2)}) copy-start(bf16[768,768]{1,0:T(8,128)(2,1)} %param.25) | copy-start | bytes 3538948
  7.2 7.0 copy-start.74
  7.2 7.9 copy-start.70
  7.2 92.3 %all-gather.3.cloned.1.call-start = ((), (), s32[]{:S(2)}) async-start(), calls=%async_computation.6 | async-start | bytes 5898240 | tf_op jit(solution)/shard_map/all_gather | solution.py:115
  15.7 10.0 copy-start.7
  15.7 10.0 copy-start.16
  39.7 119.1 %all-gather.5.cloned.1.call-start = ((), (), s32[]{:S(2)}) async-start(), calls=%async_computation.7 | async-start | bytes 5898240 | tf_op jit(solution)/shard_map/all_gather | solution.py:116
  42.7 463.1 %reduce-scatter.7.cloned.1.call-start = ((), (), s32[]{:S(2)}) async-start(), calls=%async_computation.8 | async-start | bytes 11796480 | tf_op jit(solution)/shard_map/reduce_scatter | solution.py:209
  210.3 18.2 %copy-start.46 = (f32[3,768]{1,0:T(4,128)S(1)}, f32[3,768]{1,0:T(4,128)}, u32[]{:S(2)}) copy-start(f32[3,768]{1,0:T(4,128)} %get-tuple-element.296) | copy-start | bytes 27652
  231.6 7.8 copy-start.52
  231.9 7.6 slice-start.1
  239.5 7.3 copy-start.78
  239.5 7.3 copy-start.30
  239.5 19.9 %slice-start.3 = ((s8[4718592]{0:T(1024)(128)(4,1)}), s8[4194304]{0:T(1024)(128)(4,1)S(1)}, s32[]{:S(2)}) async-start(s8[4718592]{0:T(1024)(128)(4,1)} %bitcast.250), calls=%async_computation.19 | async-start | bytes 8388608
  246.8 12.6 %slice-start.4 = ((s8[4718592]{0:T(1024)(128)(4,1)}), s8[524288]{0:T(1024)(128)(4,1)S(1)}, s32[]{:S(2)}) async-start(s8[4718592]{0:T(1024)(128)(4,1)} %bitcast.250), calls=%async_computation.20 | async-start | bytes 1048576
  259.5 11.5 %copy-start.17 = (bf16[3,256,768]{2,1,0:T(8,128)(2,1)S(1)}, bf16[3,256,768]{2,1,0:T(8,128)(2,1)}, u32[]{:S(2)}) copy-start(bf16[3,256,768]{2,1,0:T(8,128)(2,1)} %param.31) | copy-start | bytes 3538948
  271.0 6.5 copy-start.47
  289.2 12.5 %copy-start.2 = (bf16[3,256,12,64]{1,3,2,0:T(8,128)(2,1)}, bf16[3,256,12,64]{1,3,2,0:T(8,128)(2,1)S(1)}, u32[]{:S(2)}) copy-start(bf16[3,256,12,64]{1,3,2,0:T(8,128)(2,1)S(1)} %get-tuple-element.416) | copy-start | bytes 3538948 | tf_op jit(solution)/shard_map/while
  289.2 12.5 %copy-start.19 = (bf16[3,256,12,64]{1,3,2,0:T(8,128)(2,1)}, bf16[3,256,12,64]{1,3,2,0:T(8,128)(2,1)S(1)}, u32[]{:S(2)}) copy-start(bf16[3,256,12,64]{1,3,2,0:T(8,128)(2,1)S(1)} %get-tuple-element.419) | copy-start | bytes 3538948 | tf_op jit(solution)/shard_map/while
  349.4 12.5 %copy-start.2 = (bf16[3,256,12,64]{1,3,2,0:T(8,128)(2,1)}, bf16[3,256,12,64]{1,3,2,0:T(8,128)(2,1)S(1)}, u32[]{:S(2)}) copy-start(bf16[3,256,12,64]{1,3,2,0:T(8,128)(2,1)S(1)} %get-tuple-element.416) | copy-start | bytes 3538948 | tf_op jit(solution)/shard_map/while
  349.4 12.5 %copy-start.19 = (bf16[3,256,12,64]{1,3,2,0:T(8,128)(2,1)}, bf16[3,256,12,64]{1,3,2,0:T(8,128)(2,1)S(1)}, u32[]{:S(2)}) copy-start(bf16[3,256,12,64]{1,3,2,0:T(8,128)(2,1)S(1)} %get-tuple-element.419) | copy-start | bytes 3538948 | tf_op jit(solution)/shard_map/while
  410.6 133.6 %reduce-scatter.13.cloned.1.call-start = ((), (), s32[]{:S(2)}) async-start(), calls=%async_computation.11 | async-start | bytes 2654208 | tf_op jit(solution)/shard_map/reduce_scatter | solution.py:239
  415.7 229.4 %reduce-scatter.17.cloned.1.call-start = ((), (), s32[]{:S(2)}) async-start(), calls=%async_computation.13 | async-start | bytes 10616832 | tf_op jit(solution)/shard_map/reduce_scatter | solution.py:241
  430.6 314.6 %reduce-scatter.15.cloned.1.call-start = ((), (), s32[]{:S(2)}) async-start(), calls=%async_computation.12 | async-start | bytes 10616832 | tf_op jit(solution)/shard_map/reduce_scatter | solution.py:240
  440.7 341.4 %reduce-scatter.9.cloned.1.call-start = ((), (), s32[]{:S(2)}) async-start(), calls=%async_computation.9 | async-start | bytes 2654208 | tf_op jit(solution)/shard_map/reduce_scatter | solution.py:237
  528.3 332.6 %reduce-scatter.11.cloned.1.call-start = ((), (), s32[]{:S(2)}) async-start(), calls=%async_computation.10 | async-start | bytes 7962624 | tf_op jit(solution)/shard_map/reduce_scatter | solution.py:238
  538.2 393.7 %all-reduce.7.cloned.1.call-start = ((), (), s32[]{:S(2)}) async-start(), calls=%async_computation.15 | async-start | bytes 3833856 | tf_op jit(solution)/shard_map/psum | solution.py:244
  783.8 87.2 %copy-start.9 = (bf16[3,256,768]{2,1,0:T(8,128)(2,1)S(1)}, bf16[3,256,768]{2,1,0:T(8,128)(2,1)}, u32[]{:S(2)}) copy-start(bf16[3,256,768]{2,1,0:T(8,128)(2,1)} %param.17) | copy-start | bytes 3538948
  783.8 87.2 %copy-start.11 = (f32[3,256,768]{2,1,0:T(8,128)S(1)}, f32[3,256,768]{2,1,0:T(8,128)}, u32[]{:S(2)}) copy-start(f32[3,256,768]{2,1,0:T(8,128)} %copy-done.10) | copy-start | bytes 7077892
  862.9 198.3 %all-reduce.5.cloned.1.call-start = ((), (), s32[]{:S(2)}) async-start(), calls=%async_computation.14 | async-start | bytes 155648 | tf_op jit(solution)/shard_map/psum | solution.py:250
  931.9 6.6 copy-start.37
  935.3 133.7 %copy-start.1 = (bf16[768,768]{1,0:T(8,128)(2,1)S(1)}, bf16[768,768]{1,0:T(8,128)(2,1)}, u32[]{:S(2)}) copy-start(bf16[768,768]{1,0:T(8,128)(2,1)} %param.25) | copy-start | bytes 3538948
  (66 other events, 220.1 us)
Sparse Core Ops, SparseCore 0:
  39.8 59.6 all-gather.2
  101.9 56.9 all-gather.4
  410.7 94.9 reduce-scatter.6
  507.9 36.2 reduce-scatter.12
  546.3 98.7 reduce-scatter.16
  647.3 97.8 reduce-scatter.14
  747.5 34.5 reduce-scatter.8
  784.4 76.4 reduce-scatter.10
  865.8 66.0 all-reduce.6
  939.3 121.7 all-reduce.4
where the time goes:
time: 1080 us
  waiting for transfers between devices  656 us (61%)
  matrix products  204 us (19%)
  local copies, waits for them, and re-layouts  106 us (10%)
  other arithmetic  92.5 us (9%)
  between operations  15.2 us (1%)
    psum x1, waiting for transfers between devices, per_device(): lax.psum((grad_table, grad_b_ada, grad_gain_a, grad_gain_m, grad_b_up, gr...  122 us
    reduce_scatter x1, waiting for transfers between devices, per_device(): lax.psum_scatter(grad_w_down, 'rows', scatter_dimension=0, tiled=True)  99.3 us
    reduce_scatter x1, waiting for transfers between devices, per_device(): lax.psum_scatter(grad_w_up, 'rows', scatter_dimension=0, tiled=True)  97.9 us
    reduce_scatter x1, waiting for transfers between devices, per_device(): lax.psum_scatter(grad_w_qkv, 'rows', scatter_dimension=0, tiled=True)  77.1 us
    reduce_scatter x1, waiting for transfers between devices, per_device(): lax.psum_scatter(paired_rows.astype(jnp.bfloat16), 'blk', scatter_dimensi...  65 us
    psum x1, waiting for transfers between devices, per_device(): lax.psum(shares[0].astype(jnp.bfloat16), 'blk').astype(jnp.float32)  57.9 us
    all_gather x1, waiting for transfers between devices, per_device(): piece_k = lax.all_gather(key_flat, 'blk', axis=1, tiled=True)  52 us
    unnamed x173, local copies, waits for them, and re-layouts  46.2 us
  transfers between devices with their start and end apart: 10, of which 10 were waited for; matrix products, arithmetic and copies ran while one was open for 9% of the time, Pallas kernels for 0%

commit v1 on v0

v1 whole, which is shorter than its diff:
```python
import functools
import math

import jax
import jax.numpy as jnp
from jax import lax
from jax.experimental import pallas as pl
from jax.experimental.pallas import tpu as pltpu
from jax.sharding import PartitionSpec as P

H = 12
NDOC = 8
LANES = 128
CHUNK = 256
MIB = 1 << 20

epsilon = 1e-05
highest = lax.Precision.HIGHEST
bf16 = jnp.bfloat16
f32 = jnp.float32
MESH = pl.DeviceIdType.MESH


def dot(a, b):
    return jnp.dot(a, b, preferred_element_type=f32)


def dot_nt(a, b):
    return lax.dot_general(a, b, (((1,), (1,)), ((), ())), preferred_element_type=f32)


def dot_tn(a, b):
    return lax.dot_general(a, b, (((0,), (0,)), ((), ())), preferred_element_type=f32)


def norm_rows(values):
    centre = jnp.mean(values, axis=-1, keepdims=True)
    centred = values - centre
    spread = jnp.mean(centred * centred, axis=-1, keepdims=True)
    inverse = lax.rsqrt(spread + epsilon)
    return (centred * inverse, inverse)


def norm_back(grad_normed, normed, inverse):
    first = jnp.mean(grad_normed, axis=-1, keepdims=True)
    second = jnp.mean(grad_normed * normed, axis=-1, keepdims=True)
    return inverse * (grad_normed - first - normed * second)


def lane_of(shape):
    return lax.broadcasted_iota(jnp.int32, shape, len(shape) - 1)


def swap_halves(values, half):
    lane = lane_of(values.shape)
    width = values.shape[-1]
    ahead = pltpu.roll(values, width - half, values.ndim - 1)
    behind = pltpu.roll(values, half, values.ndim - 1)
    return jnp.where(lane % (2 * half) < half, ahead, behind)


def in_three(values):
    high = values.astype(bf16)
    rest = values - high.astype(f32)
    middle = rest.astype(bf16)
    low = (rest - middle.astype(f32)).astype(bf16)
    return (high, middle, low)


def project_kernel(x_ref, factor_ref, shift_ref, w_ref, cos_ref, sin_ref, h_ref, q_ref, k_ref, v_ref):
    normed, unused = norm_rows(x_ref[...].astype(f32))
    hidden = (normed * factor_ref[...] + shift_ref[...]).astype(bf16)
    h_ref[...] = hidden
    width = x_ref.shape[-1]
    half = width // H // 2
    scale = 1.0 / math.sqrt(2 * half)
    cosine, sine = cos_ref[...], sin_ref[...]
    for part in range(3):
        out = dot(hidden, w_ref[:, part * width : (part + 1) * width])
        for group in range(width // LANES):
            cols = slice(group * LANES, (group + 1) * LANES)
            piece = out[:, cols]
            if part == 2:
                v_ref[:, cols] = piece.astype(bf16)
                continue
            turned = (piece * cosine + swap_halves(piece, half) * sine).astype(bf16)
            if part == 0:
                q_ref[:, cols] = (turned.astype(f32) * scale).astype(bf16)
            else:
                k_ref[:, cols] = turned


def project(x, factor, shift, w_qkv, cosine, sine):
    seq, width = x.shape
    rows = lambda cols: pl.BlockSpec((CHUNK, cols), lambda i: (i, 0))
    fixed = lambda shape: pl.BlockSpec(shape, lambda i: (0, 0))
    return pl.pallas_call(
        project_kernel,
        grid=(seq // CHUNK,),
        in_specs=[
            rows(width),
            fixed((1, width)),
            fixed((1, width)),
            fixed(w_qkv.shape),
            rows(LANES),
            rows(LANES),
        ],
        out_specs=[rows(width)] * 4,
        out_shape=[jax.ShapeDtypeStruct((seq, width), bf16)] * 4,
        compiler_params=pltpu.CompilerParams(vmem_limit_bytes=40 * MIB),
        cost_estimate=pl.CostEstimate(
            flops=2 * seq * width * 3 * width, bytes_accessed=12 * seq * width, transcendentals=0
        ),
    )(x, factor, shift, w_qkv, cosine, sine)


def attend_kernel(q_ref, k_ref, v_ref, fq_ref, fk_ref, att_ref, lse_ref):
    seq = q_ref.shape[0]
    first = lane_of((1, LANES)) < LANES // 2
    one = jnp.ones((), bf16)
    for begin in range(0, seq, CHUNK):
        rows = slice(begin, begin + CHUNK)
        pieces = []
        for head in range(2):
            own = first if head == 0 else jnp.logical_not(first)
            keys = jnp.where(own, k_ref[...], fk_ref[...])
            values = jnp.where(own, v_ref[...], one)
            queries = jnp.where(own, q_ref[rows, :], fq_ref[rows, :])
            score = dot_nt(queries, keys)
            top = jnp.max(score, axis=-1, keepdims=True)
            weight = jnp.exp(score - top).astype(bf16)
            mixed = dot(weight, values)
            pieces.append((mixed / pltpu.roll(mixed, LANES // 2, 1), top + jnp.log(mixed)))
        att_ref[rows, :] = jnp.where(first, pieces[0][0], pieces[1][0])
        lse_ref[rows, :] = jnp.where(first, pieces[1][1], pieces[0][1])


def attend(q, k, v, fq, fk):
    seq, width = q.shape
    pair = pl.BlockSpec((seq, LANES), lambda i: (0, i))
    fixed = pl.BlockSpec((seq, LANES), lambda i: (0, 0))
    return pl.pallas_call(
        attend_kernel,
        grid=(width // LANES,),
        in_specs=[pair, pair, pair, fixed, fixed],
        out_specs=[pair, pair],
        out_shape=[jax.ShapeDtypeStruct((seq, width), f32)] * 2,
        compiler_params=pltpu.CompilerParams(vmem_limit_bytes=40 * MIB),
        cost_estimate=pl.CostEstimate(
            flops=16 * seq * seq * width, bytes_accessed=14 * seq * width, transcendentals=H * seq * seq
        ),
    )(q, k, v, fq, fk)


def attend_back_kernel(
    q_ref, k_ref, v_ref, d_ref, att_ref, lse_ref, fq_ref, fk_ref, cos_ref, sin_ref,
    dq_ref, dk_ref, dv_ref, qa_ref, da_ref, dq_acc
):
    seq = q_ref.shape[0]
    half = LANES // 4
    scale = 1.0 / math.sqrt(2 * half)
    lane = lane_of((1, LANES))
    first = lane < 2 * half
    place = lane % (2 * half)
    one = jnp.ones((), bf16)
    outs = []
    for head in range(2):
        own = first if head == 0 else jnp.logical_not(first)
        lse = in_three(-lse_ref[...])
        feature = fq_ref[...]
        for i in range(3):
            feature = jnp.where(place == NDOC + i, lse[i], feature)
        qa_ref[...] = jnp.where(own, q_ref[...], feature)
        grads = d_ref[...]
        both = jnp.where(own, grads.astype(f32) * att_ref[...], 0.0)
        delta = in_three(jnp.broadcast_to(-jnp.sum(both, axis=-1, keepdims=True), both.shape))
        feature = jnp.zeros_like(grads)
        for i in range(3):
            feature = jnp.where(place == NDOC + i, delta[i], feature)
        da_ref[...] = jnp.where(own, grads, feature)
        pieces = []
        for begin in range(0, seq, CHUNK):
            rows = slice(begin, begin + CHUNK)
            keys = jnp.where(own, k_ref[rows, :], fk_ref[rows, :])
            values = jnp.where(own, v_ref[rows, :], one)
            prob = jnp.exp(dot_nt(keys, qa_ref[...]))
            grad_v = dot(prob.astype(bf16), d_ref[...])
            grad_s = (prob * dot_nt(values, da_ref[...])).astype(bf16)
            grad_k = dot(grad_s, q_ref[...])
            added = dot_tn(grad_s, k_ref[rows, :])
            if begin == 0:
                dq_acc[head] = added
            else:
                dq_acc[head] += added
            pieces.append((grad_k, grad_v))
        outs.append(pieces)
    for step, begin in enumerate(range(0, seq, CHUNK)):
        rows = slice(begin, begin + CHUNK)
        cosine, sine = cos_ref[rows, :], sin_ref[rows, :]
        grad_k = jnp.where(first, outs[0][step][0], outs[1][step][0])
        dk_ref[rows, :] = (grad_k * cosine - swap_halves(grad_k, half) * sine).astype(bf16)
        dv_ref[rows, :] = jnp.where(first, outs[0][step][1], outs[1][step][1]).astype(bf16)
        grad_q = jnp.where(first, dq_acc[0, rows, :], dq_acc[1, rows, :]) * scale
        dq_ref[rows, :] = (grad_q * cosine - swap_halves(grad_q, half) * sine).astype(bf16)


def attend_back(q, k, v, grads, att, lse, fq, fk, cosine, sine):
    seq, width = q.shape
    pair = pl.BlockSpec((seq, LANES), lambda i: (0, i))
    fixed = pl.BlockSpec((seq, LANES), lambda i: (0, 0))
    return pl.pallas_call(
        attend_back_kernel,
        grid=(width // LANES,),
        in_specs=[pair] * 6 + [fixed] * 4,
        out_specs=[pair] * 3,
        out_shape=[jax.ShapeDtypeStruct((seq, width), bf16)] * 3,
        scratch_shapes=[
            pltpu.VMEM((seq, LANES), bf16),
            pltpu.VMEM((seq, LANES), bf16),
            pltpu.VMEM((2, seq, LANES), f32),
        ],
        compiler_params=pltpu.CompilerParams(vmem_limit_bytes=48 * MIB),
        cost_estimate=pl.CostEstimate(
            flops=40 * seq * seq * width, bytes_accessed=24 * seq * width, transcendentals=H * seq * seq
        ),
    )(q, k, v, grads, att, lse, fq, fk, cosine, sine)


def gather_kernel(nblk, nrows, in_ref, out_ref, send_r, recv_r, send_b, recv_b):
    blk, row = lax.axis_index("blk"), lax.axis_index("rows")
    barrier = pltpu.get_barrier_semaphore()
    for step in range(1, nblk):
        pl.semaphore_signal(
            barrier, inc=1, device_id=(lax.rem(blk + step, nblk), row), device_id_type=MESH
        )

    def greet(step, unused):
        pl.semaphore_signal(
            barrier, inc=1, device_id=(blk, lax.rem(row + step, nrows)), device_id_type=MESH
        )
        return unused

    lax.fori_loop(1, nrows, greet, 0)
    pl.semaphore_wait(barrier, nblk + nrows - 2)
    out_ref[blk, row] = in_ref[...]

    def over_rows(step):
        other = lax.rem(row + step, nrows)
        return pltpu.make_async_remote_copy(
            src_ref=in_ref,
            dst_ref=out_ref.at[blk, row],
            send_sem=send_r.at[step],
            recv_sem=recv_r.at[step],
            device_id=(blk, other),
            device_id_type=MESH,
        )

    def over_blk(step):
        other = lax.rem(blk + step, nblk)
        return pltpu.make_async_remote_copy(
            src_ref=out_ref.at[blk],
            dst_ref=out_ref.at[blk],
            send_sem=send_b.at[step],
            recv_sem=recv_b.at[step],
            device_id=(other, row),
            device_id_type=MESH,
        )

    def start(step, unused):
        over_rows(step).start()
        return unused

    def finish(step, unused):
        over_rows(step).wait()
        return unused

    lax.fori_loop(1, nrows, start, 0)
    lax.fori_loop(1, nrows, finish, 0)
    for step in range(1, nblk):
        over_blk(step).start()
    for step in range(1, nblk):
        over_blk(step).wait()


def gather_all(vector, nblk, nrows):
    count = vector.shape[0] // LANES
    return pl.pallas_call(
        functools.partial(gather_kernel, nblk, nrows),
        out_shape=jax.ShapeDtypeStruct((nblk, nrows, count, LANES), f32),
        in_specs=[pl.BlockSpec(memory_space=pltpu.VMEM)],
        out_specs=pl.BlockSpec(memory_space=pltpu.VMEM),
        scratch_shapes=[
            pltpu.SemaphoreType.DMA((nrows,)),
            pltpu.SemaphoreType.DMA((nrows,)),
            pltpu.SemaphoreType.DMA((nblk,)),
            pltpu.SemaphoreType.DMA((nblk,)),
        ],
        compiler_params=pltpu.CompilerParams(collective_id=0, has_side_effects=True),
    )(vector.reshape(count, LANES))


def rows_in(pieces, me, nblk):
    rows = pieces.shape[0]
    parts = [lax.dynamic_index_in_dim(pieces, jnp.minimum(me, rows - 1), 0, keepdims=False)]
    for k in range(1, nblk):
        part = lax.dynamic_index_in_dim(pieces, jnp.minimum(me ^ k, rows - 1), 0, keepdims=False)
        pairs = [(s, s ^ k) for s in range(nblk) if s ^ k < rows]
        parts.append(lax.ppermute(part, "blk", pairs))
    stacked = jnp.stack(parts)
    whole = jnp.take(stacked, jnp.arange(nblk) ^ me, axis=0)
    return jnp.where(me < rows, whole, jnp.zeros_like(whole))


def rows_out(whole, rows, me, nblk):
    parts = [lax.dynamic_index_in_dim(whole, me, 0, keepdims=False)]
    for k in range(1, nblk):
        part = lax.dynamic_index_in_dim(whole, me ^ k, 0, keepdims=False)
        pairs = [(s, s ^ k) for s in range(nblk) if s < rows]
        parts.append(lax.ppermute(part, "blk", pairs))
    stacked = jnp.stack(parts)
    return jnp.take(stacked, jnp.arange(rows) ^ me, axis=0)


def pick(array, index, axis=0):
    return lax.dynamic_index_in_dim(array, index, axis, keepdims=False)


def xor_move(array, axis, size, k):
    return lax.ppermute(array, axis, [(s, s ^ k) for s in range(size)])


def halve(array, axis, bit, name, size, k):
    kept = pick(array, bit, axis).astype(f32)
    sent = pick(array, 1 - bit, axis)
    return (kept + xor_move(sent, name, size, k).astype(f32)).astype(bf16)


def reduce_weight(grad, blk, row, nblk, nrows):
    total, cols = grad.shape
    share = total // nrows
    nz = nrows // 2
    core, z = row % 2, row // 2
    x, y = blk % 2, blk // 2
    part = halve(grad.reshape(nz, 2, share, cols), 1, core, "rows", nrows, 1)
    part = part.reshape(nz, 2, share // 2, cols)
    front, back = part[: nz // 2], part[nz // 2 :]
    split = lambda a: jnp.stack([a[..., : cols // 2], a[..., cols // 2 :]])
    front = halve(split(front), 0, x, "blk", nblk, 1)
    back = halve(back, 1, y, "blk", nblk, 2)
    front = halve(front, 1, y, "blk", nblk, 2)
    back = halve(split(back), 0, x, "blk", nblk, 1)
    part = jnp.concatenate([front, back], axis=0)
    if nz <= 4:
        summed = pick(part, z).astype(f32)
        for k in range(1, nz):
            summed = summed + xor_move(pick(part, z ^ k), "rows", nrows, 2 * k).astype(f32)
        part = summed.astype(bf16)
    else:
        k = nz // 2
        while k:
            pairs = part.reshape((2, k) + part.shape[1:])
            part = halve(pairs, 0, (z // k) % 2, "rows", nrows, 2 * k)
            k //= 2
        part = part[0]
    quarters = [part] + [xor_move(part, "blk", nblk, k) for k in range(1, 4)]
    quarters = jnp.take(jnp.stack(quarters), jnp.arange(4) ^ blk, axis=0)
    ordered = quarters.reshape(2, 2, share // 2, cols // 2).transpose(0, 2, 1, 3)
    return ordered.reshape(share, cols).astype(f32)


def per_device(
    tokens, timesteps, lengths, time_table, w_ada, b_ada, gain_attn, w_qkv, w_out, gain_mlp, w_up, b_up,
    w_down, b_down, grad_out
):
    rows_dev, stretch, width = tokens.shape
    nblk, nrows = lax.axis_size("blk"), lax.axis_size("rows")
    blk, row = lax.axis_index("blk"), lax.axis_index("rows")
    seq = stretch * nblk
    head_dim = width // H
    mine = jnp.minimum(blk, rows_dev - 1)

    x_blocks = rows_in(tokens, blk, nblk)
    g_blocks = rows_in(grad_out, blk, nblk)

    slots = jnp.arange(seq, dtype=jnp.int32)
    ends = jnp.cumsum(pick(lengths, mine))
    before = ends[None, :] <= slots[:, None]
    doc = jnp.sum(before.astype(jnp.int32), axis=-1)
    place = slots - jnp.max(jnp.where(before, ends[None, :], 0), axis=-1)
    freqs = 10000.0 ** (-jnp.arange(head_dim // 2, dtype=f32) * 2.0 / head_dim)
    angle = place.astype(f32)[:, None] * freqs
    cosine, sine = jnp.cos(angle), jnp.sin(angle)
    cosine = jnp.concatenate([cosine] * 4, axis=-1)
    sine = jnp.concatenate([-sine, sine] * 2, axis=-1)
    lane = jnp.arange(LANES) % head_dim
    here = lane[None, :] == doc[:, None]
    fq = jnp.where(here, -1e30, 0.0).astype(bf16)
    fk = jnp.where(here | (lane >= NDOC + 3)[None, :], 0.0, 1.0).astype(bf16)

    table = time_table.astype(f32)
    ada_full = w_ada.astype(f32)
    step = pick(timesteps, mine)
    cond = pick(table, step)[None, :]
    modulate = jnp.dot(jax.nn.silu(cond), ada_full, precision=highest) + b_ada.astype(f32)
    shift_a, scale_a, gate_a, shift_m, scale_m, gate_m = jnp.split(modulate, 6, axis=-1)
    gain_a = gain_attn.astype(f32)
    gain_m = gain_mlp.astype(f32)
    factor_a = gain_a * (1.0 + scale_a)
    factor_m = gain_m * (1.0 + scale_m)

    x_row = x_blocks.reshape(seq, width)
    hidden_a, q, k, v = project(x_row, factor_a, shift_a, w_qkv, cosine, sine)
    attended, lse = attend(q, k, v, fq, fk)
    attended_b = attended.astype(bf16)
    branch_a = dot(attended_b, w_out)
    inputs = x_row.astype(f32)
    middle = inputs + gate_a * branch_a
    normed_m, inverse_m = norm_rows(middle)
    hidden_m = (normed_m * factor_m + shift_m).astype(bf16)
    pre = dot(hidden_m, w_up) + b_up.astype(f32)
    gelu_value, gelu_pull = jax.vjp(lambda values: jax.nn.gelu(values, approximate=True), pre)
    active = gelu_value.astype(bf16)
    branch_m = dot(active, w_down) + b_down.astype(f32)
    result = (middle + gate_m * branch_m).astype(bf16)
    out = rows_out(result.reshape(nblk, stretch, width), rows_dev, blk, nblk)

    grad = g_blocks.reshape(seq, width).astype(f32)
    grad_branch = (gate_m * grad).astype(bf16)
    grad_w_down = dot_tn(active, grad_branch).astype(bf16)
    share_w_down = reduce_weight(grad_w_down, blk, row, nblk, nrows)
    grad_b_down = jnp.sum(grad_branch.astype(f32), axis=0)
    dgate_m = jnp.sum(grad * branch_m, axis=0)
    grad_active = dot_nt(grad_branch, w_down)
    grad_pre = gelu_pull(grad_active)[0].astype(bf16)
    grad_w_up = dot_tn(hidden_m, grad_pre).astype(bf16)
    share_w_up = reduce_weight(grad_w_up, blk, row, nblk, nrows)
    grad_b_up = jnp.sum(grad_pre.astype(f32), axis=0)
    grad_hm = dot_nt(grad_pre, w_up)
    dshift_m = jnp.sum(grad_hm, axis=0)
    along_m = jnp.sum(grad_hm * normed_m, axis=0)
    grad_mid = grad + norm_back(grad_hm * factor_m, normed_m, inverse_m)
    dgate_a = jnp.sum(grad_mid * branch_a, axis=0)
    grad_ya = (gate_a * grad_mid).astype(bf16)
    grad_w_out = dot_tn(attended_b, grad_ya).astype(bf16)
    share_w_out = reduce_weight(grad_w_out, blk, row, nblk, nrows)
    grad_att = dot_nt(grad_ya, w_out).astype(bf16)

    dq, dk, dv = attend_back(q, k, v, grad_att, attended, lse, fq, fk, cosine, sine)
    grad_qkv = jnp.concatenate([dq, dk, dv], axis=-1)
    grad_w_qkv = dot_tn(hidden_a, grad_qkv).astype(bf16)
    share_w_qkv = reduce_weight(grad_w_qkv, blk, row, nblk, nrows)
    grad_ha = dot_nt(grad_qkv, w_qkv)
    normed_a, inverse_a = norm_rows(inputs)
    dshift_a = jnp.sum(grad_ha, axis=0)
    along_a = jnp.sum(grad_ha * normed_a, axis=0)
    grad_in = (grad_mid + norm_back(grad_ha * factor_a, normed_a, inverse_a)).astype(bf16)
    grad_tokens = rows_out(grad_in.reshape(nblk, stretch, width), rows_dev, blk, nblk)

    packed = jnp.concatenate(
        [
            dshift_a, along_a * gain_a, dgate_a, dshift_m, along_m * gain_m, dgate_m,
            along_a * (1.0 + scale_a[0]), along_m * (1.0 + scale_m[0]), grad_b_up, grad_b_down,
            jnp.broadcast_to(step.astype(f32), (LANES,)),
        ]
    )
    gathered = gather_all(packed, nblk, nrows).reshape(nblk, nrows, -1)
    gathered = gathered[:rows_dev].reshape(rows_dev * nrows, -1)
    six = 6 * width
    grad_mod = gathered[:, :six]
    smalls = jnp.sum(gathered, axis=0)
    grad_gain_a, grad_gain_m = smalls[six : six + width], smalls[six + width : six + 2 * width]
    rest = six + 2 * width
    ff = b_up.shape[0]
    total_b_up, total_b_down = smalls[rest : rest + ff], smalls[rest + ff : rest + ff + width]
    steps = gathered[:, -1].astype(jnp.int32)
    onehot = (steps[:, None] == jnp.arange(table.shape[0], dtype=jnp.int32)[None, :]).astype(f32)
    conds = jnp.dot(onehot, table, precision=highest)
    share = conds.shape[1] // nrows
    my_conds = lax.dynamic_slice_in_dim(conds, row * share, share, axis=1)
    grad_w_ada = jnp.dot(jax.nn.silu(my_conds).T, grad_mod, precision=highest)
    grad_cond_act = lax.dot_general(
        grad_mod, ada_full, (((1,), (1,)), ((), ())), precision=highest, preferred_element_type=f32
    )
    sigmoid = jax.nn.sigmoid(conds)
    grad_cond = grad_cond_act * sigmoid * (1.0 + conds * (1.0 - sigmoid))
    grad_table = jnp.dot(onehot.T, grad_cond, precision=highest)
    return (
        out,
        grad_tokens,
        grad_table,
        grad_w_ada,
        smalls[:six],
        grad_gain_a,
        share_w_qkv,
        share_w_out,
        grad_gain_m,
        share_w_up,
        total_b_up,
        share_w_down,
        total_b_down,
    )


def solution(mesh):
    whole, split = P(), P("rows", None)
    tokens = P("rows", "blk", None)
    return jax.shard_map(
        per_device,
        mesh=mesh,
        in_specs=(tokens, P("rows"), split) + (whole,) * 11 + (tokens,),
        out_specs=(
            tokens, tokens, whole, split, whole, whole, split, split, whole, split, whole, split, whole
        ),
        check_vma=False,
    )
```

time: 1080 us -> 435 us (0.40)
  waiting for transfers between devices: 656 us -> 59.2 us
  matrix products: 204 us -> 87.8 us
  Pallas kernels: 0 us -> 101 us
  starting transfers between devices: 0.76 us -> 84.9 us
  local copies, waits for them, and re-layouts: 106 us -> 40.3 us
  other arithmetic: 92.5 us -> 49.8 us
    reduce_scatter x6 -> x0, waiting for transfers between devices: 380 us -> none  [the longest x1 99.3 us: per_device(): lax.psum_scatter(grad_w_down, 'rows', scatter_dimension=0, tiled=True)]
    psum x2 -> x0, waiting for transfers between devices: 180 us -> none  [the longest x1 122 us: per_device(): lax.psum((grad_table, grad_b_ada, grad_gain_a, grad_gain_m, grad_b_up, gr...]
    dot_general x28 -> x15, matrix products: 203 us -> 86.9 us  [the longest x4 35.8 us: dot_nt(): lax.dot_general(a, b, (((1,), (1,)), ((), ())), preferred_element_type=f32)]
    pallas_call x0 -> x4, Pallas kernels: none -> 101 us  [the longest x1 41.7 us: attend_back(): pl.pallas_call(attend_back_kernel, grid=(width // LANES,), in_specs=[pair...]
    all_gather x2 -> x0, waiting for transfers between devices: 96.5 us -> none  [the longest x1 52 us: per_device(): piece_k = lax.all_gather(key_flat, 'blk', axis=1, tiled=True)]
    ppermute x0 -> x56, starting transfers between devices: none -> 84.9 us  [the longest x44 47.2 us: xor_move(): return lax.ppermute(array, axis, [(s, s ^ k) for s in range(size)])]
    ppermute x0 -> x56, waiting for transfers between devices: none -> 59.2 us  [the longest x44 57.2 us: xor_move(): return lax.ppermute(array, axis, [(s, s ^ k) for s in range(size)])]
    unnamed x173 -> x175, local copies, waits for them, and re-layouts: 46.2 us -> 10.1 us
  transfers between devices with their start and end apart: 10 -> 56, of which waited for: 10 -> 20; matrix products, arithmetic and copies ran while one was open for 9% -> 17% of each run, Pallas kernels for 0% -> 0%
where the time goes in v1:
time: 435 us; the launch traced here: 428 us
  Pallas kernels  101 us (23%)
  matrix products  87.8 us (20%)
  starting transfers between devices  84.9 us (20%)
  waiting for transfers between devices  59.2 us (14%)
  other arithmetic  49.8 us (11%)
  local copies, waits for them, and re-layouts  40.3 us (9%)
  between operations  5.32 us (1%)
    ppermute x44, waiting for transfers between devices, xor_move(): return lax.ppermute(array, axis, [(s, s ^ k) for s in range(size)])  57.2 us
    ppermute x44, starting transfers between devices, xor_move(): return lax.ppermute(array, axis, [(s, s ^ k) for s in range(size)])  47.2 us
    pallas_call x1, Pallas kernels, attend_back(): pl.pallas_call(attend_back_kernel, grid=(width // LANES,), in_specs=[pair...  41.7 us
    dot_general x4, matrix products, dot_nt(): lax.dot_general(a, b, (((1,), (1,)), ((), ())), preferred_element_type=f32)  35.8 us
    pallas_call x1, Pallas kernels, gather_all(): pl.pallas_call(functools.partial(gather_kernel, nblk, nrows), out_shape=j...  27.5 us
    pallas_call x1, Pallas kernels, attend(): pl.pallas_call(attend_kernel, grid=(width // LANES,), in_specs=[pair, pai...  25.6 us
    dot_general x3, matrix products, dot(): return jnp.dot(a, b, preferred_element_type=f32)  24.3 us
    dot_general x4, matrix products, dot_tn(): lax.dot_general(a, b, (((0,), (0,)), ((), ())), preferred_element_type=f32)  23.1 us
  transfers between devices with their start and end apart: 56, of which 20 were waited for; matrix products, arithmetic and copies ran while one was open for 17% of the time, Pallas kernels for 0%

profile of v1, /device:TPU:0, one launch (start us, length us, event | category | flops | bytes accessed | tf_op | source)
XLA Modules:
  0.0 428.2 jit_solution(11263023751156891666)
XLA Ops:
  4.7 6.9 %collective-permute-start.7 = (bf16[256,768]{1,0:T(8,128)(2,1)}, bf16[256,768]{1,0:T(8,128)(2,1)}, u32[]{:S(2)}, u32[]{:S(2)}) collective-permute-start(bf16[256,768]{1,0:T(8,128)(2,1)} %get-tuple-element.84), channel_id=1, source_target_pairs={{0,16},{16,0},{24,8},{1,17},{17,1},{25,9},{2,18},{18,2},{26,10},{3... | collective-permute-start | bytes 1179656 | tf_op jit(solution)/shard_map/ppermute | solution.py:308
  16.2 6.0 %collective-permute-start.1 = (bf16[256,768]{1,0:T(8,128)(2,1)}, bf16[256,768]{1,0:T(8,128)(2,1)}, u32[]{:S(2)}, u32[]{:S(2)}) collective-permute-start(bf16[256,768]{1,0:T(8,128)(2,1)} %get-tuple-element.88), channel_id=1, source_target_pairs={{0,16},{16,0},{24,8},{1,17},{17,1},{25,9},{2,18},{18,2},{26,10},{3... | collective-permute-start | bytes 1179656 | tf_op jit(solution)/shard_map/ppermute | solution.py:308
  41.9 2.7 pad_maximum_fusion.2
  51.5 3.3 gather_fusion.4
  59.3 5.9 %shard_map.246 = (bf16[1024,768]{1,0:T(8,128)(2,1)S(1)}, bf16[1024,768]{1,0:T(8,128)(2,1)S(1)}, bf16[1024,768]{1,0:T(8,128)(2,1)S(1)}, bf16[1024,768]{1,0:T(8,128)(2,1)S(1)}) custom-call(bf16[1024,768]{1,0:T(8,128)(2,1)S(1)} %bitcast.358, f32[1,768]{1,0:T(1,128)S(1)} %get-tuple-element.120.factor_ref, f32[1,768]{1,0:T(1,128)S(1)} %get-tuple-element.118.shift_ref, ...), custom_call_target="tpu_custom_call" | custom-call | flops 3623878656 | bytes 9437184 | tf_op jit(solution)/shard_map/pallas_call | solution.py:97
  66.4 25.6 %shard_map.247 = (f32[1024,768]{1,0:T(8,128)S(1)}, f32[1024,768]{1,0:T(8,128)S(1)}) custom-call(bf16[1024,768]{1,0:T(8,128)(2,1)S(1)} %get-tuple-element.24.q_ref, bf16[1024,768]{1,0:T(8,128)(2,1)S(1)} %get-tuple-element.25.k_ref, bf16[1024,768]{1,0:T(8,128)(2,1)S(1)} %get-tuple-element.26.v_ref, bf16[1024,128]{1,0:T(8,128)(2,1)S(1)} %copy-done.4, ...), custom_call_target="tpu_custom_call" | custom-call | flops 12884901888 | bytes 11010048 | tf_op jit(solution)/shard_map/pallas_call | solution.py:142
  92.1 3.3 fusion.153
  97.8 11.3 %multiply_convert_fusion = (bf16[1024,3072]{1,0:T(8,128)(2,1)}, f32[1024,3072]{1,0:T(8,128)}) fusion(f32[3072]{0:T(1024)S(1)} %copy-done.46, bf16[768,3072]{1,0:T(8,128)(2,1)S(1)} %bitcast.453, f32[1024,768]{1,0:T(8,128)S(1)} %get-tuple-element.56, f32[768]{0:T(1024)S(1)} %copy-done.56, f32[768]{0:T(1024)S(1)} %copy-done.40, f32[1024]{0:T(1024)S(1)} %add_rsqrt_fusion, ...), kind=kOutput, calls=%fused_computation.18 | convolution fusion | flops 4867227648 | bytes 26765312 | tf_op jit(solution)/shard_map/dot_general | solution.py:25
  109.1 16.7 %convert_reduce_fusion = (f32[3072]{0:T(1024)S(1)}, bf16[1024,3072]{1,0:T(8,128)(2,1)}) fusion(f32[1024,3072]{1,0:T(8,128)} %get-tuple-element.133, f32[3072]{0:T(1024)S(1)} %copy-done.46, bf16[1024,768]{1,0:T(8,128)(2,1)S(1)} %copy-done.30, bf16[3072,768]{1,0:T(8,128)(2,1)S(1)} %bitcast.390), kind=kOutput, calls=%fused_computation.17 | convolution fusion | flops 4904186880 | bytes 25190400 | tf_op jit(solution)/shard_map/dot_general | solution.py:29
  125.9 10.4 %multiply_reduce_fusion = (f32[768]{0:T(1024)S(1)}, f32[1024]{0:T(1024)S(1)}, f32[1024]{0:T(1024)S(1)}, f32[768]{0:T(1024)S(1)}, f32[1024,768]{1,0:T(8,128)}) fusion(f32[1024,768]{1,0:T(8,128)S(1)} %get-tuple-element.56, f32[1024]{0:T(1024)S(1)} %add_rsqrt_fusion, f32[1024]{0:T(1024)S(1)} %broadcast_multiply_fusion.5, f32[768]{0:T(1024)S(1)} %copy-done.40, ...), kind=kOutput, calls=%fused_computation.52 | convolution fusion | flops 4838912000 | bytes 17327104 | tf_op jit(solution)/shard_map/dot_general | solution.py:29
  137.0 9.7 %fusion.24 = (f32[768]{0:T(1024)S(1)}, bf16[1024,768]{1,0:T(8,128)(2,1)}, f32[768]{0:T(1024)S(1)}, f32[1024,768]{1,0:T(8,128)S(1)}) fusion(f32[768]{0:T(1024)S(1)} %copy-done.36, bf16[4,256,768]{2,1,0:T(8,128)(2,1)S(1)} %copy-done.15, pred[4]{0:T(512)(128)(4,1)S(1)} %copy-done.55, pred[]{:T(512)S(6)} %lt.207, f32[1024,768]{1,0:T(8,128)S(1)} %get-tuple-element.56, ...), kind=kOutput, calls=%fused_computation.50 | convolution fusion | flops 4846778368 | bytes 26770436 | tf_op jit(solution)/shard_map/dot_general | solution.py:25
  149.3 41.7 %shard_map.248 = (bf16[1024,768]{1,0:T(8,128)(2,1)S(1)}, bf16[1024,768]{1,0:T(8,128)(2,1)S(1)}, bf16[1024,768]{1,0:T(8,128)(2,1)}) custom-call(bf16[1024,768]{1,0:T(8,128)(2,1)} %copy-done.8, bf16[1024,768]{1,0:T(8,128)(2,1)} %copy-done.9, bf16[1024,768]{1,0:T(8,128)(2,1)} %copy-done.10, bf16[1024,768]{1,0:T(8,128)(2,1)} %convolution_convert_fusion.3.d_ref, ...), custom_call_target="tpu_custom_call" | custom-call | flops 32212254720 | bytes 18874368 | tf_op jit(solution)/shard_map/pallas_call | solution.py:211
  192.6 6.1 %fusion.19 = (f32[768]{0:T(1024)S(1)}, f32[1024]{0:T(1024)S(1)}, f32[1024]{0:T(1024)S(1)}, f32[768]{0:T(1024)S(1)}, f32[1024,768]{1,0:T(8,128)}) fusion(f32[1024]{0:T(1024)S(1)} %bitcast.447, f32[1024]{0:T(1024)S(1)} %bitcast.449, bf16[4,256,768]{2,1,0:T(8,128)(2,1)S(1)} %get-tuple-element.54, f32[768]{0:T(1024)S(1)} %copy-done.39, ...), kind=kOutput, calls=%fused_computation.41 | convolution fusion | flops 3631739392 | bytes 13001728 | tf_op jit(solution)/shard_map/dot_general | solution.py:29
  199.4 27.5 %shard_map.249 = f32[4,8,79,128]{3,2,1,0:T(8,128)} custom-call(f32[79,128]{1,0:T(8,128)} %bitcast.443), custom_call_target="tpu_custom_call" | custom-call | tf_op jit(solution)/shard_map/pallas_call | solution.py:287
  229.5 4.4 %convolution_convert_fusion.4 = bf16[768,768]{1,0:T(8,128)(2,1)S(1)} fusion(f32[1024,768]{1,0:T(8,128)} %copy-done.2, f32[1024,768]{1,0:T(8,128)} %copy-done.16, f32[768]{0:T(1024)S(1)} %copy-done.43), kind=kOutput, calls=%fused_computation.72 | convolution fusion | flops 1210908672 | bytes 7474176 | tf_op jit(solution)/shard_map/dot_general | solution.py:33
  234.0 8.9 %convolution_convert_fusion.1 = bf16[768,3072]{1,0:T(8,128)(2,1)S(1)} fusion(bf16[1024,3072]{1,0:T(8,128)(2,1)} %get-tuple-element.137, f32[1024,768]{1,0:T(8,128)S(1)} %copy-done.13, f32[768]{0:T(1024)S(1)} %copy-done.57, f32[768]{0:T(1024)S(1)} %copy-done.41, f32[1024]{0:T(1024)S(1)} %add_rsqrt_fusion, f32[1024]{0:T(1024)S(1)} %broadcast_multiply_fusion.5), kind=kOutput, calls=%fused_computation.20 | convolution fusion | flops 4838129664 | bytes 14170112 | tf_op jit(solution)/shard_map/dot_general | solution.py:33
  243.7 5.6 %convolution_convert_fusion = bf16[3072,768]{1,0:T(8,128)(2,1)S(1)} fusion(bf16[1024,3072]{1,0:T(8,128)(2,1)S(1)} %bitcast.363, bf16[1024,768]{1,0:T(8,128)(2,1)S(1)} %copy-done.31), kind=kOutput, calls=%fused_computation.19 | convolution fusion | flops 4834197504 | bytes 12582912 | tf_op jit(solution)/shard_map/dot_general | solution.py:33
  250.9 4.4 %collective-permute-start.11 = (bf16[256,768]{1,0:T(8,128)(2,1)S(1)}, bf16[256,768]{1,0:T(8,128)(2,1)S(1)}, u32[]{:S(2)}, u32[]{:S(2)}) collective-permute-start(bf16[256,768]{1,0:T(8,128)(2,1)S(1)} %get-tuple-element.68), channel_id=1, source_target_pairs={{0,24},{8,16},{16,8},{1,25},{9,17},{17,9},{2,26},{10,18},{18,10},{... | collective-permute-start | bytes 1179656 | tf_op jit(solution)/shard_map/ppermute | solution.py:319
  265.0 4.2 convolution_convert_fusion.2
  274.1 6.0 %collective-permute-start.4 = (bf16[256,768]{1,0:T(8,128)(2,1)S(1)}, bf16[256,768]{1,0:T(8,128)(2,1)S(1)}, u32[]{:S(2)}, u32[]{:S(2)}) collective-permute-start(bf16[256,768]{1,0:T(8,128)(2,1)S(1)} %get-tuple-element.73), channel_id=1, source_target_pairs={{0,16},{8,24},{16,0},{1,17},{9,25},{17,1},{2,18},{10,26},{18,2},{3... | collective-permute-start | bytes 1179656 | tf_op jit(solution)/shard_map/ppermute | solution.py:319
  285.2 11.4 %collective-permute-done.24 = bf16[2,2,48,384]{3,2,0,1:T(8,128)(2,1)S(1)} collective-permute-done((bf16[2,2,48,384]{3,2,0,1:T(8,128)(2,1)S(1)}, bf16[2,2,48,384]{3,2,0,1:T(8,128)(2,1)S(1)}, u32[]{:S(2)}, u32[]{:S(2)}) %collective-permute-start.24) | collective-permute-done | bytes 147488 | tf_op jit(solution)/shard_map/ppermute | solution.py:329
  296.7 5.0 %collective-permute-done.26 = bf16[2,48,768]{2,1,0:T(8,128)(2,1)S(1)} collective-permute-done((bf16[2,48,768]{2,1,0:T(8,128)(2,1)S(1)}, bf16[2,48,768]{2,1,0:T(8,128)(2,1)S(1)}, u32[]{:S(2)}, u32[]{:S(2)}) %collective-permute-start.26) | collective-permute-done | bytes 147488 | tf_op jit(solution)/shard_map/ppermute | solution.py:329
  301.9 4.2 collective-permute-done.25
  306.5 3.9 collective-permute-done.27
  310.6 4.2 collective-permute-start.30
  332.2 9.1 %collective-permute-done.13 = bf16[2,2,48,1152]{3,2,0,1:T(8,128)(2,1)S(1)} collective-permute-done((bf16[2,2,48,1152]{3,2,0,1:T(8,128)(2,1)S(1)}, bf16[2,2,48,1152]{3,2,0,1:T(8,128)(2,1)S(1)}, u32[]{:S(2)}, u32[]{:S(2)}) %collective-permute-start.13) | collective-permute-done | bytes 442400 | tf_op jit(solution)/shard_map/ppermute | solution.py:329
  343.0 2.8 collective-permute-start.16
  354.3 3.8 collective-permute-start.19
  361.6 3.5 collective-permute-done.18
  384.9 3.0 collective-permute-done.46
  403.9 5.0 %collective-permute-start.50 = (bf16[192,384]{1,0:T(8,128)(2,1)S(1)}, bf16[192,384]{1,0:T(8,128)(2,1)S(1)}, u32[]{:S(2)}, u32[]{:S(2)}) collective-permute-start(bf16[192,384]{1,0:T(8,128)(2,1)S(1)} %get-tuple-element.91), channel_id=1, source_target_pairs={{0,2},{1,3},{2,0},{3,1},{4,6},{5,7},{6,4},{7,5},{8,10},{9,11},{10,... | collective-permute-start | bytes 442376 | tf_op jit(solution)/shard_map/ppermute | solution.py:329
  408.9 4.4 %collective-permute-done.40 = bf16[48,1536]{1,0:T(8,128)(2,1)S(1)} collective-permute-done((bf16[48,1536]{1,0:T(8,128)(2,1)S(1)}, bf16[48,1536]{1,0:T(8,128)(2,1)S(1)}, u32[]{:S(2)}, u32[]{:S(2)}) %collective-permute-start.40) | collective-permute-done | bytes 147488 | tf_op jit(solution)/shard_map/ppermute | solution.py:329
  (423 shorter events, 152.1 us)
Async XLA Ops:
  3.4 33.7 %collective-permute-start.8 = (bf16[256,768]{1,0:T(8,128)(2,1)}, bf16[256,768]{1,0:T(8,128)(2,1)}, u32[]{:S(2)}, u32[]{:S(2)}) collective-permute-start(bf16[256,768]{1,0:T(8,128)(2,1)} %get-tuple-element.83), channel_id=1, source_target_pairs={{8,16},{16,8},{24,0},{9,17},{17,9},{25,1},{10,18},{18,10},{26,2},{... | collective-permute-start | bytes 1179656 | tf_op jit(solution)/shard_map/ppermute | solution.py:308
  4.7 37.2 %collective-permute-start.7 = (bf16[256,768]{1,0:T(8,128)(2,1)}, bf16[256,768]{1,0:T(8,128)(2,1)}, u32[]{:S(2)}, u32[]{:S(2)}) collective-permute-start(bf16[256,768]{1,0:T(8,128)(2,1)} %get-tuple-element.84), channel_id=1, source_target_pairs={{0,16},{16,0},{24,8},{1,17},{17,1},{25,9},{2,18},{18,2},{26,10},{3... | collective-permute-start | bytes 1179656 | tf_op jit(solution)/shard_map/ppermute | solution.py:308
  11.6 30.2 %collective-permute-start.6 = (bf16[256,768]{1,0:T(8,128)(2,1)}, bf16[256,768]{1,0:T(8,128)(2,1)}, u32[]{:S(2)}, u32[]{:S(2)}) collective-permute-start(bf16[256,768]{1,0:T(8,128)(2,1)} %get-tuple-element.82), channel_id=1, source_target_pairs={{0,8},{8,0},{24,16},{1,9},{9,1},{25,17},{2,10},{10,2},{26,18},{3,1... | collective-permute-start | bytes 1179656 | tf_op jit(solution)/shard_map/ppermute | solution.py:308
  14.8 32.0 %collective-permute-start.2 = (bf16[256,768]{1,0:T(8,128)(2,1)}, bf16[256,768]{1,0:T(8,128)(2,1)}, u32[]{:S(2)}, u32[]{:S(2)}) collective-permute-start(bf16[256,768]{1,0:T(8,128)(2,1)} %get-tuple-element.87), channel_id=1, source_target_pairs={{8,16},{16,8},{24,0},{9,17},{17,9},{25,1},{10,18},{18,10},{26,2},{... | collective-permute-start | bytes 1179656 | tf_op jit(solution)/shard_map/ppermute | solution.py:308
  16.2 30.6 %collective-permute-start.1 = (bf16[256,768]{1,0:T(8,128)(2,1)}, bf16[256,768]{1,0:T(8,128)(2,1)}, u32[]{:S(2)}, u32[]{:S(2)}) collective-permute-start(bf16[256,768]{1,0:T(8,128)(2,1)} %get-tuple-element.88), channel_id=1, source_target_pairs={{0,16},{16,0},{24,8},{1,17},{17,1},{25,9},{2,18},{18,2},{26,10},{3... | collective-permute-start | bytes 1179656 | tf_op jit(solution)/shard_map/ppermute | solution.py:308
  37.2 11.7 %collective-permute-start = (bf16[256,768]{1,0:T(8,128)(2,1)}, bf16[256,768]{1,0:T(8,128)(2,1)}, u32[]{:S(2)}, u32[]{:S(2)}) collective-permute-start(bf16[256,768]{1,0:T(8,128)(2,1)} %get-tuple-element.86), channel_id=1, source_target_pairs={{0,8},{8,0},{24,16},{1,9},{9,1},{25,17},{2,10},{10,2},{26,18},{3,1... | collective-permute-start | bytes 1179656 | tf_op jit(solution)/shard_map/ppermute | solution.py:308
  250.9 29.6 %collective-permute-start.11 = (bf16[256,768]{1,0:T(8,128)(2,1)S(1)}, bf16[256,768]{1,0:T(8,128)(2,1)S(1)}, u32[]{:S(2)}, u32[]{:S(2)}) collective-permute-start(bf16[256,768]{1,0:T(8,128)(2,1)S(1)} %get-tuple-element.68), channel_id=1, source_target_pairs={{0,24},{8,16},{16,8},{1,25},{9,17},{17,9},{2,26},{10,18},{18,10},{... | collective-permute-start | bytes 1179656 | tf_op jit(solution)/shard_map/ppermute | solution.py:319
  255.3 27.5 %collective-permute-start.10 = (bf16[256,768]{1,0:T(8,128)(2,1)S(1)}, bf16[256,768]{1,0:T(8,128)(2,1)S(1)}, u32[]{:S(2)}, u32[]{:S(2)}) collective-permute-start(bf16[256,768]{1,0:T(8,128)(2,1)S(1)} %get-tuple-element.69), channel_id=1, source_target_pairs={{0,16},{8,24},{16,0},{1,17},{9,25},{17,1},{2,18},{10,26},{18,2},{3... | collective-permute-start | bytes 1179656 | tf_op jit(solution)/shard_map/ppermute | solution.py:319
  257.5 25.4 %collective-permute-start.9 = (bf16[256,768]{1,0:T(8,128)(2,1)S(1)}, bf16[256,768]{1,0:T(8,128)(2,1)S(1)}, u32[]{:S(2)}, u32[]{:S(2)}) collective-permute-start(bf16[256,768]{1,0:T(8,128)(2,1)S(1)} %get-tuple-element.70), channel_id=1, source_target_pairs={{0,8},{8,0},{16,24},{1,9},{9,1},{17,25},{2,10},{10,2},{18,26},{3,1... | collective-permute-start | bytes 1179656 | tf_op jit(solution)/shard_map/ppermute | solution.py:319
  259.6 51.0 %collective-permute-start.5 = (bf16[256,768]{1,0:T(8,128)(2,1)S(1)}, bf16[256,768]{1,0:T(8,128)(2,1)S(1)}, u32[]{:S(2)}, u32[]{:S(2)}) collective-permute-start(bf16[256,768]{1,0:T(8,128)(2,1)S(1)} %get-tuple-element.72), channel_id=1, source_target_pairs={{0,24},{8,16},{16,8},{1,25},{9,17},{17,9},{2,26},{10,18},{18,10},{... | collective-permute-start | bytes 1179656 | tf_op jit(solution)/shard_map/ppermute | solution.py:319
  274.1 40.6 %collective-permute-start.4 = (bf16[256,768]{1,0:T(8,128)(2,1)S(1)}, bf16[256,768]{1,0:T(8,128)(2,1)S(1)}, u32[]{:S(2)}, u32[]{:S(2)}) collective-permute-start(bf16[256,768]{1,0:T(8,128)(2,1)S(1)} %get-tuple-element.73), channel_id=1, source_target_pairs={{0,16},{8,24},{16,0},{1,17},{9,25},{17,1},{2,18},{10,26},{18,2},{3... | collective-permute-start | bytes 1179656 | tf_op jit(solution)/shard_map/ppermute | solution.py:319
  280.5 34.3 %collective-permute-start.3 = (bf16[256,768]{1,0:T(8,128)(2,1)S(1)}, bf16[256,768]{1,0:T(8,128)(2,1)S(1)}, u32[]{:S(2)}, u32[]{:S(2)}) collective-permute-start(bf16[256,768]{1,0:T(8,128)(2,1)S(1)} %get-tuple-element.74), channel_id=1, source_target_pairs={{0,8},{8,0},{16,24},{1,9},{9,1},{17,25},{2,10},{10,2},{18,26},{3,1... | collective-permute-start | bytes 1179656 | tf_op jit(solution)/shard_map/ppermute | solution.py:319
  282.8 43.6 %collective-permute-start.12 = (bf16[4,96,2304]{2,1,0:T(8,128)(2,1)}, bf16[4,96,2304]{2,1,0:T(8,128)(2,1)}, u32[]{:S(2)}, u32[]{:S(2)}) collective-permute-start(bf16[4,96,2304]{2,1,0:T(8,128)(2,1)} %dynamic-slice_bitcast_fusion.2), channel_id=1, source_target_pairs={{0,1},{1,0},{2,3},{3,2},{4,5},{5,4},{6,7},{7,6},{8,9},{9,8},{10,11... | collective-permute-start | bytes 5308424 | tf_op jit(solution)/shard_map/ppermute | solution.py:329
  282.9 13.7 %collective-permute-start.24 = (bf16[2,2,48,384]{3,2,0,1:T(8,128)(2,1)S(1)}, bf16[2,2,48,384]{3,2,0,1:T(8,128)(2,1)S(1)}, u32[]{:S(2)}, u32[]{:S(2)}) collective-permute-start(bf16[2,2,48,384]{3,2,0,1:T(8,128)(2,1)S(1)} %fusion.83), channel_id=1, source_target_pairs={{0,8},{8,0},{16,24},{24,16},{1,9},{9,1},{17,25},{25,17},{2,10},{10... | collective-permute-start | bytes 442376 | tf_op jit(solution)/shard_map/ppermute | solution.py:329
  310.4 35.4 %collective-permute-start.34 = (bf16[4,96,3072]{2,1,0:T(8,128)(2,1)}, bf16[4,96,3072]{2,1,0:T(8,128)(2,1)}, u32[]{:S(2)}, u32[]{:S(2)}) collective-permute-start(bf16[4,96,3072]{2,1,0:T(8,128)(2,1)} %dynamic-slice_bitcast_fusion.1), channel_id=1, source_target_pairs={{0,1},{1,0},{2,3},{3,2},{4,5},{5,4},{6,7},{7,6},{8,9},{9,8},{10,11... | collective-permute-start | bytes 7077896 | tf_op jit(solution)/shard_map/ppermute | solution.py:329
  325.1 26.0 %collective-permute-start.45 = (bf16[4,384,768]{2,1,0:T(8,128)(2,1)}, bf16[4,384,768]{2,1,0:T(8,128)(2,1)}, u32[]{:S(2)}, u32[]{:S(2)}) collective-permute-start(bf16[4,384,768]{2,1,0:T(8,128)(2,1)} %dynamic-slice_bitcast_fusion), channel_id=1, source_target_pairs={{0,1},{1,0},{2,3},{3,2},{4,5},{5,4},{6,7},{7,6},{8,9},{9,8},{10,11... | collective-permute-start | bytes 7077896 | tf_op jit(solution)/shard_map/ppermute | solution.py:329
  329.4 12.0 %collective-permute-start.13 = (bf16[2,2,48,1152]{3,2,0,1:T(8,128)(2,1)S(1)}, bf16[2,2,48,1152]{3,2,0,1:T(8,128)(2,1)S(1)}, u32[]{:S(2)}, u32[]{:S(2)}) collective-permute-start(bf16[2,2,48,1152]{3,2,0,1:T(8,128)(2,1)S(1)} %fusion.50), channel_id=1, source_target_pairs={{0,8},{8,0},{16,24},{24,16},{1,9},{9,1},{17,25},{25,17},{2,10},{10... | collective-permute-start | bytes 1327112 | tf_op jit(solution)/shard_map/ppermute | solution.py:329
  332.1 10.6 %collective-permute-start.15 = (bf16[2,48,2304]{2,1,0:T(8,128)(2,1)S(1)}, bf16[2,48,2304]{2,1,0:T(8,128)(2,1)S(1)}, u32[]{:S(2)}, u32[]{:S(2)}) collective-permute-start(bf16[2,48,2304]{2,1,0:T(8,128)(2,1)S(1)} %dynamic-slice_bitcast_fusion.6), channel_id=1, source_target_pairs={{0,16},{8,24},{16,0},{24,8},{1,17},{9,25},{17,1},{25,9},{2,18},{10... | collective-permute-start | bytes 1327112 | tf_op jit(solution)/shard_map/ppermute | solution.py:329
  341.6 12.2 %collective-permute-start.14 = (bf16[2,48,1152]{2,1,0:T(8,128)(2,1)S(1)}, bf16[2,48,1152]{2,1,0:T(8,128)(2,1)S(1)}, u32[]{:S(2)}, u32[]{:S(2)}) collective-permute-start(bf16[2,48,1152]{2,1,0:T(8,128)(2,1)S(1)} %dynamic-slice_bitcast_fusion.21), channel_id=1, source_target_pairs={{0,16},{8,24},{16,0},{24,8},{1,17},{9,25},{17,1},{25,9},{2,18},{10... | collective-permute-start | bytes 663560 | tf_op jit(solution)/shard_map/ppermute | solution.py:329
  343.0 10.9 %collective-permute-start.16 = (bf16[2,48,1152]{2,1,0:T(8,128)(2,1)S(1)}, bf16[2,48,1152]{2,1,0:T(8,128)(2,1)S(1)}, u32[]{:S(2)}, u32[]{:S(2)}) collective-permute-start(bf16[2,48,1152]{2,1,0:T(8,128)(2,1)S(1)} %fusion.75), channel_id=1, source_target_pairs={{0,8},{8,0},{16,24},{24,16},{1,9},{9,1},{17,25},{25,17},{2,10},{10... | collective-permute-start | bytes 663560 | tf_op jit(solution)/shard_map/ppermute | solution.py:329
  349.9 29.7 %collective-permute-start.35 = (bf16[2,2,48,1536]{3,2,0,1:T(8,128)(2,1)}, bf16[2,2,48,1536]{3,2,0,1:T(8,128)(2,1)}, u32[]{:S(2)}, u32[]{:S(2)}) collective-permute-start(bf16[2,2,48,1536]{3,2,0,1:T(8,128)(2,1)} %fusion.41), channel_id=1, source_target_pairs={{0,8},{8,0},{16,24},{24,16},{1,9},{9,1},{17,25},{25,17},{2,10},{10... | collective-permute-start | bytes 1769480 | tf_op jit(solution)/shard_map/ppermute | solution.py:329
  350.8 31.8 %collective-permute-start.37 = (bf16[2,48,3072]{2,1,0:T(8,128)(2,1)}, bf16[2,48,3072]{2,1,0:T(8,128)(2,1)}, u32[]{:S(2)}, u32[]{:S(2)}) collective-permute-start(bf16[2,48,3072]{2,1,0:T(8,128)(2,1)} %dynamic-slice_bitcast_fusion.4), channel_id=1, source_target_pairs={{0,16},{8,24},{16,0},{24,8},{1,17},{9,25},{17,1},{25,9},{2,18},{10... | collective-permute-start | bytes 1769480 | tf_op jit(solution)/shard_map/ppermute | solution.py:329
  372.1 15.7 %collective-permute-start.46 = (bf16[2,2,192,384]{3,2,0,1:T(8,128)(2,1)}, bf16[2,2,192,384]{3,2,0,1:T(8,128)(2,1)}, u32[]{:S(2)}, u32[]{:S(2)}) collective-permute-start(bf16[2,2,192,384]{3,2,0,1:T(8,128)(2,1)} %fusion.37), channel_id=1, source_target_pairs={{0,8},{8,0},{16,24},{24,16},{1,9},{9,1},{17,25},{25,17},{2,10},{10... | collective-permute-start | bytes 1769480 | tf_op jit(solution)/shard_map/ppermute | solution.py:329
  373.4 16.6 %collective-permute-start.48 = (bf16[2,192,768]{2,1,0:T(8,128)(2,1)}, bf16[2,192,768]{2,1,0:T(8,128)(2,1)}, u32[]{:S(2)}, u32[]{:S(2)}) collective-permute-start(bf16[2,192,768]{2,1,0:T(8,128)(2,1)} %dynamic-slice_bitcast_fusion.3), channel_id=1, source_target_pairs={{0,16},{8,24},{16,0},{24,8},{1,17},{9,25},{17,1},{25,9},{2,18},{10... | collective-permute-start | bytes 1769480 | tf_op jit(solution)/shard_map/ppermute | solution.py:329
  381.0 13.8 %collective-permute-start.36 = (bf16[2,48,1536]{2,1,0:T(8,128)(2,1)S(1)}, bf16[2,48,1536]{2,1,0:T(8,128)(2,1)S(1)}, u32[]{:S(2)}, u32[]{:S(2)}) collective-permute-start(bf16[2,48,1536]{2,1,0:T(8,128)(2,1)S(1)} %dynamic-slice_bitcast_fusion.20), channel_id=1, source_target_pairs={{0,16},{8,24},{16,0},{24,8},{1,17},{9,25},{17,1},{25,9},{2,18},{10... | collective-permute-start | bytes 884744 | tf_op jit(solution)/shard_map/ppermute | solution.py:329
  384.1 10.8 %collective-permute-start.38 = (bf16[2,48,1536]{2,1,0:T(8,128)(2,1)S(1)}, bf16[2,48,1536]{2,1,0:T(8,128)(2,1)S(1)}, u32[]{:S(2)}, u32[]{:S(2)}) collective-permute-start(bf16[2,48,1536]{2,1,0:T(8,128)(2,1)S(1)} %fusion.63), channel_id=1, source_target_pairs={{0,8},{8,0},{16,24},{24,16},{1,9},{9,1},{17,25},{25,17},{2,10},{10... | collective-permute-start | bytes 884744 | tf_op jit(solution)/shard_map/ppermute | solution.py:329
  389.3 10.4 %collective-permute-start.47 = (bf16[2,192,384]{2,1,0:T(8,128)(2,1)S(1)}, bf16[2,192,384]{2,1,0:T(8,128)(2,1)S(1)}, u32[]{:S(2)}, u32[]{:S(2)}) collective-permute-start(bf16[2,192,384]{2,1,0:T(8,128)(2,1)S(1)} %dynamic-slice_bitcast_fusion.19), channel_id=1, source_target_pairs={{0,16},{8,24},{16,0},{24,8},{1,17},{9,25},{17,1},{25,9},{2,18},{10... | collective-permute-start | bytes 884744 | tf_op jit(solution)/shard_map/ppermute | solution.py:329
  397.1 16.2 %collective-permute-start.40 = (bf16[48,1536]{1,0:T(8,128)(2,1)S(1)}, bf16[48,1536]{1,0:T(8,128)(2,1)S(1)}, u32[]{:S(2)}, u32[]{:S(2)}) collective-permute-start(bf16[48,1536]{1,0:T(8,128)(2,1)S(1)} %get-tuple-element.97), channel_id=1, source_target_pairs={{0,4},{1,5},{2,6},{3,7},{4,0},{5,1},{6,2},{7,3},{8,12},{9,13},{10,... | collective-permute-start | bytes 442376 | tf_op jit(solution)/shard_map/ppermute | solution.py:329
  397.2 16.1 %collective-permute-start.39 = (bf16[48,1536]{1,0:T(8,128)(2,1)S(1)}, bf16[48,1536]{1,0:T(8,128)(2,1)S(1)}, u32[]{:S(2)}, u32[]{:S(2)}) collective-permute-start(bf16[48,1536]{1,0:T(8,128)(2,1)S(1)} %get-tuple-element.96), channel_id=1, source_target_pairs={{0,2},{1,3},{2,0},{3,1},{4,6},{5,7},{6,4},{7,5},{8,10},{9,11},{10,... | collective-permute-start | bytes 442376 | tf_op jit(solution)/shard_map/ppermute | solution.py:329
  400.4 15.8 %collective-permute-start.52 = (bf16[192,384]{1,0:T(8,128)(2,1)S(1)}, bf16[192,384]{1,0:T(8,128)(2,1)S(1)}, u32[]{:S(2)}, u32[]{:S(2)}) collective-permute-start(bf16[192,384]{1,0:T(8,128)(2,1)S(1)} %get-tuple-element.93), channel_id=1, source_target_pairs={{0,6},{1,7},{2,4},{3,5},{4,2},{5,3},{6,0},{7,1},{8,14},{9,15},{10,... | collective-permute-start | bytes 442376 | tf_op jit(solution)/shard_map/ppermute | solution.py:329
  402.2 14.8 %collective-permute-start.51 = (bf16[192,384]{1,0:T(8,128)(2,1)S(1)}, bf16[192,384]{1,0:T(8,128)(2,1)S(1)}, u32[]{:S(2)}, u32[]{:S(2)}) collective-permute-start(bf16[192,384]{1,0:T(8,128)(2,1)S(1)} %get-tuple-element.92), channel_id=1, source_target_pairs={{0,4},{1,5},{2,6},{3,7},{4,0},{5,1},{6,2},{7,3},{8,12},{9,13},{10,... | collective-permute-start | bytes 442376 | tf_op jit(solution)/shard_map/ppermute | solution.py:329
  403.9 13.1 %collective-permute-start.50 = (bf16[192,384]{1,0:T(8,128)(2,1)S(1)}, bf16[192,384]{1,0:T(8,128)(2,1)S(1)}, u32[]{:S(2)}, u32[]{:S(2)}) collective-permute-start(bf16[192,384]{1,0:T(8,128)(2,1)S(1)} %get-tuple-element.91), channel_id=1, source_target_pairs={{0,2},{1,3},{2,0},{3,1},{4,6},{5,7},{6,4},{7,5},{8,10},{9,11},{10,... | collective-permute-start | bytes 442376 | tf_op jit(solution)/shard_map/ppermute | solution.py:329
  (100 other events, 1110.8 us)

commit v2 on v1

--- a/solution.py
+++ b/solution.py
@@ -67,89 +67,192 @@
     return (high, middle, low)
 
 
-def project_kernel(x_ref, factor_ref, shift_ref, w_ref, cos_ref, sin_ref, h_ref, q_ref, k_ref, v_ref):
-    normed, unused = norm_rows(x_ref[...].astype(f32))
-    hidden = (normed * factor_ref[...] + shift_ref[...]).astype(bf16)
-    h_ref[...] = hidden
-    width = x_ref.shape[-1]
+def partner(blk, k):
+    other = blk
+    bit = 1
+    while bit <= k:
+        if k & bit:
+            other = other + bit - 2 * bit * (other // bit % 2)
+        bit *= 2
+    return other
+
+
+def remote(source, target, send, recv, blk, row):
+    return pltpu.make_async_remote_copy(
+        src_ref=source, dst_ref=target, send_sem=send, recv_sem=recv, device_id=(blk, row), device_id_type=MESH
+    )
+
+
+def ahead_kernel(
+    tok_ref, grad_ref, vec_ref, w_ref, cos_ref, sin_ref, fq_ref, fk_ref,
+    x_out, g_out, h_out, ht_out, q_out, k_out, v_out, att_ref, lse_ref, ab_ref,
+    x_s, own_s, h_s, ht_s, q_s, k_s, v_s, w_s, zero_s, send_x, recv_x, send_g, recv_g, local
+):
+    step, last = pl.program_id(0), pl.num_programs(0) - 1
+    blk, row = lax.axis_index("blk"), lax.axis_index("rows")
+    rows_dev, stretch, width = tok_ref.shape
+    nblk = x_s.shape[0]
     half = width // H // 2
     scale = 1.0 / math.sqrt(2 * half)
-    cosine, sine = cos_ref[...], sin_ref[...]
-    for part in range(3):
-        out = dot(hidden, w_ref[:, part * width : (part + 1) * width])
-        for group in range(width // LANES):
-            cols = slice(group * LANES, (group + 1) * LANES)
-            piece = out[:, cols]
-            if part == 2:
-                v_ref[:, cols] = piece.astype(bf16)
-                continue
-            turned = (piece * cosine + swap_halves(piece, half) * sine).astype(bf16)
-            if part == 0:
-                q_ref[:, cols] = (turned.astype(f32) * scale).astype(bf16)
-            else:
-                k_ref[:, cols] = turned
-
-
-def project(x, factor, shift, w_qkv, cosine, sine):
-    seq, width = x.shape
-    rows = lambda cols: pl.BlockSpec((CHUNK, cols), lambda i: (i, 0))
-    fixed = lambda shape: pl.BlockSpec(shape, lambda i: (0, 0))
-    return pl.pallas_call(
-        project_kernel,
-        grid=(seq // CHUNK,),
-        in_specs=[
-            rows(width),
-            fixed((1, width)),
-            fixed((1, width)),
-            fixed(w_qkv.shape),
-            rows(LANES),
-            rows(LANES),
-        ],
-        out_specs=[rows(width)] * 4,
-        out_shape=[jax.ShapeDtypeStruct((seq, width), bf16)] * 4,
-        compiler_params=pltpu.CompilerParams(vmem_limit_bytes=40 * MIB),
-        cost_estimate=pl.CostEstimate(
-            flops=2 * seq * width * 3 * width, bytes_accessed=12 * seq * width, transcendentals=0
-        ),
-    )(x, factor, shift, w_qkv, cosine, sine)
-
-
-def attend_kernel(q_ref, k_ref, v_ref, fq_ref, fk_ref, att_ref, lse_ref):
-    seq = q_ref.shape[0]
+    has_row = blk < rows_dev
+    mine = jnp.minimum(blk, rows_dev - 1)
+    kept = ((x_s, x_out), (h_s, h_out), (ht_s, ht_out), (q_s, q_out), (k_s, k_out), (v_s, v_out))
+
+    def move(k, source, target, send, recv, other):
+        return remote(source.at[jnp.minimum(other, rows_dev - 1)], target.at[blk], send.at[k], recv.at[k], other, row)
+
+    def each_sent(source, target, send, recv, what):
+        for k in range(1, nblk):
+            other = partner(blk, k)
+
+            @pl.when(other < rows_dev)
+            def sent():
+                what(move(k, source, target, send, recv, other))
+
+    def store(i):
+        return pltpu.make_async_copy(kept[i][0], kept[i][1], local.at[i])
+
+    def own_grad():
+        return pltpu.make_async_copy(grad_ref.at[mine], g_out.at[blk], local.at[8])
+
+    def chunk(source):
+        rows = pl.ds(pl.multiple_of(source * stretch, stretch), stretch)
+        normed, unused = norm_rows(x_s[source].astype(f32))
+        hidden = normed * vec_ref[0:1, :] + vec_ref[1:2, :]
+        hidden_b = hidden.astype(bf16)
+        h_s[rows, :] = hidden_b
+        ht_s[:, rows] = hidden.T.astype(bf16)
+        cosine, sine = cos_ref[rows, :], sin_ref[rows, :]
+        for part in range(3):
+            out = dot(hidden_b, w_s[:, part * width : (part + 1) * width])
+            for group in range(width // LANES):
+                cols = slice(group * LANES, (group + 1) * LANES)
+                piece = out[:, cols]
+                if part == 2:
+                    v_s[rows, cols] = piece.astype(bf16)
+                    continue
+                turned = (piece * cosine + swap_halves(piece, half) * sine).astype(bf16)
+                if part == 0:
+                    q_s[rows, cols] = (turned.astype(f32) * scale).astype(bf16)
+                else:
+                    k_s[rows, cols] = turned
+
+    @pl.when(step == 0)
+    def begin():
+        barrier = pltpu.get_barrier_semaphore()
+        for k in range(1, nblk):
+            pl.semaphore_signal(barrier, inc=1, device_id=(partner(blk, k), row), device_id_type=MESH)
+        weights = pltpu.make_async_copy(w_ref, w_s, local.at[6])
+        weights.start()
+        own = pltpu.make_async_copy(tok_ref.at[mine], own_s, local.at[7])
+        own.start()
+        pl.semaphore_wait(barrier, nblk - 1)
+        each_sent(tok_ref, x_s, send_x, recv_x, lambda copy: copy.start())
+        own.wait()
+
+        @pl.when(has_row)
+        def mine_first():
+            x_s[blk] = own_s[...]
+
+        @pl.when(jnp.logical_not(has_row))
+        def nothing():
+            x_s[...] = jnp.zeros_like(x_s)
+
+        weights.wait()
+        for k in range(nblk):
+            source = partner(blk, k)
+            if k:
+                @pl.when(has_row)
+                def arrived():
+                    move(k, tok_ref, x_s, send_x, recv_x, source).wait_recv()
+
+            chunk(source)
+        each_sent(tok_ref, x_s, send_x, recv_x, lambda copy: copy.wait_send())
+        each_sent(grad_ref, g_out, send_g, recv_g, lambda copy: copy.start())
+        zero_s[...] = jnp.zeros_like(zero_s)
+
+        @pl.when(has_row)
+        def own_part():
+            own_grad().start()
+
+        @pl.when(jnp.logical_not(has_row))
+        def no_part():
+            for i in range(nblk):
+                pltpu.make_async_copy(zero_s, g_out.at[i], local.at[9 + i]).start()
+
+        for i in range(len(kept)):
+            store(i).start()
+
+    cols = pl.ds(pl.multiple_of(step * LANES, LANES), LANES)
+    seq = q_s.shape[0]
     first = lane_of((1, LANES)) < LANES // 2
     one = jnp.ones((), bf16)
-    for begin in range(0, seq, CHUNK):
-        rows = slice(begin, begin + CHUNK)
+    for start in range(0, seq, CHUNK):
+        rows = slice(start, start + CHUNK)
         pieces = []
         for head in range(2):
             own = first if head == 0 else jnp.logical_not(first)
-            keys = jnp.where(own, k_ref[...], fk_ref[...])
-            values = jnp.where(own, v_ref[...], one)
-            queries = jnp.where(own, q_ref[rows, :], fq_ref[rows, :])
+            keys = jnp.where(own, k_s[:, cols], fk_ref[...])
+            values = jnp.where(own, v_s[:, cols], one)
+            queries = jnp.where(own, q_s[rows, cols], fq_ref[rows, :])
             score = dot_nt(queries, keys)
             top = jnp.max(score, axis=-1, keepdims=True)
             weight = jnp.exp(score - top).astype(bf16)
             mixed = dot(weight, values)
             pieces.append((mixed / pltpu.roll(mixed, LANES // 2, 1), top + jnp.log(mixed)))
-        att_ref[rows, :] = jnp.where(first, pieces[0][0], pieces[1][0])
+        attended = jnp.where(first, pieces[0][0], pieces[1][0])
+        att_ref[rows, :] = attended
+        ab_ref[rows, :] = attended.astype(bf16)
         lse_ref[rows, :] = jnp.where(first, pieces[1][1], pieces[0][1])
 
-
-def attend(q, k, v, fq, fk):
-    seq, width = q.shape
+    @pl.when(step == last)
+    def end():
+        for i in range(len(kept)):
+            store(i).wait()
+        each_sent(grad_ref, g_out, send_g, recv_g, lambda copy: copy.wait_send())
+
+        @pl.when(has_row)
+        def received():
+            own_grad().wait()
+            for k in range(1, nblk):
+                move(k, grad_ref, g_out, send_g, recv_g, partner(blk, k)).wait_recv()
+
+        @pl.when(jnp.logical_not(has_row))
+        def cleared():
+            for i in range(nblk):
+                pltpu.make_async_copy(zero_s, g_out.at[i], local.at[9 + i]).wait()
+
+
+def ahead(tokens, grads, vec, w_qkv, cosine, sine, fq, fk, nblk):
+    rows_dev, stretch, width = tokens.shape
+    seq = nblk * stretch
     pair = pl.BlockSpec((seq, LANES), lambda i: (0, i))
     fixed = pl.BlockSpec((seq, LANES), lambda i: (0, 0))
+    away = pl.BlockSpec(memory_space=pl.ANY)
+    blocks, flat = (nblk, stretch, width), (seq, width)
+    shape = jax.ShapeDtypeStruct
     return pl.pallas_call(
-        attend_kernel,
+        ahead_kernel,
         grid=(width // LANES,),
-        in_specs=[pair, pair, pair, fixed, fixed],
-        out_specs=[pair, pair],
-        out_shape=[jax.ShapeDtypeStruct((seq, width), f32)] * 2,
-        compiler_params=pltpu.CompilerParams(vmem_limit_bytes=40 * MIB),
+        in_specs=[away, away, pl.BlockSpec(vec.shape, lambda i: (0, 0)), away, fixed, fixed, fixed, fixed],
+        out_specs=[away] * 7 + [pair] * 3,
+        out_shape=[
+            shape(blocks, bf16), shape(blocks, bf16), shape(flat, bf16), shape(flat[::-1], bf16),
+            shape(flat, bf16), shape(flat, bf16), shape(flat, bf16),
+            shape(flat, f32), shape(flat, f32), shape(flat, bf16),
+        ],
+        scratch_shapes=[
+            pltpu.VMEM(blocks, bf16), pltpu.VMEM((stretch, width), bf16), pltpu.VMEM(flat, bf16),
+            pltpu.VMEM(flat[::-1], bf16), pltpu.VMEM(flat, bf16), pltpu.VMEM(flat, bf16), pltpu.VMEM(flat, bf16),
+            pltpu.VMEM(w_qkv.shape, bf16), pltpu.VMEM((stretch, width), bf16),
+        ] + [pltpu.SemaphoreType.DMA((nblk,))] * 4 + [pltpu.SemaphoreType.DMA((9 + nblk,))],
+        compiler_params=pltpu.CompilerParams(
+            collective_id=1, has_side_effects=True, vmem_limit_bytes=56 * MIB
+        ),
         cost_estimate=pl.CostEstimate(
-            flops=16 * seq * seq * width, bytes_accessed=14 * seq * width, transcendentals=H * seq * seq
+            flops=22 * seq * seq * width, bytes_accessed=24 * seq * width, transcendentals=H * seq * seq
         ),
-    )(q, k, v, fq, fk)
+    )(tokens, grads, vec, w_qkv, cosine, sine, fq, fk)
 
 
 def attend_back_kernel(
@@ -226,6 +329,114 @@
     )(q, k, v, grads, att, lse, fq, fk, cosine, sine)
 
 
+GELU = math.sqrt(2.0 / math.pi)
+CUBE = 0.044715
+
+
+def feed_kernel(
+    ab_ref, x_ref, g_ref, vec_ref, w_out_ref, w_up_ref, b_up_ref, w_down_ref, b_down_ref,
+    result_ref, dx_ref, datt_ref, g_out_ref, g_up_ref, g_down_ref, gb_up_ref, sums_ref,
+    h_s, ht_s, dz_s, dzt_s, y_s, z_s, dh_s, act_s, du_s, dyt_s
+):
+    step, last = pl.program_id(0), pl.num_programs(0) - 1
+    seq, width = x_ref.shape
+    gate_a, factor_m, shift_m, gate_m = (vec_ref[i : i + 1, :] for i in range(4))
+    chunks = [slice(begin, begin + CHUNK) for begin in range(0, seq, CHUNK)]
+
+    @pl.when(step == 0)
+    def before():
+        for rows in chunks:
+            y = dot(ab_ref[rows, :], w_out_ref[...])
+            y_s[rows, :] = y
+            normed, unused = norm_rows(x_ref[rows, :].astype(f32) + gate_a * y)
+            hidden = normed * factor_m + shift_m
+            h_s[rows, :] = hidden.astype(bf16)
+            ht_s[:, rows] = hidden.T.astype(bf16)
+            grad = gate_m * g_ref[rows, :].astype(f32)
+            dz_s[rows, :] = grad.astype(bf16)
+            dzt_s[:, rows] = grad.T.astype(bf16)
+        z_s[...] = jnp.zeros_like(z_s)
+        dh_s[...] = jnp.zeros_like(dh_s)
+
+    bias_sum = jnp.zeros((1, w_up_ref.shape[1]), f32)
+    for rows in chunks:
+        u = dot(h_s[rows, :], w_up_ref[...]) + b_up_ref[...]
+        square = u * u
+        turn = jnp.tanh(GELU * u * (1.0 + CUBE * square))
+        half = 0.5 * (1.0 + turn)
+        act = (u * half).astype(bf16)
+        slope = half + (0.5 * GELU) * u * (1.0 - turn * turn) * (1.0 + 3.0 * CUBE * square)
+        du = (dot_nt(dz_s[rows, :], w_down_ref[...]) * slope).astype(bf16)
+        act_s[rows, :] = act
+        du_s[rows, :] = du
+        bias_sum = bias_sum + jnp.sum(du.astype(f32), axis=0, keepdims=True)
+        z_s[rows, :] += dot(act, w_down_ref[...])
+        dh_s[rows, :] += dot_nt(du, w_up_ref[...])
+    gb_up_ref[...] = bias_sum
+    g_up_ref[...] = dot(ht_s[...], du_s[...]).astype(bf16)
+    g_down_ref[...] = dot(dzt_s[...], act_s[...]).astype(bf16)
+
+    @pl.when(step == last)
+    def after():
+        sums = [jnp.zeros((1, width), f32) for unused in range(5)]
+        for rows in chunks:
+            y = y_s[rows, :]
+            middle = x_ref[rows, :].astype(f32) + gate_a * y
+            normed, inverse = norm_rows(middle)
+            z = z_s[rows, :] + b_down_ref[...]
+            result_ref[rows, :] = (middle + gate_m * z).astype(bf16)
+            grad = g_ref[rows, :].astype(f32)
+            dh = dh_s[rows, :]
+            dx = grad + norm_back(dh * factor_m, normed, inverse)
+            dx_ref[rows, :] = dx
+            dy = gate_a * dx
+            dyb = dy.astype(bf16)
+            dyt_s[rows, :] = dyb
+            datt_ref[rows, :] = dot_nt(dyb, w_out_ref[...]).astype(bf16)
+            terms = (grad * z, dh, dh * normed, dx * y, dz_s[rows, :].astype(f32))
+            sums = [a + jnp.sum(b, axis=0, keepdims=True) for a, b in zip(sums, terms)]
+        g_out_ref[...] = dot_tn(ab_ref[...], dyt_s[...]).astype(bf16)
+        for i in range(5):
+            sums_ref[i : i + 1, :] = sums[i]
+
+
+def feed(ab, x, g, vec, w_out, w_up, b_up, w_down, b_down):
+    seq, width = x.shape
+    ff = w_up.shape[1]
+    wide = width
+    fixed = lambda a: pl.BlockSpec(a.shape, lambda i: (0, 0))
+    one = lambda shape: pl.BlockSpec(shape, lambda i: (0, 0))
+    col = lambda r: pl.BlockSpec((r, wide), lambda i: (0, i))
+    shape = jax.ShapeDtypeStruct
+    return pl.pallas_call(
+        feed_kernel,
+        grid=(ff // wide,),
+        in_specs=[
+            fixed(ab), fixed(x), fixed(g), fixed(vec), fixed(w_out), col(width), col(1),
+            pl.BlockSpec((wide, width), lambda i: (i, 0)), fixed(b_down),
+        ],
+        out_specs=[
+            one((seq, width)), one((seq, width)), one((seq, width)), one((width, width)),
+            col(width), col(width), col(1), one((8, width)),
+        ],
+        out_shape=[
+            shape((seq, width), bf16), shape((seq, width), f32), shape((seq, width), bf16),
+            shape((width, width), bf16), shape((width, ff), bf16), shape((width, ff), bf16),
+            shape((1, ff), f32), shape((8, width), f32),
+        ],
+        scratch_shapes=[
+            pltpu.VMEM((seq, width), bf16), pltpu.VMEM((width, seq), bf16),
+            pltpu.VMEM((seq, width), bf16), pltpu.VMEM((width, seq), bf16),
+            pltpu.VMEM((seq, width), f32), pltpu.VMEM((seq, width), f32), pltpu.VMEM((seq, width), f32),
+            pltpu.VMEM((seq, wide), bf16), pltpu.VMEM((seq, wide), bf16), pltpu.VMEM((seq, width), bf16),
+        ],
+        compiler_params=pltpu.CompilerParams(vmem_limit_bytes=60 * MIB),
+        cost_estimate=pl.CostEstimate(
+            flops=12 * seq * width * ff, bytes_accessed=30 * seq * width, transcendentals=seq * ff
+        ),
+    )(ab, x, g, vec, w_out, w_up, b_up, w_down, b_down)
+
+
 def gather_kernel(nblk, nrows, in_ref, out_ref, send_r, recv_r, send_b, recv_b):
     blk, row = lax.axis_index("blk"), lax.axis_index("rows")
     barrier = pltpu.get_barrier_semaphore()
@@ -297,18 +508,6 @@
         ],
         compiler_params=pltpu.CompilerParams(collective_id=0, has_side_effects=True),
     )(vector.reshape(count, LANES))
-
-
-def rows_in(pieces, me, nblk):
-    rows = pieces.shape[0]
-    parts = [lax.dynamic_index_in_dim(pieces, jnp.minimum(me, rows - 1), 0, keepdims=False)]
-    for k in range(1, nblk):
-        part = lax.dynamic_index_in_dim(pieces, jnp.minimum(me ^ k, rows - 1), 0, keepdims=False)
-        pairs = [(s, s ^ k) for s in range(nblk) if s ^ k < rows]
-        parts.append(lax.ppermute(part, "blk", pairs))
-    stacked = jnp.stack(parts)
-    whole = jnp.take(stacked, jnp.arange(nblk) ^ me, axis=0)
-    return jnp.where(me < rows, whole, jnp.zeros_like(whole))
 
 
 def rows_out(whole, rows, me, nblk):
@@ -379,9 +578,6 @@
     head_dim = width // H
     mine = jnp.minimum(blk, rows_dev - 1)
 
-    x_blocks = rows_in(tokens, blk, nblk)
-    g_blocks = rows_in(grad_out, blk, nblk)
-
     slots = jnp.arange(seq, dtype=jnp.int32)
     ends = jnp.cumsum(pick(lengths, mine))
     before = ends[None, :] <= slots[:, None]
@@ -408,49 +604,31 @@
     factor_a = gain_a * (1.0 + scale_a)
     factor_m = gain_m * (1.0 + scale_m)
 
+    vec = jnp.concatenate([factor_a, shift_a], axis=0)
+    x_blocks, g_blocks, hidden_a, hidden_t, q, k, v, attended, lse, attended_b = ahead(
+        tokens, grad_out, vec, w_qkv, cosine, sine, fq, fk, nblk
+    )
     x_row = x_blocks.reshape(seq, width)
-    hidden_a, q, k, v = project(x_row, factor_a, shift_a, w_qkv, cosine, sine)
-    attended, lse = attend(q, k, v, fq, fk)
-    attended_b = attended.astype(bf16)
-    branch_a = dot(attended_b, w_out)
-    inputs = x_row.astype(f32)
-    middle = inputs + gate_a * branch_a
-    normed_m, inverse_m = norm_rows(middle)
-    hidden_m = (normed_m * factor_m + shift_m).astype(bf16)
-    pre = dot(hidden_m, w_up) + b_up.astype(f32)
-    gelu_value, gelu_pull = jax.vjp(lambda values: jax.nn.gelu(values, approximate=True), pre)
-    active = gelu_value.astype(bf16)
-    branch_m = dot(active, w_down) + b_down.astype(f32)
-    result = (middle + gate_m * branch_m).astype(bf16)
+
+    g_row = g_blocks.reshape(seq, width)
+    vec = jnp.concatenate([gate_a, factor_m, shift_m, gate_m], axis=0)
+    result, grad_mid, grad_att, grad_w_out, grad_w_up, grad_w_down, gb_up, sums = feed(
+        attended_b, x_row, g_row, vec, w_out, w_up, b_up.astype(f32)[None, :], w_down,
+        b_down.astype(f32)[None, :]
+    )
     out = rows_out(result.reshape(nblk, stretch, width), rows_dev, blk, nblk)
-
-    grad = g_blocks.reshape(seq, width).astype(f32)
-    grad_branch = (gate_m * grad).astype(bf16)
-    grad_w_down = dot_tn(active, grad_branch).astype(bf16)
-    share_w_down = reduce_weight(grad_w_down, blk, row, nblk, nrows)
-    grad_b_down = jnp.sum(grad_branch.astype(f32), axis=0)
-    dgate_m = jnp.sum(grad * branch_m, axis=0)
-    grad_active = dot_nt(grad_branch, w_down)
-    grad_pre = gelu_pull(grad_active)[0].astype(bf16)
-    grad_w_up = dot_tn(hidden_m, grad_pre).astype(bf16)
+    dgate_m, dshift_m, along_m, dgate_a, grad_b_down = (sums[i] for i in range(5))
+    grad_b_up = gb_up[0]
+    share_w_down = reduce_weight(grad_w_down.T, blk, row, nblk, nrows)
     share_w_up = reduce_weight(grad_w_up, blk, row, nblk, nrows)
-    grad_b_up = jnp.sum(grad_pre.astype(f32), axis=0)
-    grad_hm = dot_nt(grad_pre, w_up)
-    dshift_m = jnp.sum(grad_hm, axis=0)
-    along_m = jnp.sum(grad_hm * normed_m, axis=0)
-    grad_mid = grad + norm_back(grad_hm * factor_m, normed_m, inverse_m)
-    dgate_a = jnp.sum(grad_mid * branch_a, axis=0)
-    grad_ya = (gate_a * grad_mid).astype(bf16)
-    grad_w_out = dot_tn(attended_b, grad_ya).astype(bf16)
     share_w_out = reduce_weight(grad_w_out, blk, row, nblk, nrows)
-    grad_att = dot_nt(grad_ya, w_out).astype(bf16)
 
     dq, dk, dv = attend_back(q, k, v, grad_att, attended, lse, fq, fk, cosine, sine)
     grad_qkv = jnp.concatenate([dq, dk, dv], axis=-1)
-    grad_w_qkv = dot_tn(hidden_a, grad_qkv).astype(bf16)
+    grad_w_qkv = dot(hidden_t, grad_qkv).astype(bf16)
     share_w_qkv = reduce_weight(grad_w_qkv, blk, row, nblk, nrows)
     grad_ha = dot_nt(grad_qkv, w_qkv)
-    normed_a, inverse_a = norm_rows(inputs)
+    normed_a, inverse_a = norm_rows(x_row.astype(f32))
     dshift_a = jnp.sum(grad_ha, axis=0)
     along_a = jnp.sum(grad_ha * normed_a, axis=0)
     grad_in = (grad_mid + norm_back(grad_ha * factor_a, normed_a, inverse_a)).astype(bf16)

time: 435 us -> 461 us (1.060)
  Pallas kernels: 101 us -> 173 us
  matrix products: 87.8 us -> 17.1 us
  local copies, waits for them, and re-layouts: 40.3 us -> 88.8 us
  starting transfers between devices: 84.9 us -> 64.8 us
    pallas_call x2, Pallas kernels: 31.5 us -> 101 us  [the longest x1 51.8 us: ahead(): pl.pallas_call(ahead_kernel, grid=(width // LANES,), in_specs=[away, away...]
    dot_general x4 -> x1, matrix products: 35.8 us -> 5.9 us  [dot_nt(): lax.dot_general(a, b, (((1,), (1,)), ((), ())), preferred_element_type=f32)]
    unnamed x175 -> x95, local copies, waits for them, and re-layouts: 10.1 us -> 33.7 us
    dot_general x4 -> x0, matrix products: 23.1 us -> none  [dot_tn(): lax.dot_general(a, b, (((0,), (0,)), ((), ())), preferred_element_type=f32)]
    ppermute x6 -> x0, starting transfers between devices: 19.5 us -> none  [rows_in(): parts.append(lax.ppermute(part, 'blk', pairs))]
    dot_general x3 -> x1, matrix products: 24.3 us -> 6.63 us  [dot(): return jnp.dot(a, b, preferred_element_type=f32)]
    dynamic_slice x1 -> x2, local copies, waits for them, and re-layouts: 0.58 us -> 13.6 us  [pick(): return lax.dynamic_index_in_dim(array, index, axis, keepdims=False)]
    reshape x0 -> x1, local copies, waits for them, and re-layouts: none -> 11.6 us  [reduce_weight(): part = halve(grad.reshape(nz, 2, share, cols), 1, core, 'rows', nrows, 1)]
  transfers between devices with their start and end apart: 56 -> 50, of which waited for: 20 -> 17; matrix products, arithmetic and copies ran while one was open for 17% -> 26% of each run, Pallas kernels for 0% -> 7%
where the time goes in v2:
time: 461 us; the launch traced here: 456 us
  Pallas kernels  173 us (38%)
  local copies, waits for them, and re-layouts  88.8 us (19%)
  starting transfers between devices  64.8 us (14%)
  waiting for transfers between devices  58.4 us (13%)
  other arithmetic  49.2 us (11%)
  matrix products  17.1 us (4%)
  between operations  4.75 us (1%)
    ppermute x44, waiting for transfers between devices, xor_move(): return lax.ppermute(array, axis, [(s, s ^ k) for s in range(size)])  58.4 us
    pallas_call x1, Pallas kernels, ahead(): pl.pallas_call(ahead_kernel, grid=(width // LANES,), in_specs=[away, away...  51.8 us
    pallas_call x1, Pallas kernels, feed(): pl.pallas_call(feed_kernel, grid=(ff // wide,), in_specs=[fixed(ab), fixe...  48.8 us
    ppermute x44, starting transfers between devices, xor_move(): return lax.ppermute(array, axis, [(s, s ^ k) for s in range(size)])  47.3 us
    pallas_call x1, Pallas kernels, attend_back(): pl.pallas_call(attend_back_kernel, grid=(width // LANES,), in_specs=[pair...  41.5 us
    unnamed x95, local copies, waits for them, and re-layouts  33.7 us
    pallas_call x1, Pallas kernels, gather_all(): pl.pallas_call(functools.partial(gather_kernel, nblk, nrows), out_shape=j...  30.5 us
    ppermute x6, starting transfers between devices, rows_out(): parts.append(lax.ppermute(part, 'blk', pairs))  17.5 us
  transfers between devices with their start and end apart: 50, of which 17 were waited for; matrix products, arithmetic and copies ran while one was open for 26% of the time, Pallas kernels for 7%

profile of v2, /device:TPU:0, one launch (start us, length us, event | category | flops | bytes accessed | tf_op | source)
XLA Modules:
  0.0 455.7 jit_solution(3647729206099527055)
XLA Ops:
  16.3 51.8 %shard_map.246 = (bf16[4,256,768]{2,1,0:T(8,128)(2,1)}, bf16[4,256,768]{2,1,0:T(8,128)(2,1)}, bf16[1024,768]{1,0:T(8,128)(2,1)}, bf16[768,1024]{1,0:T(8,128)(2,1...) custom-call(bf16[3,256,768]{2,1,0:T(8,128)(2,1)} %tok_ref.1, ...), custom_call_target="tpu_custom_call" | custom-call | flops 17716740096 | bytes 18874368 | tf_op jit(solution)/shard_map/pallas_call | solution.py:234
  71.3 48.8 %shard_map.247 = (bf16[1024,768]{1,0:T(8,128)(2,1)}, f32[1024,768]{1,0:T(8,128)}, bf16[1024,768]{1,0:T(8,128)(2,1)}, bf16[768,768]{1,0:T(8,128)(2,1)}, bf16[768,...) custom-call(bf16[1024,768]{1,0:T(8,128)(2,1)} %get-tuple-element.34.ab_ref, ...), custom_call_target="tpu_custom_call" | custom-call | flops 28991029248 | bytes 23592960 | tf_op jit(solution)/shard_map/pallas_call | solution.py:411
  120.1 41.5 %shard_map.248 = (bf16[1024,768]{1,0:T(8,128)(2,1)S(1)}, bf16[1024,768]{1,0:T(8,128)(2,1)S(1)}, bf16[1024,768]{1,0:T(8,128)(2,1)}) custom-call(bf16[1024,768]{1,0:T(8,128)(2,1)} %get-tuple-element.39.q_ref, bf16[1024,768]{1,0:T(8,128)(2,1)} %get-tuple-element.40.k_ref, bf16[1024,768]{1,0:T(8,128)(2,1)} %get-tuple-element.41.v_ref, ...), custom_call_target="tpu_custom_call" | custom-call | flops 32212254720 | bytes 18874368 | tf_op jit(solution)/shard_map/pallas_call | solution.py:314
  165.7 5.9 %multiply_reduce_fusion = (f32[768]{0:T(1024)S(1)}, f32[1024]{0:T(1024)S(1)}, f32[1024]{0:T(1024)S(1)}, f32[768]{0:T(1024)S(1)}, f32[1024,768]{1,0:T(8,128)}) fusion(f32[1024]{0:T(1024)S(1)} %bitcast.389, f32[1024]{0:T(1024)S(1)} %bitcast.391, bf16[4,256,768]{2,1,0:T(8,128)(2,1)S(1)} %copy-done.6, f32[768]{0:T(1024)S(1)} %get-tuple-element.125, ...), kind=kOutput, calls=%fused_computation.17 | convolution fusion | flops 3631739392 | bytes 13001728 | tf_op jit(solution)/shard_map/dot_general | solution.py:29
  171.6 3.5 add_convert_fusion
  178.3 5.3 %collective-permute-start.4 = (bf16[256,768]{1,0:T(8,128)(2,1)}, bf16[256,768]{1,0:T(8,128)(2,1)}, u32[]{:S(2)}, u32[]{:S(2)}) collective-permute-start(bf16[256,768]{1,0:T(8,128)(2,1)} %get-tuple-element.79), channel_id=1, source_target_pairs={{0,16},{8,24},{16,0},{1,17},{9,25},{17,1},{2,18},{10,26},{18,2},{3... | collective-permute-start | bytes 1179656 | tf_op jit(solution)/shard_map/ppermute | solution.py:518
  191.4 30.5 %shard_map.249 = f32[4,8,79,128]{3,2,1,0:T(8,128)} custom-call(f32[79,128]{1,0:T(8,128)} %bitcast.385), custom_call_target="tpu_custom_call" | custom-call | tf_op jit(solution)/shard_map/pallas_call | solution.py:498
  228.3 6.6 %convolution_convert_fusion = bf16[768,2304]{1,0:T(8,128)(2,1)S(1)} fusion(bf16[768,1024]{1,0:T(8,128)(2,1)} %get-tuple-element.50, bf16[1024,2304]{1,0:T(8,128)(2,1)} %copy-done.23), kind=kOutput, calls=%fused_computation.6 | convolution fusion | flops 3625648128 | bytes 9830400 | tf_op jit(solution)/shard_map/dot_general | solution.py:25
  238.1 11.6 %reshape.287 = bf16[4,2,384,768]{2,1,0,3:T(2,128)(2,1)} reshape(bf16[3072,768]{0,1:T(8,128)(2,1)} %bitcast.329) | data formatting | bytes 9437184 | tf_op jit(solution)/shard_map/reshape | solution.py:543
  249.7 12.3 %constant_dynamic-slice_fusion.1 = (bf16[4,1,384,768]{2,1,0,3:T(2,128)(2,1)}, bf16[4,1,384,768]{2,1,0,3:T(2,128)(2,1)}) fusion(bf16[4,2,384,768]{2,1,0,3:T(2,128)(2,1)} %reshape.287, s32[]{:T(128)S(6)} %select_n.255, s32[]{:T(128)S(6)} %select_n.256), kind=kLoop, calls=%fused_computation.267 | loop fusion | bytes 9437192 | tf_op jit(solution)/shard_map/jit(dynamic_index_in_dim)/dynamic_slice | solution.py:524
  262.0 11.8 %copy.89 = bf16[4,1,384,768]{3,2,0,1:T(8,128)(2,1)} copy(bf16[4,1,384,768]{2,1,0,3:T(2,128)(2,1)} %get-tuple-element.70) | data formatting | bytes 4718592
  273.7 10.1 %copy.88 = bf16[4,1,384,768]{3,2,0,1:T(8,128)(2,1)S(1)} copy(bf16[4,1,384,768]{2,1,0,3:T(2,128)(2,1)} %get-tuple-element.69) | data formatting | bytes 4718592
  285.3 3.3 dynamic-slice_bitcast_fusion
  288.6 2.7 collective-permute-start.1
  293.6 3.5 collective-permute-start
  298.1 2.6 pad_maximum_fusion.1
  300.7 8.8 %collective-permute-done.18 = bf16[2,2,48,384]{3,2,0,1:T(8,128)(2,1)S(1)} collective-permute-done((bf16[2,2,48,384]{3,2,0,1:T(8,128)(2,1)S(1)}, bf16[2,2,48,384]{3,2,0,1:T(8,128)(2,1)S(1)}, u32[]{:S(2)}, u32[]{:S(2)}) %collective-permute-start.18) | collective-permute-done | bytes 147488 | tf_op jit(solution)/shard_map/ppermute | solution.py:528
  309.6 5.0 %collective-permute-done.20 = bf16[2,48,768]{2,1,0:T(8,128)(2,1)S(1)} collective-permute-done((bf16[2,48,768]{2,1,0:T(8,128)(2,1)S(1)}, bf16[2,48,768]{2,1,0:T(8,128)(2,1)S(1)}, u32[]{:S(2)}, u32[]{:S(2)}) %collective-permute-start.20) | collective-permute-done | bytes 147488 | tf_op jit(solution)/shard_map/ppermute | solution.py:528
  314.7 4.2 collective-permute-done.19
  320.2 3.1 collective-permute-done.21
  324.1 3.6 collective-permute-start.24
  330.9 3.1 gather_fusion.5
  333.9 3.1 gather_fusion.4
  341.4 3.3 broadcast_select_fusion
  353.0 10.1 %collective-permute-done.7 = bf16[2,2,48,1152]{3,2,0,1:T(8,128)(2,1)S(1)} collective-permute-done((bf16[2,2,48,1152]{3,2,0,1:T(8,128)(2,1)S(1)}, bf16[2,2,48,1152]{3,2,0,1:T(8,128)(2,1)S(1)}, u32[]{:S(2)}, u32[]{:S(2)}) %collective-permute-start.7) | collective-permute-done | bytes 442400 | tf_op jit(solution)/shard_map/ppermute | solution.py:528
  366.5 2.6 fusion.1
  376.1 3.8 collective-permute-start.13
  383.3 4.8 %collective-permute-done.12 = bf16[48,1152]{1,0:T(8,128)(2,1)S(1)} collective-permute-done((bf16[48,1152]{1,0:T(8,128)(2,1)S(1)}, bf16[48,1152]{1,0:T(8,128)(2,1)S(1)}, u32[]{:S(2)}, u32[]{:S(2)}) %collective-permute-start.12) | collective-permute-done | bytes 110624 | tf_op jit(solution)/shard_map/ppermute | solution.py:528
  415.0 3.9 collective-permute-done.30
  420.3 3.5 collective-permute-start.33
  429.7 4.8 %collective-permute-done.34 = bf16[48,1536]{1,0:T(8,128)(2,1)S(1)} collective-permute-done((bf16[48,1536]{1,0:T(8,128)(2,1)S(1)}, bf16[48,1536]{1,0:T(8,128)(2,1)S(1)}, u32[]{:S(2)}, u32[]{:S(2)}) %collective-permute-start.34) | collective-permute-done | bytes 147488 | tf_op jit(solution)/shard_map/ppermute | solution.py:528
  436.0 4.1 collective-permute-start.37
  (305 shorter events, 127.5 us)
Async XLA Ops:
  176.3 116.5 %collective-permute-start.5 = (bf16[256,768]{1,0:T(8,128)(2,1)}, bf16[256,768]{1,0:T(8,128)(2,1)}, u32[]{:S(2)}, u32[]{:S(2)}) collective-permute-start(bf16[256,768]{1,0:T(8,128)(2,1)} %get-tuple-element.78), channel_id=1, source_target_pairs={{0,24},{8,16},{16,8},{1,25},{9,17},{17,9},{2,26},{10,18},{18,10},{... | collective-permute-start | bytes 1179656 | tf_op jit(solution)/shard_map/ppermute | solution.py:518
  178.3 118.7 %collective-permute-start.4 = (bf16[256,768]{1,0:T(8,128)(2,1)}, bf16[256,768]{1,0:T(8,128)(2,1)}, u32[]{:S(2)}, u32[]{:S(2)}) collective-permute-start(bf16[256,768]{1,0:T(8,128)(2,1)} %get-tuple-element.79), channel_id=1, source_target_pairs={{0,16},{8,24},{16,0},{1,17},{9,25},{17,1},{2,18},{10,26},{18,2},{3... | collective-permute-start | bytes 1179656 | tf_op jit(solution)/shard_map/ppermute | solution.py:518
  183.6 113.5 %collective-permute-start.3 = (bf16[256,768]{1,0:T(8,128)(2,1)}, bf16[256,768]{1,0:T(8,128)(2,1)}, u32[]{:S(2)}, u32[]{:S(2)}) collective-permute-start(bf16[256,768]{1,0:T(8,128)(2,1)} %get-tuple-element.80), channel_id=1, source_target_pairs={{0,8},{8,0},{16,24},{1,9},{9,1},{17,25},{2,10},{10,2},{18,26},{3,1... | collective-permute-start | bytes 1179656 | tf_op jit(solution)/shard_map/ppermute | solution.py:518
  186.8 137.3 %collective-permute-start.2 = (bf16[256,768]{1,0:T(8,128)(2,1)}, bf16[256,768]{1,0:T(8,128)(2,1)}, u32[]{:S(2)}, u32[]{:S(2)}) collective-permute-start(bf16[256,768]{1,0:T(8,128)(2,1)} %get-tuple-element.82), channel_id=1, source_target_pairs={{0,24},{8,16},{16,8},{1,25},{9,17},{17,9},{2,26},{10,18},{18,10},{... | collective-permute-start | bytes 1179656 | tf_op jit(solution)/shard_map/ppermute | solution.py:518
  189.8 98.8 %collective-permute-start.17 = (bf16[4,96,768]{2,1,0:T(8,128)(2,1)}, bf16[4,96,768]{2,1,0:T(8,128)(2,1)}, u32[]{:S(2)}, u32[]{:S(2)}) collective-permute-start(bf16[4,96,768]{2,1,0:T(8,128)(2,1)} %dynamic-slice_bitcast_fusion.4), channel_id=1, source_target_pairs={{0,1},{1,0},{2,3},{3,2},{4,5},{5,4},{6,7},{7,6},{8,9},{9,8},{10,11... | collective-permute-start | bytes 1769480 | tf_op jit(solution)/shard_map/ppermute | solution.py:528
  288.6 39.1 %collective-permute-start.1 = (bf16[256,768]{1,0:T(8,128)(2,1)S(1)}, bf16[256,768]{1,0:T(8,128)(2,1)S(1)}, u32[]{:S(2)}, u32[]{:S(2)}) collective-permute-start(bf16[256,768]{1,0:T(8,128)(2,1)S(1)} %copy-done.25), channel_id=1, source_target_pairs={{0,16},{8,24},{16,0},{1,17},{9,25},{17,1},{2,18},{10,26},{18,2},{3... | collective-permute-start | bytes 1179656 | tf_op jit(solution)/shard_map/ppermute | solution.py:518
  293.6 34.1 %collective-permute-start = (bf16[256,768]{1,0:T(8,128)(2,1)S(1)}, bf16[256,768]{1,0:T(8,128)(2,1)S(1)}, u32[]{:S(2)}, u32[]{:S(2)}) collective-permute-start(bf16[256,768]{1,0:T(8,128)(2,1)S(1)} %copy-done.24), channel_id=1, source_target_pairs={{0,8},{8,0},{16,24},{1,9},{9,1},{17,25},{2,10},{10,2},{18,26},{3,1... | collective-permute-start | bytes 1179656 | tf_op jit(solution)/shard_map/ppermute | solution.py:518
  297.1 50.5 %collective-permute-start.6 = (bf16[4,96,2304]{2,1,0:T(8,128)(2,1)}, bf16[4,96,2304]{2,1,0:T(8,128)(2,1)}, u32[]{:S(2)}, u32[]{:S(2)}) collective-permute-start(bf16[4,96,2304]{2,1,0:T(8,128)(2,1)} %dynamic-slice_bitcast_fusion.1), channel_id=1, source_target_pairs={{0,1},{1,0},{2,3},{3,2},{4,5},{5,4},{6,7},{7,6},{8,9},{9,8},{10,11... | collective-permute-start | bytes 5308424 | tf_op jit(solution)/shard_map/ppermute | solution.py:528
  297.2 12.3 %collective-permute-start.18 = (bf16[2,2,48,384]{3,2,0,1:T(8,128)(2,1)S(1)}, bf16[2,2,48,384]{3,2,0,1:T(8,128)(2,1)S(1)}, u32[]{:S(2)}, u32[]{:S(2)}) collective-permute-start(bf16[2,2,48,384]{3,2,0,1:T(8,128)(2,1)S(1)} %fusion.60), channel_id=1, source_target_pairs={{0,8},{8,0},{16,24},{24,16},{1,9},{9,1},{17,25},{25,17},{2,10},{10... | collective-permute-start | bytes 442376 | tf_op jit(solution)/shard_map/ppermute | solution.py:528
  323.3 43.2 %collective-permute-start.28 = (bf16[4,96,3072]{2,1,0:T(8,128)(2,1)}, bf16[4,96,3072]{2,1,0:T(8,128)(2,1)}, u32[]{:S(2)}, u32[]{:S(2)}) collective-permute-start(bf16[4,96,3072]{2,1,0:T(8,128)(2,1)} %dynamic-slice_bitcast_fusion), channel_id=1, source_target_pairs={{0,1},{1,0},{2,3},{3,2},{4,5},{5,4},{6,7},{7,6},{8,9},{9,8},{10,11... | collective-permute-start | bytes 7077896 | tf_op jit(solution)/shard_map/ppermute | solution.py:528
  324.1 12.9 %collective-permute-start.24 = (bf16[48,384]{1,0:T(8,128)(2,1)}, bf16[48,384]{1,0:T(8,128)(2,1)}, u32[]{:S(2)}, u32[]{:S(2)}) collective-permute-start(bf16[48,384]{1,0:T(8,128)(2,1)} %get-tuple-element.114), channel_id=1, source_target_pairs={{0,6},{1,7},{2,4},{3,5},{4,2},{5,3},{6,0},{7,1},{8,14},{9,15},{10,... | collective-permute-start | bytes 110600 | tf_op jit(solution)/shard_map/ppermute | solution.py:528
  327.7 9.3 %collective-permute-start.23 = (bf16[48,384]{1,0:T(8,128)(2,1)}, bf16[48,384]{1,0:T(8,128)(2,1)}, u32[]{:S(2)}, u32[]{:S(2)}) collective-permute-start(bf16[48,384]{1,0:T(8,128)(2,1)} %get-tuple-element.113), channel_id=1, source_target_pairs={{0,4},{1,5},{2,6},{3,7},{4,0},{5,1},{6,2},{7,3},{8,12},{9,13},{10,... | collective-permute-start | bytes 110600 | tf_op jit(solution)/shard_map/ppermute | solution.py:528
  344.8 28.4 %collective-permute-start.39 = (bf16[4,384,768]{2,1,0:T(8,128)(2,1)}, bf16[4,384,768]{2,1,0:T(8,128)(2,1)}, u32[]{:S(2)}, u32[]{:S(2)}) collective-permute-start(bf16[4,384,768]{2,1,0:T(8,128)(2,1)} %bitcast.112), channel_id=1, source_target_pairs={{0,1},{1,0},{2,3},{3,2},{4,5},{5,4},{6,7},{7,6},{8,9},{9,8},{10,11... | collective-permute-start | bytes 7077896 | tf_op jit(solution)/shard_map/ppermute | solution.py:528
  350.5 12.6 %collective-permute-start.7 = (bf16[2,2,48,1152]{3,2,0,1:T(8,128)(2,1)S(1)}, bf16[2,2,48,1152]{3,2,0,1:T(8,128)(2,1)S(1)}, u32[]{:S(2)}, u32[]{:S(2)}) collective-permute-start(bf16[2,2,48,1152]{3,2,0,1:T(8,128)(2,1)S(1)} %fusion.27), channel_id=1, source_target_pairs={{0,8},{8,0},{16,24},{24,16},{1,9},{9,1},{17,25},{25,17},{2,10},{10... | collective-permute-start | bytes 1327112 | tf_op jit(solution)/shard_map/ppermute | solution.py:528
  352.9 12.4 %collective-permute-start.9 = (bf16[2,48,2304]{2,1,0:T(8,128)(2,1)S(1)}, bf16[2,48,2304]{2,1,0:T(8,128)(2,1)S(1)}, u32[]{:S(2)}, u32[]{:S(2)}) collective-permute-start(bf16[2,48,2304]{2,1,0:T(8,128)(2,1)S(1)} %dynamic-slice_bitcast_fusion.5), channel_id=1, source_target_pairs={{0,16},{8,24},{16,0},{24,8},{1,17},{9,25},{17,1},{25,9},{2,18},{10... | collective-permute-start | bytes 1327112 | tf_op jit(solution)/shard_map/ppermute | solution.py:528
  363.4 12.2 %collective-permute-start.8 = (bf16[2,48,1152]{2,1,0:T(8,128)(2,1)S(1)}, bf16[2,48,1152]{2,1,0:T(8,128)(2,1)S(1)}, u32[]{:S(2)}, u32[]{:S(2)}) collective-permute-start(bf16[2,48,1152]{2,1,0:T(8,128)(2,1)S(1)} %dynamic-slice_bitcast_fusion.14), channel_id=1, source_target_pairs={{0,16},{8,24},{16,0},{24,8},{1,17},{9,25},{17,1},{25,9},{2,18},{10... | collective-permute-start | bytes 663560 | tf_op jit(solution)/shard_map/ppermute | solution.py:528
  365.5 10.3 %collective-permute-start.10 = (bf16[2,48,1152]{2,1,0:T(8,128)(2,1)S(1)}, bf16[2,48,1152]{2,1,0:T(8,128)(2,1)S(1)}, u32[]{:S(2)}, u32[]{:S(2)}) collective-permute-start(bf16[2,48,1152]{2,1,0:T(8,128)(2,1)S(1)} %fusion.52), channel_id=1, source_target_pairs={{0,8},{8,0},{16,24},{24,16},{1,9},{9,1},{17,25},{25,17},{2,10},{10... | collective-permute-start | bytes 663560 | tf_op jit(solution)/shard_map/ppermute | solution.py:528
  370.9 32.1 %collective-permute-start.29 = (bf16[2,2,48,1536]{3,2,0,1:T(8,128)(2,1)}, bf16[2,2,48,1536]{3,2,0,1:T(8,128)(2,1)}, u32[]{:S(2)}, u32[]{:S(2)}) collective-permute-start(bf16[2,2,48,1536]{3,2,0,1:T(8,128)(2,1)} %fusion.18), channel_id=1, source_target_pairs={{0,8},{8,0},{16,24},{24,16},{1,9},{9,1},{17,25},{25,17},{2,10},{10... | collective-permute-start | bytes 1769480 | tf_op jit(solution)/shard_map/ppermute | solution.py:528
  372.8 32.8 %collective-permute-start.31 = (bf16[2,48,3072]{2,1,0:T(8,128)(2,1)}, bf16[2,48,3072]{2,1,0:T(8,128)(2,1)}, u32[]{:S(2)}, u32[]{:S(2)}) collective-permute-start(bf16[2,48,3072]{2,1,0:T(8,128)(2,1)} %dynamic-slice_bitcast_fusion.3), channel_id=1, source_target_pairs={{0,16},{8,24},{16,0},{24,8},{1,17},{9,25},{17,1},{25,9},{2,18},{10... | collective-permute-start | bytes 1769480 | tf_op jit(solution)/shard_map/ppermute | solution.py:528
  394.9 14.4 %collective-permute-start.40 = (bf16[2,2,192,384]{3,2,1,0:T(8,128)(2,1)}, bf16[2,2,192,384]{3,2,1,0:T(8,128)(2,1)}, u32[]{:S(2)}, u32[]{:S(2)}) collective-permute-start(bf16[2,2,192,384]{3,2,1,0:T(8,128)(2,1)} %fusion.14), channel_id=1, source_target_pairs={{0,8},{8,0},{16,24},{24,16},{1,9},{9,1},{17,25},{25,17},{2,10},{10... | collective-permute-start | bytes 1769480 | tf_op jit(solution)/shard_map/ppermute | solution.py:528
  396.1 16.6 %collective-permute-start.42 = (bf16[2,192,768]{2,1,0:T(8,128)(2,1)}, bf16[2,192,768]{2,1,0:T(8,128)(2,1)}, u32[]{:S(2)}, u32[]{:S(2)}) collective-permute-start(bf16[2,192,768]{2,1,0:T(8,128)(2,1)} %dynamic-slice_bitcast_fusion.2), channel_id=1, source_target_pairs={{0,16},{8,24},{16,0},{24,8},{1,17},{9,25},{17,1},{25,9},{2,18},{10... | collective-permute-start | bytes 1769480 | tf_op jit(solution)/shard_map/ppermute | solution.py:528
  404.5 14.4 %collective-permute-start.30 = (bf16[2,48,1536]{2,1,0:T(8,128)(2,1)S(1)}, bf16[2,48,1536]{2,1,0:T(8,128)(2,1)S(1)}, u32[]{:S(2)}, u32[]{:S(2)}) collective-permute-start(bf16[2,48,1536]{2,1,0:T(8,128)(2,1)S(1)} %dynamic-slice_bitcast_fusion.13), channel_id=1, source_target_pairs={{0,16},{8,24},{16,0},{24,8},{1,17},{9,25},{17,1},{25,9},{2,18},{10... | collective-permute-start | bytes 884744 | tf_op jit(solution)/shard_map/ppermute | solution.py:528
  407.0 12.0 %collective-permute-start.32 = (bf16[2,48,1536]{2,1,0:T(8,128)(2,1)S(1)}, bf16[2,48,1536]{2,1,0:T(8,128)(2,1)S(1)}, u32[]{:S(2)}, u32[]{:S(2)}) collective-permute-start(bf16[2,48,1536]{2,1,0:T(8,128)(2,1)S(1)} %fusion.40), channel_id=1, source_target_pairs={{0,8},{8,0},{16,24},{24,16},{1,9},{9,1},{17,25},{25,17},{2,10},{10... | collective-permute-start | bytes 884744 | tf_op jit(solution)/shard_map/ppermute | solution.py:528
  410.7 13.1 %collective-permute-start.41 = (bf16[2,192,384]{2,1,0:T(8,128)(2,1)S(1)}, bf16[2,192,384]{2,1,0:T(8,128)(2,1)S(1)}, u32[]{:S(2)}, u32[]{:S(2)}) collective-permute-start(bf16[2,192,384]{2,1,0:T(8,128)(2,1)S(1)} %dynamic-slice_bitcast_fusion.12), channel_id=1, source_target_pairs={{0,16},{8,24},{16,0},{24,8},{1,17},{9,25},{17,1},{25,9},{2,18},{10... | collective-permute-start | bytes 884744 | tf_op jit(solution)/shard_map/ppermute | solution.py:528
  414.1 10.0 %collective-permute-start.43 = (bf16[2,192,384]{2,1,0:T(8,128)(2,1)S(1)}, bf16[2,192,384]{2,1,0:T(8,128)(2,1)S(1)}, u32[]{:S(2)}, u32[]{:S(2)}) collective-permute-start(bf16[2,192,384]{2,1,0:T(8,128)(2,1)S(1)} %fusion.36), channel_id=1, source_target_pairs={{0,8},{8,0},{16,24},{24,16},{1,9},{9,1},{17,25},{25,17},{2,10},{10... | collective-permute-start | bytes 884744 | tf_op jit(solution)/shard_map/ppermute | solution.py:528
  420.3 14.2 %collective-permute-start.34 = (bf16[48,1536]{1,0:T(8,128)(2,1)S(1)}, bf16[48,1536]{1,0:T(8,128)(2,1)S(1)}, u32[]{:S(2)}, u32[]{:S(2)}) collective-permute-start(bf16[48,1536]{1,0:T(8,128)(2,1)S(1)} %get-tuple-element.99), channel_id=1, source_target_pairs={{0,4},{1,5},{2,6},{3,7},{4,0},{5,1},{6,2},{7,3},{8,12},{9,13},{10,... | collective-permute-start | bytes 442376 | tf_op jit(solution)/shard_map/ppermute | solution.py:528
  420.3 14.2 %collective-permute-start.33 = (bf16[48,1536]{1,0:T(8,128)(2,1)S(1)}, bf16[48,1536]{1,0:T(8,128)(2,1)S(1)}, u32[]{:S(2)}, u32[]{:S(2)}) collective-permute-start(bf16[48,1536]{1,0:T(8,128)(2,1)S(1)} %get-tuple-element.98), channel_id=1, source_target_pairs={{0,2},{1,3},{2,0},{3,1},{4,6},{5,7},{6,4},{7,5},{8,10},{9,11},{10,... | collective-permute-start | bytes 442376 | tf_op jit(solution)/shard_map/ppermute | solution.py:528
  424.5 15.6 %collective-permute-start.46 = (bf16[192,384]{1,0:T(8,128)(2,1)S(1)}, bf16[192,384]{1,0:T(8,128)(2,1)S(1)}, u32[]{:S(2)}, u32[]{:S(2)}) collective-permute-start(bf16[192,384]{1,0:T(8,128)(2,1)S(1)} %get-tuple-element.95), channel_id=1, source_target_pairs={{0,6},{1,7},{2,4},{3,5},{4,2},{5,3},{6,0},{7,1},{8,14},{9,15},{10,... | collective-permute-start | bytes 442376 | tf_op jit(solution)/shard_map/ppermute | solution.py:528
  425.4 16.1 %collective-permute-start.45 = (bf16[192,384]{1,0:T(8,128)(2,1)S(1)}, bf16[192,384]{1,0:T(8,128)(2,1)S(1)}, u32[]{:S(2)}, u32[]{:S(2)}) collective-permute-start(bf16[192,384]{1,0:T(8,128)(2,1)S(1)} %get-tuple-element.94), channel_id=1, source_target_pairs={{0,4},{1,5},{2,6},{3,7},{4,0},{5,1},{6,2},{7,3},{8,12},{9,13},{10,... | collective-permute-start | bytes 442376 | tf_op jit(solution)/shard_map/ppermute | solution.py:528
  428.2 13.4 %collective-permute-start.44 = (bf16[192,384]{1,0:T(8,128)(2,1)S(1)}, bf16[192,384]{1,0:T(8,128)(2,1)S(1)}, u32[]{:S(2)}, u32[]{:S(2)}) collective-permute-start(bf16[192,384]{1,0:T(8,128)(2,1)S(1)} %get-tuple-element.93), channel_id=1, source_target_pairs={{0,2},{1,3},{2,0},{3,1},{4,6},{5,7},{6,4},{7,5},{8,10},{9,11},{10,... | collective-permute-start | bytes 442376 | tf_op jit(solution)/shard_map/ppermute | solution.py:528
  436.0 11.4 %collective-permute-start.37 = (bf16[48,1536]{1,0:T(8,128)(2,1)S(1)}, bf16[48,1536]{1,0:T(8,128)(2,1)S(1)}, u32[]{:S(2)}, u32[]{:S(2)}) collective-permute-start(bf16[48,1536]{1,0:T(8,128)(2,1)S(1)} %fusion.48), channel_id=1, source_target_pairs={{0,16},{8,24},{16,0},{24,8},{1,17},{9,25},{17,1},{25,9},{2,18},{10... | collective-permute-start | bytes 442376 | tf_op jit(solution)/shard_map/ppermute | solution.py:528
  441.7 10.7 %collective-permute-start.49 = (bf16[192,384]{1,0:T(8,128)(2,1)S(1)}, bf16[192,384]{1,0:T(8,128)(2,1)S(1)}, u32[]{:S(2)}, u32[]{:S(2)}) collective-permute-start(bf16[192,384]{1,0:T(8,128)(2,1)S(1)} %fusion.45), channel_id=1, source_target_pairs={{0,24},{8,16},{16,8},{24,0},{1,25},{9,17},{17,9},{25,1},{2,26},{10... | collective-permute-start | bytes 442376 | tf_op jit(solution)/shard_map/ppermute | solution.py:528
  (54 other events, 482.6 us)

commit v3 on v2

--- a/solution.py
+++ b/solution.py
@@ -340,6 +340,7 @@
 ):
     step, last = pl.program_id(0), pl.num_programs(0) - 1
     seq, width = x_ref.shape
+    wide = w_up_ref.shape[1]
     gate_a, factor_m, shift_m, gate_m = (vec_ref[i : i + 1, :] for i in range(4))
     chunks = [slice(begin, begin + CHUNK) for begin in range(0, seq, CHUNK)]
 
@@ -373,8 +374,10 @@
         z_s[rows, :] += dot(act, w_down_ref[...])
         dh_s[rows, :] += dot_nt(du, w_up_ref[...])
     gb_up_ref[...] = bias_sum
-    g_up_ref[...] = dot(ht_s[...], du_s[...]).astype(bf16)
-    g_down_ref[...] = dot(dzt_s[...], act_s[...]).astype(bf16)
+    g_up_ref[0] = dot(ht_s[...], du_s[...]).astype(bf16)
+    down = dot(dzt_s[...], act_s[...]).astype(bf16)
+    g_down_ref[0, 0] = down[:, : wide // 2]
+    g_down_ref[0, 1] = down[:, wide // 2 :]
 
     @pl.when(step == last)
     def after():
@@ -417,11 +420,13 @@
         ],
         out_specs=[
             one((seq, width)), one((seq, width)), one((seq, width)), one((width, width)),
-            col(width), col(width), col(1), one((8, width)),
+            pl.BlockSpec((1, width, wide), lambda i: (i, 0, 0)),
+            pl.BlockSpec((1, 2, width, wide // 2), lambda i: (i, 0, 0, 0)), col(1), one((8, width)),
         ],
         out_shape=[
             shape((seq, width), bf16), shape((seq, width), f32), shape((seq, width), bf16),
-            shape((width, width), bf16), shape((width, ff), bf16), shape((width, ff), bf16),
+            shape((width, width), bf16), shape((ff // wide, width, wide), bf16),
+            shape((ff // wide, 2, width, wide // 2), bf16),
             shape((1, ff), f32), shape((8, width), f32),
         ],
         scratch_shapes=[
@@ -508,6 +513,538 @@
         ],
         compiler_params=pltpu.CompilerParams(collective_id=0, has_side_effects=True),
     )(vector.reshape(count, LANES))
+
+
+class Place:
+    def __init__(self):
+        self.blk, self.row = lax.axis_index("blk"), lax.axis_index("rows")
+        self.x, self.y = self.blk % 2, self.blk // 2
+        self.core, self.z = self.row % 2, self.row // 2
+
+    def along_blk(self, k):
+        return (partner(self.blk, k), self.row)
+
+    def along_rows(self, k):
+        return (self.blk, partner(self.row, k))
+
+
+class Sems:
+    def __init__(self, send, recv):
+        self.send, self.recv, self.used = send, recv, 0
+
+    def take(self, count):
+        self.used += count
+        return self.used - count
+
+    def copy(self, index, source, target, device):
+        return remote(source, target, self.send.at[index], self.recv.at[index], *device)
+
+
+def part(index, size, step):
+    return pl.ds(pl.multiple_of(index * size, step), size)
+
+
+class RowPiece:
+    SEMS = 11
+
+    @staticmethod
+    def scratch(nz, share, cols):
+        hs, hc = share // 2, cols // 2
+        shapes = [
+            (nz, share, cols), (nz // 2, share, hc), (nz // 2, hs, cols), (nz // 2, hs, hc), (nz // 2, hs, hc),
+            (nz, hs, hc), (nz, hs, hc), (4, hs, hc),
+        ]
+        return [pltpu.VMEM(shape, bf16) for shape in shapes]
+
+    def __init__(self, place, sems, whole, own, bufs, store):
+        self.p, self.sems, self.base = place, sems, sems.take(self.SEMS)
+        self.whole, self.own, self.store = whole, own, store
+        self.core, self.a1, self.b1, self.a2, self.b2, self.r3, self.zr, self.ag = bufs
+        self.nz, share, cols = self.core.shape
+        self.hs, self.hc, self.hz = share // 2, cols // 2, self.nz // 2
+
+    def copies(self, stage):
+        p, at = self.p, self.base
+        low, high = slice(0, self.hz), slice(self.hz, self.nz)
+        row = lambda y: part(y, self.hs, 16)
+        col = lambda x: part(x, self.hc, LANES)
+        if stage == 0:
+            return [self.sems.copy(at, self.whole.at[:, 1 - p.core], self.core, p.along_rows(1))]
+        if stage == 1:
+            return [
+                self.sems.copy(at + 1, self.core.at[low, :, col(1 - p.x)], self.a1, p.along_blk(1)),
+                self.sems.copy(at + 2, self.core.at[high, row(1 - p.y), :], self.b1, p.along_blk(2)),
+            ]
+        if stage == 2:
+            return [
+                self.sems.copy(at + 3, self.a1.at[:, row(1 - p.y), :], self.a2, p.along_blk(2)),
+                self.sems.copy(at + 4, self.b1.at[:, :, col(1 - p.x)], self.b2, p.along_blk(1)),
+            ]
+        if stage == 3:
+            return [
+                self.sems.copy(at + 4 + k, self.r3.at[partner(p.z, k)], self.zr.at[p.z], p.along_rows(2 * k))
+                for k in range(1, self.nz)
+            ]
+        return [
+            self.sems.copy(at + 7 + k, self.ag.at[p.blk], self.ag.at[p.blk], p.along_blk(k)) for k in range(1, 4)
+        ]
+
+    def wait(self, stage):
+        for copy in self.copies(stage):
+            copy.wait()
+
+    def run(self, stage):
+        p = self.p
+        if stage:
+            self.wait(stage - 1)
+        mine_row, mine_col = part(p.y, self.hs, 16), part(p.x, self.hc, LANES)
+        if stage == 1:
+            self.core[...] = self.core[...] + self.own()
+        if stage == 2:
+            self.a1[...] = self.a1[...] + self.core[: self.hz, :, mine_col]
+            self.b1[...] = self.b1[...] + self.core[self.hz :, mine_row, :]
+        if stage == 3:
+            self.r3[: self.hz] = self.a1[:, mine_row, :] + self.a2[...]
+            self.r3[self.hz :] = self.b1[:, :, mine_col] + self.b2[...]
+        if stage == 4:
+            total = self.r3[p.z].astype(f32)
+            for k in range(1, self.nz):
+                total = total + self.zr[partner(p.z, k)].astype(f32)
+            self.ag[p.blk] = total.astype(bf16)
+        if stage == 5:
+            for q in range(4):
+                rows = slice(q // 2 * self.hs, (q // 2 + 1) * self.hs)
+                self.store(rows, q % 2 * self.hc, self.ag[q].astype(f32))
+            return
+        for copy in self.copies(stage):
+            copy.start()
+
+
+class ColPiece:
+    SEMS = 12
+
+    @staticmethod
+    def scratch(nz, depth, cols):
+        shapes = [
+            (2, 2, 2, depth, cols), (2, depth, cols), (2, depth, cols), (depth, cols), (depth, cols),
+            (2, depth, cols), (nz, 2, depth, cols),
+        ]
+        return [pltpu.VMEM(shape, bf16) for shape in shapes]
+
+    def __init__(self, place, sems, whole, own, bufs, gathered, store, owner):
+        self.p, self.sems, self.base = place, sems, sems.take(self.SEMS)
+        self.whole, self.own, self.store, self.owner = whole, own, store, owner
+        self.core, self.a1, self.b1, self.a2, self.b2, self.r3, self.zr = bufs
+        self.ag = gathered
+        self.nz = self.zr.shape[0]
+
+    def copies(self, stage):
+        p, at = self.p, self.base
+        if stage == 0:
+            return [self.sems.copy(at, self.whole.at[1 - p.core], self.core, p.along_rows(1))]
+        if stage == 1:
+            return [
+                self.sems.copy(at + 1, self.core.at[:, 1 - p.x, 0], self.a1, p.along_blk(1)),
+                self.sems.copy(at + 2, self.core.at[1 - p.y, :, 1], self.b1, p.along_blk(2)),
+            ]
+        if stage == 2:
+            return [
+                self.sems.copy(at + 3, self.a1.at[1 - p.y], self.a2, p.along_blk(2)),
+                self.sems.copy(at + 4, self.b1.at[1 - p.x], self.b2, p.along_blk(1)),
+            ]
+        return [
+            self.sems.copy(at + 8 + k, self.ag.at[p.blk], self.ag.at[p.blk], p.along_blk(k)) for k in range(1, 4)
+        ]
+
+    def over_z(self, k):
+        p = self.p
+        device = (p.blk, 2 * self.owner + p.core)
+        return self.sems.copy(self.base + 5 + k, self.r3, self.zr.at[p.z], device)
+
+    def run(self, stage):
+        p, is_owner = self.p, self.p.z == self.owner
+        if stage in (1, 2, 3):
+            for copy in self.copies(stage - 1):
+                copy.wait()
+        if stage == 1:
+            self.core[...] = self.core[...] + self.own()
+        if stage == 2:
+            self.a1[...] = self.a1[...] + self.core[:, p.x, 0]
+            self.b1[...] = self.b1[...] + self.core[p.y, :, 1]
+        if stage == 3:
+            self.r3[0] = self.a1[p.y] + self.a2[...]
+            self.r3[1] = self.b1[p.x] + self.b2[...]
+            for k in range(1, self.nz):
+                @pl.when(p.z == self.owner ^ k)
+                def sent():
+                    self.over_z(k).start()
+            return
+        if stage == 4:
+            for k in range(1, self.nz):
+                @pl.when(p.z == self.owner ^ k)
+                def left():
+                    self.over_z(k).wait_send()
+
+            @pl.when(is_owner)
+            def summed():
+                total = self.r3[...].astype(f32)
+                for k in range(1, self.nz):
+                    self.over_z(k).wait_recv()
+                    total = total + self.zr[self.owner ^ k].astype(f32)
+                self.ag[p.blk] = total.astype(bf16)
+                for copy in self.copies(4):
+                    copy.start()
+            return
+        if stage == 5:
+            @pl.when(is_owner)
+            def whole():
+                for copy in self.copies(4):
+                    copy.wait()
+                depth = self.r3.shape[1]
+                for q in range(8):
+                    self.store(slice(q * depth, (q + 1) * depth), self.ag[q // 2, q % 2].astype(f32))
+            return
+        for copy in self.copies(stage):
+            copy.start()
+
+
+class Gather:
+    def __init__(self, place, sems, source, target):
+        self.p, self.sems, self.source, self.target = place, sems, source, target
+        self.nblk, self.nrows = target.shape[:2]
+        self.base = sems.take(self.nblk + self.nrows)
+
+    def copies(self, stage):
+        p = self.p
+        if stage == 0:
+            return [
+                self.sems.copy(self.base + k, self.source, self.target.at[p.blk, p.row], p.along_rows(k))
+                for k in range(1, self.nrows)
+            ]
+        return [
+            self.sems.copy(self.base + self.nrows + k, self.target.at[p.blk], self.target.at[p.blk], p.along_blk(k))
+            for k in range(1, self.nblk)
+        ]
+
+    def run(self, stage):
+        if stage:
+            for copy in self.copies(stage - 1):
+                copy.wait()
+        else:
+            self.target[self.p.blk, self.p.row] = self.source[...]
+        if stage < 2:
+            for copy in self.copies(stage):
+                copy.start()
+
+
+class Return:
+    def __init__(self, place, sems, source, target, local):
+        self.p, self.sems, self.source, self.target, self.local = place, sems, source, target, local
+        self.rows, self.nblk = target.shape[0], source.shape[0]
+        self.base = sems.take(self.nblk)
+        self.mine = jnp.minimum(place.blk, self.rows - 1)
+
+    def copy(self, k):
+        device = self.p.along_blk(k)
+        return self.sems.copy(self.base + k, self.source.at[device[0]], self.target.at[self.mine], device)
+
+    def own(self):
+        return pltpu.make_async_copy(self.source.at[self.p.blk], self.target.at[self.mine], self.local)
+
+    def start(self, ks):
+        @pl.when(self.p.blk < self.rows)
+        def sent():
+            for k in ks:
+                (self.copy(k) if k else self.own()).start()
+
+    def finish(self):
+        @pl.when(self.p.blk < self.rows)
+        def left():
+            self.own().wait()
+            for k in range(1, self.nblk):
+                self.copy(k).wait_send()
+
+        for k in range(1, self.nblk):
+            @pl.when(partner(self.p.blk, k) < self.rows)
+            def arrived():
+                self.copy(k).wait_recv()
+
+
+def greet(place, nblk, nrows):
+    barrier = pltpu.get_barrier_semaphore()
+    for k in range(1, nblk):
+        pl.semaphore_signal(barrier, inc=1, device_id=place.along_blk(k), device_id_type=MESH)
+    for k in range(1, nrows):
+        pl.semaphore_signal(barrier, inc=1, device_id=place.along_rows(k), device_id_type=MESH)
+    pl.semaphore_wait(barrier, nblk + nrows - 2)
+
+
+def behind_kernel(
+    n_up, owners,
+    q_ref, k_ref, v_ref, d_ref, att_ref, lse_ref, fq_ref, fk_ref, cos_ref, sin_ref, wq_ref, wk_ref, wv_ref,
+    ht_ref, x_ref, dx_ref, vec_ref, early_ref, up_ref, down_ref, out_ref, result_ref,
+    tok_out, grad_out, share_qkv, share_out, share_up, share_down, early_out, late_out,
+    qa_ref, da_ref, dq_acc, dqkv_s, dh_s, gq_s, gt_s, early_s, late_s, late_b, early_g, late_g, down_ag,
+    own_up, own_down, own_out, send, recv, local, *bufs
+):
+    step, last = pl.program_id(0), pl.num_programs(0) - 1
+    place = Place()
+    sems = Sems(send, recv)
+    nblk, stretch, width = x_ref.shape
+    nrows = early_g.shape[1]
+    seq = nblk * stretch
+    n_down = len(owners)
+    bufs = list(bufs)
+
+    def taken(count):
+        out = bufs[:count]
+        del bufs[:count]
+        return out
+
+    def store_at(ref, begin):
+        def store(rows, col, value):
+            ref[rows, begin + col : begin + col + value.shape[1]] = value
+        return store
+
+    def store_qkv(j):
+        def store(rows, col, value):
+            for group in range(value.shape[1] // LANES):
+                lane = col + group * LANES
+                at = lane // (2 * LANES) * width + j * 2 * LANES + lane % (2 * LANES)
+                share_qkv[rows, at : at + LANES] = value[:, group * LANES : (group + 1) * LANES]
+        return store
+
+    def store_down(rows, value):
+        share_down[rows, :] = value
+
+    pieces = []
+    loads = []
+    for i in range(n_up):
+        pieces.append(RowPiece(place, sems, up_ref.at[i], lambda i=i: own_up[i], taken(8), store_at(share_up, i * width)))
+        loads.append((up_ref.at[i, :, place.core], own_up.at[i]))
+    for i in range(n_down):
+        pieces.append(
+            ColPiece(place, sems, down_ref.at[i], lambda i=i: own_down[i], taken(7), down_ag, store_down, owners[i])
+        )
+        loads.append((down_ref.at[i, place.core], own_down.at[i]))
+    pieces.append(RowPiece(place, sems, out_ref, lambda: own_out[...], taken(8), store_at(share_out, 0)))
+    loads.append((out_ref.at[:, place.core], own_out))
+    loads = [pltpu.make_async_copy(a, b, local.at[2 + i]) for i, (a, b) in enumerate(loads)]
+    late_pieces = [
+        RowPiece(place, sems, gq_s.at[j], lambda j=j: gq_s[j, :, place.core], taken(8), store_qkv(j)) for j in range(3)
+    ]
+    results = Return(place, sems, result_ref, tok_out, local.at[0])
+    grads = Return(place, sems, gt_s, grad_out, local.at[1])
+    early = Gather(place, sems, early_s, early_g)
+    late = Gather(place, sems, late_b, late_g)
+
+    plan = {}
+
+    def at(slot, *actions):
+        plan.setdefault(slot, []).extend(actions)
+
+    def stage(piece, number):
+        return lambda: piece.run(number)
+
+    def loaded():
+        for load in loads:
+            load.wait()
+
+    half_way = len(pieces)
+    at(0, lambda: greet(place, nblk, nrows))
+    at(0, *[load.start for load in loads])
+    at(0, *[stage(piece, 0) for piece in pieces])
+    at(0, lambda: results.start(range(nblk)))
+    at(1, loaded)
+    for e, piece in enumerate(pieces):
+        begin = 1 + e * 5 // half_way
+        for number in range(1, 6):
+            at(min(begin + 2 * number - 2, 20), stage(piece, number))
+    at(2, lambda: early_start(), lambda: early.run(0))
+    at(4, lambda: early.run(1))
+    at(8, lambda: early.run(2))
+    for number in range(1, 6):
+        at(3 + 2 * number, stage(late_pieces[0], number))
+    for number in (1, 2):
+        at(7 + 2 * number, stage(late_pieces[1], number))
+
+    def early_start():
+        early_s[...] = early_ref[...]
+
+    def slot(number):
+        if number in plan:
+            @pl.when(step == number // 2)
+            def actions():
+                for action in plan[number]:
+                    action()
+
+    half = LANES // 4
+    scale = 1.0 / math.sqrt(2 * half)
+    lane = lane_of((1, LANES))
+    first = lane < 2 * half
+    where = lane % (2 * half)
+    one = jnp.ones((), bf16)
+    outs = []
+    for head in range(2):
+        for i in range(6):
+            slot(2 * i + head)
+        own = first if head == 0 else jnp.logical_not(first)
+        lse = in_three(-lse_ref[...])
+        feature = fq_ref[...]
+        for i in range(3):
+            feature = jnp.where(where == NDOC + i, lse[i], feature)
+        qa_ref[...] = jnp.where(own, q_ref[...], feature)
+        datt = d_ref[...]
+        both = jnp.where(own, datt.astype(f32) * att_ref[...], 0.0)
+        delta = in_three(jnp.broadcast_to(-jnp.sum(both, axis=-1, keepdims=True), both.shape))
+        feature = jnp.zeros_like(datt)
+        for i in range(3):
+            feature = jnp.where(where == NDOC + i, delta[i], feature)
+        da_ref[...] = jnp.where(own, datt, feature)
+        blocks = []
+        for begin in range(0, seq, CHUNK):
+            rows = slice(begin, begin + CHUNK)
+            keys = jnp.where(own, k_ref[rows, :], fk_ref[rows, :])
+            values = jnp.where(own, v_ref[rows, :], one)
+            prob = jnp.exp(dot_nt(keys, qa_ref[...]))
+            grad_v = dot(prob.astype(bf16), d_ref[...])
+            grad_s = (prob * dot_nt(values, da_ref[...])).astype(bf16)
+            grad_k = dot(grad_s, q_ref[...])
+            added = dot_tn(grad_s, k_ref[rows, :])
+            if begin == 0:
+                dq_acc[head] = added
+            else:
+                dq_acc[head] += added
+            blocks.append((grad_k, grad_v))
+        outs.append(blocks)
+    side = step % 2 * LANES
+    for number, begin in enumerate(range(0, seq, CHUNK)):
+        rows = slice(begin, begin + CHUNK)
+        cosine, sine = cos_ref[rows, :], sin_ref[rows, :]
+        grad_k = jnp.where(first, outs[0][number][0], outs[1][number][0])
+        grad_k = (grad_k * cosine - swap_halves(grad_k, half) * sine).astype(bf16)
+        grad_v = jnp.where(first, outs[0][number][1], outs[1][number][1]).astype(bf16)
+        grad_q = jnp.where(first, dq_acc[0, rows, :], dq_acc[1, rows, :]) * scale
+        grad_q = (grad_q * cosine - swap_halves(grad_q, half) * sine).astype(bf16)
+        for i, grad in enumerate((grad_q, grad_k, grad_v)):
+            dqkv_s[rows, pl.ds(pl.multiple_of(2 * i * LANES + side, LANES), LANES)] = grad
+
+    @pl.when(step % 2 == 1)
+    def projections():
+        group = step // 2
+        grad_w = dot(ht_ref[...], dqkv_s[...]).astype(bf16)
+        gq_s[group] = grad_w.reshape(gq_s.shape[1:])
+        for rows in (slice(begin, begin + CHUNK) for begin in range(0, seq, CHUNK)):
+            added = dot_nt(dqkv_s[rows, : 2 * LANES], wq_ref[...])
+            added = added + dot_nt(dqkv_s[rows, 2 * LANES : 4 * LANES], wk_ref[...])
+            added = added + dot_nt(dqkv_s[rows, 4 * LANES :], wv_ref[...])
+
+            @pl.when(group == 0)
+            def fresh():
+                dh_s[rows, :] = added
+
+            @pl.when(group > 0)
+            def more():
+                dh_s[rows, :] += added
+
+        for j, piece in enumerate(late_pieces):
+            @pl.when(group == j)
+            def sent():
+                piece.run(0)
+
+    @pl.when(step == last)
+    def tail():
+        factor, gain, scaled = (vec_ref[i : i + 1, :] for i in range(3))
+        total = [jnp.zeros((1, width), f32) for unused in range(2)]
+
+        def chunk(k):
+            slot = partner(place.blk, k)
+            rows = pl.ds(pl.multiple_of(slot * stretch, stretch), stretch)
+            normed, inverse = norm_rows(x_ref[slot].astype(f32))
+            dh = dh_s[rows, :]
+            gt_s[slot] = (dx_ref[rows, :] + norm_back(dh * factor, normed, inverse)).astype(bf16)
+            grads.start([k])
+            total[0] = total[0] + jnp.sum(dh, axis=0, keepdims=True)
+            total[1] = total[1] + jnp.sum(dh * normed, axis=0, keepdims=True)
+
+        before, middle, after = late_pieces
+        chunk(1)
+        chunk(2)
+        middle.run(3)
+        after.run(1)
+        chunk(3)
+        chunk(0)
+        late_s[...] = jnp.zeros_like(late_s)
+        for i, row in enumerate((total[0], total[1] * gain, total[1] * scaled)):
+            for group in range(width // LANES):
+                at_row = i * (width // LANES) + group
+                late_s[at_row : at_row + 1, :] = row[:, group * LANES : (group + 1) * LANES]
+        late_b[...] = late_s[...].astype(bf16)
+        late.run(0)
+        after.run(2)
+        late.run(1)
+        middle.run(4)
+        after.run(3)
+        for number in range(12, 21):
+            for action in plan.get(number, []):
+                action()
+        late.run(2)
+        middle.run(5)
+        after.run(4)
+        early_out[...] = early_g[...]
+        late_out[...] = late_g[...]
+        after.run(5)
+        results.finish()
+        grads.finish()
+
+
+def behind(q, k, v, grads, att, lse, fq, fk, cosine, sine, w_qkv, hidden_t, x, dx, vec, early, g_up, g_down, g_out,
+           result, rows_dev, nrows, owners):
+    seq, width = q.shape
+    nblk, stretch, unused = x.shape
+    n_up, nz, unused, share, cols = g_up.shape
+    n_down, depth, dcols = g_down.shape[0], g_down.shape[-2], g_down.shape[-1]
+    pair = pl.BlockSpec((seq, LANES), lambda i: (0, i))
+    once = pl.Buffered(buffer_count=1)
+    fixed = lambda a: pl.BlockSpec(a.shape, lambda i: (0,) * len(a.shape), pipeline_mode=once)
+    away = pl.BlockSpec(memory_space=pl.ANY)
+    per = width // (2 * LANES)
+    weight = lambda n: pl.BlockSpec((width, 2 * LANES), lambda i: (0, n * per + i // 2))
+    shape = jax.ShapeDtypeStruct
+    back = (rows_dev, stretch, width)
+    outs = [
+        shape((share, 3 * width), f32), shape((share, cols), f32), shape((share, n_up * cols), f32),
+        shape((8 * depth, dcols), f32), shape((nblk, nrows) + early.shape, bf16), shape((nblk, nrows, 32, LANES), bf16),
+    ]
+    row_bufs = RowPiece.scratch(nz, share, cols)
+    col_bufs = ColPiece.scratch(nz, depth, dcols)
+    sems = (n_up + 4) * RowPiece.SEMS + n_down * ColPiece.SEMS + 2 * nblk + 2 * (nblk + nrows)
+    scratch = [
+        pltpu.VMEM((seq, LANES), bf16), pltpu.VMEM((seq, LANES), bf16), pltpu.VMEM((2, seq, LANES), f32),
+        pltpu.VMEM((seq, 6 * LANES), bf16), pltpu.VMEM((seq, width), f32),
+        pltpu.VMEM((3, nz, 2, share, cols), bf16), pltpu.VMEM((nblk, stretch, width), bf16),
+        pltpu.VMEM(early.shape, bf16), pltpu.VMEM((32, LANES), f32), pltpu.VMEM((32, LANES), bf16),
+        pltpu.VMEM((nblk, nrows) + early.shape, bf16), pltpu.VMEM((nblk, nrows, 32, LANES), bf16),
+        pltpu.VMEM((4, 2, depth, dcols), bf16),
+        pltpu.VMEM((n_up, nz, share, cols), bf16), pltpu.VMEM((n_down, 2, 2, 2, depth, dcols), bf16),
+        pltpu.VMEM((nz, share, cols), bf16),
+        pltpu.SemaphoreType.DMA((sems,)), pltpu.SemaphoreType.DMA((sems,)),
+        pltpu.SemaphoreType.DMA((3 + n_up + n_down,)),
+    ] + row_bufs * n_up + col_bufs * n_down + row_bufs * 4
+    return pl.pallas_call(
+        functools.partial(behind_kernel, n_up, owners),
+        grid=(width // LANES,),
+        in_specs=[pair] * 6 + [fixed(fq), fixed(fk), fixed(cosine), fixed(sine), weight(0), weight(1), weight(2)]
+        + [fixed(hidden_t), fixed(x), fixed(dx), fixed(vec), fixed(early)] + [away] * 4,
+        out_specs=[away, away] + [pl.BlockSpec(o.shape, lambda i, n=len(o.shape): (0,) * n) for o in outs],
+        out_shape=[shape(back, bf16), shape(back, bf16)] + outs,
+        scratch_shapes=scratch,
+        compiler_params=pltpu.CompilerParams(collective_id=2, has_side_effects=True, vmem_limit_bytes=62 * MIB),
+        cost_estimate=pl.CostEstimate(
+            flops=52 * seq * seq * width, bytes_accessed=40 * seq * width, transcendentals=H * seq * seq
+        ),
+    )(q, k, v, grads, att, lse, fq, fk, cosine, sine, w_qkv, w_qkv, w_qkv, hidden_t, x, dx, vec, early, g_up, g_down,
+      g_out, result)
 
 
 def rows_out(whole, rows, me, nblk):
@@ -616,41 +1153,57 @@
         attended_b, x_row, g_row, vec, w_out, w_up, b_up.astype(f32)[None, :], w_down,
         b_down.astype(f32)[None, :]
     )
-    out = rows_out(result.reshape(nblk, stretch, width), rows_dev, blk, nblk)
+    result = result.reshape(nblk, stretch, width)
     dgate_m, dshift_m, along_m, dgate_a, grad_b_down = (sums[i] for i in range(5))
-    grad_b_up = gb_up[0]
-    share_w_down = reduce_weight(grad_w_down.T, blk, row, nblk, nrows)
-    share_w_up = reduce_weight(grad_w_up, blk, row, nblk, nrows)
-    share_w_out = reduce_weight(grad_w_out, blk, row, nblk, nrows)
-
-    dq, dk, dv = attend_back(q, k, v, grad_att, attended, lse, fq, fk, cosine, sine)
-    grad_qkv = jnp.concatenate([dq, dk, dv], axis=-1)
-    grad_w_qkv = dot(hidden_t, grad_qkv).astype(bf16)
-    share_w_qkv = reduce_weight(grad_w_qkv, blk, row, nblk, nrows)
-    grad_ha = dot_nt(grad_qkv, w_qkv)
-    normed_a, inverse_a = norm_rows(x_row.astype(f32))
-    dshift_a = jnp.sum(grad_ha, axis=0)
-    along_a = jnp.sum(grad_ha * normed_a, axis=0)
-    grad_in = (grad_mid + norm_back(grad_ha * factor_a, normed_a, inverse_a)).astype(bf16)
-    grad_tokens = rows_out(grad_in.reshape(nblk, stretch, width), rows_dev, blk, nblk)
-
-    packed = jnp.concatenate(
+    ff = b_up.shape[0]
+    early = jnp.concatenate(
         [
-            dshift_a, along_a * gain_a, dgate_a, dshift_m, along_m * gain_m, dgate_m,
-            along_a * (1.0 + scale_a[0]), along_m * (1.0 + scale_m[0]), grad_b_up, grad_b_down,
+            dgate_a, dshift_m, along_m * gain_m, dgate_m, along_m * (1.0 + scale_m[0]), grad_b_down, gb_up[0],
             jnp.broadcast_to(step.astype(f32), (LANES,)),
         ]
     )
-    gathered = gather_all(packed, nblk, nrows).reshape(nblk, nrows, -1)
-    gathered = gathered[:rows_dev].reshape(rows_dev * nrows, -1)
-    six = 6 * width
-    grad_mod = gathered[:, :six]
-    smalls = jnp.sum(gathered, axis=0)
-    grad_gain_a, grad_gain_m = smalls[six : six + width], smalls[six + width : six + 2 * width]
-    rest = six + 2 * width
-    ff = b_up.shape[0]
-    total_b_up, total_b_down = smalls[rest : rest + ff], smalls[rest + ff : rest + ff + width]
-    steps = gathered[:, -1].astype(jnp.int32)
+    count = early.shape[0]
+
+    if (nblk, nrows) == (4, 8):
+        rows_early = -(-count // (16 * LANES)) * 16
+        early = jnp.pad(early, (0, rows_early * LANES - count)).reshape(rows_early, LANES).astype(bf16)
+        vec = jnp.concatenate([factor_a, gain_a[None, :], 1.0 + scale_a], axis=0)
+        nf, nz, share = grad_w_up.shape[0], nrows // 2, width // nrows
+        out, grad_tokens, share_w_qkv, share_w_out, share_w_up, share_w_down, early, late = behind(
+            q, k, v, grad_att, attended, lse, fq, fk, cosine, sine, w_qkv, hidden_t, x_blocks, grad_mid, vec, early,
+            grad_w_up.reshape(nf, nz, 2, share, -1), grad_w_down.reshape(nf, 2, 2, 2, 2, width // 8, -1),
+            grad_w_out.reshape(nz, 2, share, width), result, rows_dev, nrows, tuple(range(nf)),
+        )
+        share_w_down = share_w_down.T
+        early = early.reshape(nblk, nrows, -1)[:rows_dev].reshape(rows_dev * nrows, -1).astype(f32)
+        late = late.reshape(nblk, nrows, -1)[:rows_dev].reshape(rows_dev * nrows, -1).astype(f32)
+        dshift_a, dscale_a, part_gain_a = (late[:, i * width : (i + 1) * width] for i in range(3))
+    else:
+        out = rows_out(result, rows_dev, blk, nblk)
+        share_w_down = reduce_weight(grad_w_down.transpose(2, 0, 1, 3).reshape(width, ff).T, blk, row, nblk, nrows)
+        share_w_up = reduce_weight(grad_w_up.transpose(1, 0, 2).reshape(width, ff), blk, row, nblk, nrows)
+        share_w_out = reduce_weight(grad_w_out, blk, row, nblk, nrows)
+        dq, dk, dv = attend_back(q, k, v, grad_att, attended, lse, fq, fk, cosine, sine)
+        grad_qkv = jnp.concatenate([dq, dk, dv], axis=-1)
+        grad_w_qkv = dot(hidden_t, grad_qkv).astype(bf16)
+        share_w_qkv = reduce_weight(grad_w_qkv, blk, row, nblk, nrows)
+        grad_ha = dot_nt(grad_qkv, w_qkv)
+        normed_a, inverse_a = norm_rows(x_row.astype(f32))
+        along_a = jnp.sum(grad_ha * normed_a, axis=0)
+        grad_in = (grad_mid + norm_back(grad_ha * factor_a, normed_a, inverse_a)).astype(bf16)
+        grad_tokens = rows_out(grad_in.reshape(nblk, stretch, width), rows_dev, blk, nblk)
+        packed = jnp.concatenate(
+            [early, jnp.sum(grad_ha, axis=0), along_a * gain_a, along_a * (1.0 + scale_a[0])]
+        )
+        gathered = gather_all(packed, nblk, nrows).reshape(nblk, nrows, -1)
+        early = gathered[:rows_dev].reshape(rows_dev * nrows, -1)
+        dshift_a, dscale_a, part_gain_a = (early[:, count + i * width : count + (i + 1) * width] for i in range(3))
+
+    grad_mod = jnp.concatenate([dshift_a, dscale_a, early[:, : 4 * width]], axis=-1)
+    smalls = jnp.sum(early, axis=0)
+    grad_gain_m, total_b_down = smalls[4 * width : 5 * width], smalls[5 * width : 6 * width]
+    total_b_up = smalls[6 * width : 6 * width + ff]
+    steps = early[:, 6 * width + ff].astype(jnp.int32)
     onehot = (steps[:, None] == jnp.arange(table.shape[0], dtype=jnp.int32)[None, :]).astype(f32)
     conds = jnp.dot(onehot, table, precision=highest)
     share = conds.shape[1] // nrows
@@ -667,8 +1220,8 @@
         grad_tokens,
         grad_table,
         grad_w_ada,
-        smalls[:six],
-        grad_gain_a,
+        jnp.sum(grad_mod, axis=0),
+        jnp.sum(part_gain_a, axis=0),
         share_w_qkv,
         share_w_out,
         grad_gain_m,

time: 461 us -> 299 us (0.65)
  Pallas kernels: 173 us -> 256 us
  local copies, waits for them, and re-layouts: 88.8 us -> 16.9 us
  starting transfers between devices: 64.8 us -> 0 us
  waiting for transfers between devices: 58.4 us -> 0 us
  other arithmetic: 49.2 us -> 13.8 us
  matrix products: 17.1 us -> 4.63 us
    pallas_call x2 -> x1, Pallas kernels: 72 us -> 155 us  [behind(): pl.pallas_call(functools.partial(behind_kernel, n_up, owners), grid=(widt...]
    ppermute x50 -> x0, starting transfers between devices: 64.8 us -> none  [the longest x44 47.3 us: xor_move(): return lax.ppermute(array, axis, [(s, s ^ k) for s in range(size)])]
    ppermute x50 -> x0, waiting for transfers between devices: 58.4 us -> none  [the longest x44 58.4 us: xor_move(): return lax.ppermute(array, axis, [(s, s ^ k) for s in range(size)])]
    unnamed x95 -> x40, local copies, waits for them, and re-layouts: 33.7 us -> 10 us
    convert_element_type x31 -> x1, other arithmetic: 22.1 us -> 0.01 us  [per_device(): steps = early[:, 6 * width + ff].astype(jnp.int32)]
    dot_general x2 -> x0, matrix products: 12.5 us -> none  [the longest x1 6.63 us: dot(): return jnp.dot(a, b, preferred_element_type=f32)]
    dynamic_slice x2 -> x1, local copies, waits for them, and re-layouts: 13.6 us -> 1.33 us  [pick(): return lax.dynamic_index_in_dim(array, index, axis, keepdims=False)]
    gather x6 -> x0, local copies, waits for them, and re-layouts: 11.9 us -> none  [the longest x2 6.16 us: rows_out(): return jnp.take(stacked, jnp.arange(rows) ^ me, axis=0)]
  transfers between devices with their start and end apart: 50 -> 0, of which waited for: 17 -> 0; matrix products, arithmetic and copies ran while one was open for 26% -> 0% of each run, Pallas kernels for 7% -> 0%
where the time goes in v3:
time: 299 us; the launch traced here: 295 us
  Pallas kernels  256 us (86%)
  local copies, waits for them, and re-layouts  16.9 us (6%)
  other arithmetic  13.8 us (5%)
  matrix products  4.63 us (2%)
  between operations  3.72 us (1%)
    pallas_call x1, Pallas kernels, behind(): pl.pallas_call(functools.partial(behind_kernel, n_up, owners), grid=(widt...  155 us
    pallas_call x1, Pallas kernels, ahead(): pl.pallas_call(ahead_kernel, grid=(width // LANES,), in_specs=[away, away...  51.8 us
    pallas_call x1, Pallas kernels, feed(): pl.pallas_call(feed_kernel, grid=(ff // wide,), in_specs=[fixed(ab), fixe...  48.8 us
    unnamed x40, local copies, waits for them, and re-layouts  10 us

profile of v3, /device:TPU:0, one launch (start us, length us, event | category | flops | bytes accessed | tf_op | source)
XLA Modules:
  0.0 295.1 jit_solution(6208916378388460293)
XLA Ops:
  0.7 1.3 dynamic_slice.15
  4.6 0.7 fusion.18
  5.5 1.3 reshape.130.b_down_ref
  6.8 0.7 reshape.128
  7.5 0.7 convert_element_type.63
  8.3 1.3 broadcast_in_dim.70
  9.6 1.3 convolution_reduce_fusion
  11.5 0.6 pad_maximum_fusion.6.vec_ref
  12.2 0.6 pad_maximum_fusion.5.vec_ref
  12.8 1.0 select_convert_fusion
  13.8 1.9 fusion.4
  15.7 1.8 pad_maximum_fusion
  17.5 51.8 %shard_map.246 = (bf16[4,256,768]{2,1,0:T(8,128)(2,1)}, bf16[4,256,768]{2,1,0:T(8,128)(2,1)}, bf16[1024,768]{1,0:T(8,128)(2,1)}, bf16[768,1024]{1,0:T(8,128)(2,1...) custom-call(bf16[3,256,768]{2,1,0:T(8,128)(2,1)} %tok_ref.1, ...), custom_call_target="tpu_custom_call" | custom-call | flops 17716740096 | bytes 18874368 | tf_op jit(solution)/shard_map/pallas_call | solution.py:234
  69.3 48.8 %shard_map.247 = (bf16[1024,768]{1,0:T(8,128)(2,1)}, f32[1024,768]{1,0:T(8,128)}, bf16[1024,768]{1,0:T(8,128)(2,1)}, bf16[768,768]{1,0:T(8,128)(2,1)}, bf16[4,76...) custom-call(bf16[1024,768]{1,0:T(8,128)(2,1)} %get-tuple-element.41.ab_ref, ...), custom_call_target="tpu_custom_call" | custom-call | flops 28991029248 | bytes 23592960 | tf_op jit(solution)/shard_map/pallas_call | solution.py:414
  118.1 0.8 slice_reduce_fusion.5
  118.9 0.7 convert.35
  121.0 0.7 convert_reduce_fusion.2
  122.2 0.6 pad_bitcast_fusion.early_ref
  122.8 155.5 %shard_map.248 = (bf16[3,256,768]{2,1,0:T(8,128)(2,1)}, bf16[3,256,768]{2,1,0:T(8,128)(2,1)}, f32[96,2304]{1,0:T(8,128)}, f32[96,768]{1,0:T(8,128)}, f32[96,3072...) custom-call(bf16[1024,768]{1,0:T(8,128)(2,1)} %get-tuple-element.38.q_ref, ...), custom_call_target="tpu_custom_call" | custom-call | flops 41875931136 | bytes 31457280 | tf_op jit(solution)/shard_map/pallas_call | solution.py:1034
  278.3 1.1 convert_reduce_fusion
  280.6 1.1 convert_bitcast_fusion
  283.5 1.0 fusion
  284.5 0.9 fusion.11
  285.5 0.7 fusion.2
  286.1 1.2 fusion.3
  287.4 1.4 copy.34
  288.8 1.0 copy.56
  289.8 0.7 copy-done.2
  290.5 1.0 copy.57
  292.1 0.9 copy.58
  293.2 0.7 copy.59
  293.9 1.0 copy.60
  (56 shorter events, 6.6 us)
Async XLA Ops:
  0.6 8.9 %copy-start = (bf16[128,4608]{1,0:T(8,128)(2,1)S(1)}, bf16[128,4608]{1,0:T(8,128)(2,1)}, u32[]{:S(2)}) copy-start(bf16[128,4608]{1,0:T(8,128)(2,1)} %param.19) | copy-start | bytes 3538948
  0.7 10.2 %copy-start.10 = (bf16[768]{0:T(1024)(128)(2,1)S(1)}, bf16[768]{0:T(1024)(128)(2,1)}, u32[]{:S(2)}) copy-start(bf16[768]{0:T(1024)(128)(2,1)} %param.21) | copy-start | bytes 4612
  0.7 10.2 %copy-start.8 = (bf16[4608]{0:T(1024)(128)(2,1)S(1)}, bf16[4608]{0:T(1024)(128)(2,1)}, u32[]{:S(2)}) copy-start(bf16[4608]{0:T(1024)(128)(2,1)} %param.20) | copy-start | bytes 27652
  69.3 50.4 %copy-start.9 = (bf16[768]{0:T(1024)(128)(2,1)S(1)}, bf16[768]{0:T(1024)(128)(2,1)}, u32[]{:S(2)}) copy-start(bf16[768]{0:T(1024)(128)(2,1)} %param.24) | copy-start | bytes 4612
  281.6 0.7 copy-start.11
  281.7 1.0 copy-start.7
  283.5 3.9 %copy-start.4 = (f32[768,384]{1,0:T(8,128)S(1)}, f32[768,384]{1,0:T(8,128)}, u32[]{:S(2)}) copy-start(f32[768,384]{1,0:T(8,128)} %get-tuple-element.62) | copy-start | bytes 3538948
  287.4 1.4 copy-start.3
  288.8 1.7 copy-start.2
  290.5 1.6 copy-start.5
  292.1 1.1 copy-start.6
  292.1 1.8 copy-start.1

commit v4 on v2

v4 whole, which is shorter than its diff:
```python
import functools
import math
import types

import jax
import jax.numpy as jnp
import numpy as np
from jax import lax
from jax.experimental import pallas as pl
from jax.experimental.pallas import tpu as pltpu
from jax.sharding import PartitionSpec as P

H = 12
NDOC = 8
LANES = 128
CHUNK = 256
MIB = 1 << 20

epsilon = 1e-05
highest = lax.Precision.HIGHEST
bf16 = jnp.bfloat16
f32 = jnp.float32
MESH = pl.DeviceIdType.MESH


def dot(a, b):
    return jnp.dot(a, b, preferred_element_type=f32)


def dot_nt(a, b):
    return lax.dot_general(a, b, (((1,), (1,)), ((), ())), preferred_element_type=f32)


def dot_tn(a, b):
    return lax.dot_general(a, b, (((0,), (0,)), ((), ())), preferred_element_type=f32)


def norm_rows(values):
    centre = jnp.mean(values, axis=-1, keepdims=True)
    centred = values - centre
    spread = jnp.mean(centred * centred, axis=-1, keepdims=True)
    inverse = lax.rsqrt(spread + epsilon)
    return (centred * inverse, inverse)


def norm_back(grad_normed, normed, inverse):
    first = jnp.mean(grad_normed, axis=-1, keepdims=True)
    second = jnp.mean(grad_normed * normed, axis=-1, keepdims=True)
    return inverse * (grad_normed - first - normed * second)


def lane_of(shape):
    return lax.broadcasted_iota(jnp.int32, shape, len(shape) - 1)


def swap_halves(values, half):
    lane = lane_of(values.shape)
    width = values.shape[-1]
    ahead = pltpu.roll(values, width - half, values.ndim - 1)
    behind = pltpu.roll(values, half, values.ndim - 1)
    return jnp.where(lane % (2 * half) < half, ahead, behind)


def in_three(values):
    high = values.astype(bf16)
    rest = values - high.astype(f32)
    middle = rest.astype(bf16)
    low = (rest - middle.astype(f32)).astype(bf16)
    return (high, middle, low)


def partner(blk, k):
    other = blk
    bit = 1
    while bit <= k:
        if k & bit:
            other = other + bit - 2 * bit * (other // bit % 2)
        bit *= 2
    return other


def remote(source, target, send, recv, blk, row):
    return pltpu.make_async_remote_copy(
        src_ref=source, dst_ref=target, send_sem=send, recv_sem=recv, device_id=(blk, row), device_id_type=MESH
    )


class Vec:
    shift_a, scale_a, gate_a, shift_m, scale_m, gate_m, factor_a, factor_m, gain_a, gain_m, step, b_down, b_up = range(13)


def silu(values):
    return values / (1.0 + jnp.exp(-values))


def ahead_kernel(
    tok_ref, grad_ref, w_ref, ada_ref, lengths_ref, steps_ref, table_ref, b_ada_ref, gain_a_ref, gain_m_ref, b_down_ref, b_up_ref, freq_ref,
    x_out, g_out, ht_out, q_out, k_out, v_out, cos_out, sin_out, att_ref, inv_ref, ab_ref, eb_ref, vec_ref,
    x_s, own_s, ht_s, q_s, k_s, v_s, cos_s, sin_s, w_s, ada_s, fq_s, fk_s, zero_s, send_x, recv_x, send_g, recv_g, local
):
    step, last = pl.program_id(0), pl.num_programs(0) - 1
    blk, row = lax.axis_index("blk"), lax.axis_index("rows")
    rows_dev, stretch, width = tok_ref.shape
    nblk = x_s.shape[0]
    half = width // H // 2
    scale = 1.0 / math.sqrt(2 * half)
    has_row = blk < rows_dev
    mine = jnp.minimum(blk, rows_dev - 1)
    kept = (
        (x_s, x_out), (ht_s, ht_out), (q_s, q_out), (k_s, k_out), (v_s, v_out), (cos_s, cos_out), (sin_s, sin_out)
    )
    free = len(kept)

    def move(k, source, target, send, recv, other):
        return remote(source.at[jnp.minimum(other, rows_dev - 1)], target.at[blk], send.at[k], recv.at[k], other, row)

    def each_sent(source, target, send, recv, what):
        for k in range(1, nblk):
            other = partner(blk, k)

            @pl.when(other < rows_dev)
            def sent():
                what(move(k, source, target, send, recv, other))

    def store(i):
        return pltpu.make_async_copy(kept[i][0], kept[i][1], local.at[i])

    def own_grad():
        return pltpu.make_async_copy(grad_ref.at[mine], g_out.at[blk], local.at[free + 3])

    def chunk(source):
        rows = pl.ds(pl.multiple_of(source * stretch, stretch), stretch)
        normed, unused = norm_rows(x_s[source].astype(f32))
        hidden = normed * vec(Vec.factor_a) + vec(Vec.shift_a)
        hidden_b = hidden.astype(bf16)
        ht_s[:, rows] = hidden.T.astype(bf16)
        cosine, sine = cos_s[rows, :], sin_s[rows, :]
        for part in range(3):
            out = dot(hidden_b, w_s[:, part * width : (part + 1) * width])
            for group in range(width // LANES):
                cols = slice(group * LANES, (group + 1) * LANES)
                piece = out[:, cols]
                if part == 2:
                    v_s[rows, cols] = piece.astype(bf16)
                    continue
                turned = (piece * cosine + swap_halves(piece, half) * sine).astype(bf16)
                if part == 0:
                    q_s[rows, cols] = (turned.astype(f32) * scale).astype(bf16)
                else:
                    k_s[rows, cols] = turned

    def vec(at):
        return vec_ref[at : at + 1, :]

    def prepare():
        wide = table_ref.shape[0]
        time = steps_ref[mine]
        hot = (lane_of((16, wide)) == time).astype(f32).astype(bf16)
        terms = in_three(silu(dot(hot, table_ref[...])))
        line = lax.broadcasted_iota(jnp.int32, (16, 1), 0)
        three = jnp.zeros(terms[0].shape, f32)
        for i, term in enumerate(terms):
            three = jnp.where(line == i, term.astype(f32), three)
        modulate = jnp.sum(dot(three.astype(bf16), ada_s[...]), axis=0, keepdims=True)
        flat = lambda ref: jnp.concatenate([ref[i : i + 1, :] for i in range(ref.shape[0])], axis=1).astype(f32)
        modulate = modulate + flat(b_ada_ref)
        gains = [flat(gain_a_ref), flat(gain_m_ref)]
        rows = [modulate[:, i * width : (i + 1) * width] for i in range(6)]
        rows += [gains[0] * (1.0 + rows[1]), gains[1] * (1.0 + rows[4])] + gains
        rows += [jnp.full((1, width), time, jnp.int32).astype(f32), flat(b_down_ref)]
        b_up = flat(b_up_ref)
        rows += [b_up[:, i * width : (i + 1) * width] for i in range(b_up.shape[1] // width)]
        vec_ref[...] = jnp.zeros_like(vec_ref)
        for i, value in enumerate(rows):
            vec_ref[i : i + 1, :] = value
        shape = fq_s.shape
        slots = lax.broadcasted_iota(jnp.int32, shape, 0)
        feature = lane_of(shape) % (2 * half)
        doc, start = jnp.zeros(shape, jnp.int32), jnp.zeros(shape, jnp.int32)
        last_end = jnp.int32(0)
        for i in range(lengths_ref.shape[1]):
            last_end = last_end + lengths_ref[mine, i]
            past = slots >= last_end
            doc = doc + past.astype(jnp.int32)
            start = jnp.where(past, last_end, start)
        fq_s[...] = jnp.where(feature == doc, -1e30, 0.0).astype(bf16)
        fk_s[...] = jnp.where((feature == doc) | (feature >= NDOC), 0.0, 1.0).astype(bf16)
        angle = (slots - start).astype(f32) * freq_ref[...]
        cos_s[...] = jnp.cos(angle)
        sine = jnp.sin(angle)
        sin_s[...] = jnp.where(feature < half, -sine, sine)

    @pl.when(step == 0)
    def begin():
        barrier = pltpu.get_barrier_semaphore()
        for k in range(1, nblk):
            pl.semaphore_signal(barrier, inc=1, device_id=(partner(blk, k), row), device_id_type=MESH)
        ada = pltpu.make_async_copy(ada_ref, ada_s, local.at[free])
        weights = pltpu.make_async_copy(w_ref, w_s, local.at[free + 1])
        own = pltpu.make_async_copy(tok_ref.at[mine], own_s, local.at[free + 2])
        for copy in (ada, weights, own):
            copy.start()
        pl.semaphore_wait(barrier, nblk - 1)
        each_sent(tok_ref, x_s, send_x, recv_x, lambda copy: copy.start())
        ada.wait()
        prepare()
        own.wait()

        @pl.when(has_row)
        def mine_first():
            x_s[blk] = own_s[...]

        @pl.when(jnp.logical_not(has_row))
        def nothing():
            x_s[...] = jnp.zeros_like(x_s)

        weights.wait()
        for k in range(nblk):
            source = partner(blk, k)
            if k:
                @pl.when(has_row)
                def arrived():
                    move(k, tok_ref, x_s, send_x, recv_x, source).wait_recv()

            chunk(source)
        each_sent(tok_ref, x_s, send_x, recv_x, lambda copy: copy.wait_send())
        each_sent(grad_ref, g_out, send_g, recv_g, lambda copy: copy.start())
        zero_s[...] = jnp.zeros_like(zero_s)

        @pl.when(has_row)
        def own_part():
            own_grad().start()

        @pl.when(jnp.logical_not(has_row))
        def no_part():
            for i in range(nblk):
                pltpu.make_async_copy(zero_s, g_out.at[i], local.at[free + 4 + i]).start()

        for i in range(len(kept)):
            store(i).start()

    cols = pl.ds(pl.multiple_of(step * LANES, LANES), LANES)
    seq = q_s.shape[0]
    first = lane_of((1, LANES)) < LANES // 2
    owns = (first, jnp.logical_not(first))
    one = jnp.ones((), bf16)
    keys = [jnp.where(own, k_s[:, cols], fk_s[...]) for own in owns]
    values = [jnp.where(own, v_s[:, cols], one) for own in owns]

    def score_of(start, head):
        rows = slice(start, start + CHUNK)
        return dot_nt(jnp.where(owns[head], q_s[rows, cols], fq_s[rows, :]), keys[head])

    items = [(start, head) for start in range(0, seq, CHUNK) for head in range(2)]
    ahead_score = score_of(*items[0])
    pieces = [None, None]
    for number, (start, head) in enumerate(items):
        score = ahead_score
        if number + 1 < len(items):
            ahead_score = score_of(*items[number + 1])
        rows = slice(start, start + CHUNK)
        top = jnp.max(score, axis=-1, keepdims=True)
        weight = jnp.exp(score - top).astype(bf16)
        eb_ref[0, head, rows, :] = weight
        mixed = dot(weight, values[head])
        inverse = 1.0 / pltpu.roll(mixed, LANES // 2, 1)
        pieces[head] = (mixed * inverse, inverse)
        if head == 1:
            attended = jnp.where(first, pieces[0][0], pieces[1][0])
            att_ref[rows, :] = attended
            ab_ref[rows, :] = attended.astype(bf16)
            inv_ref[rows, :] = jnp.where(first, pieces[0][1], pieces[1][1])

    @pl.when(step == last)
    def end():
        for i in range(len(kept)):
            store(i).wait()
        each_sent(grad_ref, g_out, send_g, recv_g, lambda copy: copy.wait_send())

        @pl.when(has_row)
        def received():
            own_grad().wait()
            for k in range(1, nblk):
                move(k, grad_ref, g_out, send_g, recv_g, partner(blk, k)).wait_recv()

        @pl.when(jnp.logical_not(has_row))
        def cleared():
            for i in range(nblk):
                pltpu.make_async_copy(zero_s, g_out.at[i], local.at[free + 4 + i]).wait()


def lines_of(vector):
    return vector.reshape(-1, LANES)


def ahead(tokens, grads, w_qkv, w_ada, lengths, timesteps, table, b_ada, gain_a, gain_m, b_down, b_up, nblk):
    rows_dev, stretch, width = tokens.shape
    seq = nblk * stretch
    head_dim = width // H
    freqs = np.float32(10000.0) ** (-np.arange(head_dim // 2, dtype=np.float32) * np.float32(2.0 / head_dim))
    freqs = np.concatenate([freqs] * 4)[None, :]
    small = [table, *(lines_of(a) for a in (b_ada, gain_a, gain_m, b_down, b_up)), freqs]
    pair = pl.BlockSpec((seq, LANES), lambda i: (0, i))
    fixed = lambda a: pl.BlockSpec(a.shape, lambda i: (0, 0), pipeline_mode=pl.Buffered(buffer_count=1))
    away = pl.BlockSpec(memory_space=pl.ANY)
    numbers = pl.BlockSpec(memory_space=pltpu.SMEM)
    blocks, flat, turn = (nblk, stretch, width), (seq, width), (seq, LANES)
    shape = jax.ShapeDtypeStruct
    vec = (16, width)
    return pl.pallas_call(
        ahead_kernel,
        grid=(width // LANES,),
        in_specs=[away] * 4 + [numbers] * 2 + [fixed(a) for a in small],
        out_specs=[away] * 8 + [pair] * 3
        + [pl.BlockSpec((1, 2, seq, seq), lambda i: (i, 0, 0, 0)), pl.BlockSpec(vec, lambda i: (0, 0))],
        out_shape=[
            shape(blocks, bf16), shape(blocks, bf16), shape(flat[::-1], bf16),
            shape(flat, bf16), shape(flat, bf16), shape(flat, bf16), shape(turn, f32), shape(turn, f32),
            shape(flat, f32), shape(flat, f32), shape(flat, bf16), shape((width // LANES, 2, seq, seq), bf16),
            shape(vec, f32),
        ],
        scratch_shapes=[
            pltpu.VMEM(blocks, bf16), pltpu.VMEM((stretch, width), bf16), pltpu.VMEM(flat[::-1], bf16),
            pltpu.VMEM(flat, bf16), pltpu.VMEM(flat, bf16), pltpu.VMEM(flat, bf16),
            pltpu.VMEM(turn, f32), pltpu.VMEM(turn, f32), pltpu.VMEM(w_qkv.shape, bf16), pltpu.VMEM(w_ada.shape, bf16),
            pltpu.VMEM(turn, bf16), pltpu.VMEM(turn, bf16), pltpu.VMEM((stretch, width), bf16),
        ] + [pltpu.SemaphoreType.DMA((nblk,))] * 4 + [pltpu.SemaphoreType.DMA((11 + nblk,))],
        compiler_params=pltpu.CompilerParams(
            collective_id=1, has_side_effects=True, vmem_limit_bytes=60 * MIB
        ),
        cost_estimate=pl.CostEstimate(
            flops=22 * seq * seq * width, bytes_accessed=24 * seq * width, transcendentals=H * seq * seq
        ),
    )(tokens, grads, w_qkv, w_ada, lengths, timesteps, *small)


def attend_back_pair(r, store):
    seq = r.q.shape[0]
    half = LANES // 4
    scale = 1.0 / math.sqrt(2 * half)
    lane = lane_of((1, LANES))
    first = lane < 2 * half
    owns = (first, jnp.logical_not(first))
    where = lane % (2 * half)
    one = jnp.ones((), bf16)
    scaled = r.datt[...].astype(f32) * r.inv[...]
    both = scaled * r.att[...]
    scaled_b = scaled.astype(bf16)
    values = []
    for head, own in enumerate(owns):
        total = -jnp.sum(jnp.where(own, both, 0.0), axis=-1, keepdims=True)
        delta = in_three(jnp.broadcast_to(total, both.shape))
        feature = jnp.zeros_like(scaled_b)
        for i in range(3):
            feature = jnp.where(where == i, delta[i], feature)
        r.da[head] = jnp.where(own, scaled_b, feature)
        values.append(jnp.where(own, r.v[...], one))
    queries_t = r.q[...].astype(f32).T.astype(bf16)
    scaled_t = scaled_b.astype(f32).T.astype(bf16)

    def grad_prob(start, head):
        return dot_nt(r.da[head, start : start + CHUNK, :], values[head])

    items = [(start, head) for start in range(0, seq, CHUNK) for head in range(2)]
    ahead_grad = grad_prob(*items[0])
    grad_q = {}
    for number, (start, head) in enumerate(items):
        grad_p = ahead_grad
        if number + 1 < len(items):
            ahead_grad = grad_prob(*items[number + 1])
        rows = slice(start, start + CHUNK)
        grad_s = (r.eb[0, head, rows, :].astype(f32) * grad_p).astype(bf16)
        r.ds[head, rows, :] = grad_s
        grad_q[start, head] = dot(grad_s, r.k[...])
    upper = lax.broadcasted_iota(jnp.int32, (LANES, 1), 0) < 2 * half
    grad_k = [dot(queries_t, r.ds[head]) for head in range(2)]
    grad_v = [dot(scaled_t, r.eb[0, head]) for head in range(2)]
    grad_k = jnp.where(upper, grad_k[0], grad_k[1]).T
    grad_v = jnp.where(upper, grad_v[0], grad_v[1]).T
    for start in range(0, seq, CHUNK):
        rows = slice(start, start + CHUNK)
        cosine, sine = r.cos[rows, :], r.sin[rows, :]
        turned = []
        for grad in (jnp.where(first, grad_q[start, 0], grad_q[start, 1]) * scale, grad_k[rows, :]):
            turned.append((grad * cosine - swap_halves(grad, half) * sine).astype(bf16))
        store(rows, turned[0], turned[1], grad_v[rows, :].astype(bf16))


def attend_back_kernel(names, *refs):
    r = types.SimpleNamespace(**dict(zip(names, refs)))

    def store(rows, *grads):
        for ref, grad in zip((r.dq, r.dk, r.dv), grads):
            ref[rows, :] = grad

    attend_back_pair(r, store)


def attend_back(q, k, v, grads, att, inv, eb, cosine, sine):
    seq, width = q.shape
    pair = pl.BlockSpec((seq, LANES), lambda i: (0, i))
    fixed = pl.BlockSpec((seq, LANES), lambda i: (0, 0))
    names = list(dict(q=0, k=0, v=0, datt=0, att=0, inv=0, eb=0, cos=0, sin=0, dq=0, dk=0, dv=0, da=0, ds=0))
    return pl.pallas_call(
        functools.partial(attend_back_kernel, names),
        grid=(width // LANES,),
        in_specs=[pair] * 6 + [pl.BlockSpec((1, 2, seq, seq), lambda i: (i, 0, 0, 0)), fixed, fixed],
        out_specs=[pair] * 3,
        out_shape=[jax.ShapeDtypeStruct((seq, width), bf16)] * 3,
        scratch_shapes=[pltpu.VMEM((2, seq, LANES), bf16), pltpu.VMEM((2, seq, seq), bf16)],
        compiler_params=pltpu.CompilerParams(vmem_limit_bytes=56 * MIB),
        cost_estimate=pl.CostEstimate(
            flops=32 * seq * seq * width, bytes_accessed=24 * seq * width + 2 * H * seq * seq, transcendentals=0
        ),
    )(q, k, v, grads, att, inv, eb, cosine, sine)


GELU = math.sqrt(2.0 / math.pi)
CUBE = 0.044715


def vec_rows(ref, *lines):
    return [ref[at : at + 1, :] for at in lines]


def feed_chunk(hidden, grad, w_up_ref, b_up, w_down_ref):
    u = dot(hidden, w_up_ref[...]) + b_up
    square = u * u
    turn = jnp.tanh(GELU * u * (1.0 + CUBE * square))
    half = 0.5 * (1.0 + turn)
    slope = half + (0.5 * GELU) * u * (1.0 - turn * turn) * (1.0 + 3.0 * CUBE * square)
    du = (dot_nt(grad, w_down_ref[...]) * slope).astype(bf16)
    return ((u * half).astype(bf16), du)


def feed_kernel(
    ab_ref, x_ref, g_ref, vec_ref, w_out_ref, w_up_ref, w_down_ref,
    result_ref, dx_ref, datt_ref, g_out_ref, g_up_ref, g_down_ref, gb_up_ref, sums_ref,
    h_s, ht_s, dz_s, dzt_s, y_s, z_s, dh_s, act_s, du_s, dyt_s
):
    step, last = pl.program_id(0), pl.num_programs(0) - 1
    seq, width = x_ref.shape
    wide = w_up_ref.shape[1]
    gate_a, factor_m, shift_m, gate_m, b_down = vec_rows(vec_ref, Vec.gate_a, Vec.factor_m, Vec.shift_m, Vec.gate_m, Vec.b_down)
    chunks = [slice(begin, begin + CHUNK) for begin in range(0, seq, CHUNK)]

    @pl.when(step == 0)
    def before():
        for rows in chunks:
            y = dot(ab_ref[rows, :], w_out_ref[...])
            y_s[rows, :] = y
            normed, unused = norm_rows(x_ref[rows, :].astype(f32) + gate_a * y)
            hidden = normed * factor_m + shift_m
            h_s[rows, :] = hidden.astype(bf16)
            ht_s[:, rows] = hidden.T.astype(bf16)
            grad = gate_m * g_ref[rows, :].astype(f32)
            dz_s[rows, :] = grad.astype(bf16)
            dzt_s[:, rows] = grad.T.astype(bf16)
        z_s[...] = jnp.zeros_like(z_s)
        dh_s[...] = jnp.zeros_like(dh_s)

    b_up = vec_ref[pl.ds(Vec.b_up + step, 1), :]
    bias_sum = jnp.zeros((1, wide), f32)
    for rows in chunks:
        act, du = feed_chunk(h_s[rows, :], dz_s[rows, :], w_up_ref, b_up, w_down_ref)
        act_s[rows, :] = act
        du_s[rows, :] = du
        bias_sum = bias_sum + jnp.sum(du.astype(f32), axis=0, keepdims=True)
        z_s[rows, :] += dot(act, w_down_ref[...])
        dh_s[rows, :] += dot_nt(du, w_up_ref[...])
    gb_up_ref[...] = bias_sum
    g_up_ref[0] = dot(ht_s[...], du_s[...]).astype(bf16)
    down = dot(dzt_s[...], act_s[...]).astype(bf16)
    g_down_ref[0, 0] = down[:, : wide // 2]
    g_down_ref[0, 1] = down[:, wide // 2 :]

    @pl.when(step == last)
    def after():
        sums = [jnp.zeros((1, width), f32) for unused in range(5)]
        for rows in chunks:
            y = y_s[rows, :]
            middle = x_ref[rows, :].astype(f32) + gate_a * y
            normed, inverse = norm_rows(middle)
            z = z_s[rows, :] + b_down
            result_ref[rows, :] = (middle + gate_m * z).astype(bf16)
            grad = g_ref[rows, :].astype(f32)
            dh = dh_s[rows, :]
            dx = grad + norm_back(dh * factor_m, normed, inverse)
            dx_ref[rows, :] = dx
            dy = gate_a * dx
            dyb = dy.astype(bf16)
            dyt_s[rows, :] = dyb
            datt_ref[rows, :] = dot_nt(dyb, w_out_ref[...]).astype(bf16)
            terms = (grad * z, dh, dh * normed, dx * y, dz_s[rows, :].astype(f32))
            sums = [a + jnp.sum(b, axis=0, keepdims=True) for a, b in zip(sums, terms)]
        g_out_ref[...] = dot_tn(ab_ref[...], dyt_s[...]).astype(bf16)
        for i in range(5):
            sums_ref[i : i + 1, :] = sums[i]


def feed(ab, x, g, vec, w_out, w_up, w_down):
    seq, width = x.shape
    ff = w_up.shape[1]
    wide = width
    fixed = lambda a: pl.BlockSpec(a.shape, lambda i: (0, 0))
    one = lambda shape: pl.BlockSpec(shape, lambda i: (0, 0))
    col = lambda r: pl.BlockSpec((r, wide), lambda i: (0, i))
    shape = jax.ShapeDtypeStruct
    return pl.pallas_call(
        feed_kernel,
        grid=(ff // wide,),
        in_specs=[
            fixed(ab), fixed(x), fixed(g), fixed(vec), fixed(w_out), col(width),
            pl.BlockSpec((wide, width), lambda i: (i, 0)),
        ],
        out_specs=[
            one((seq, width)), one((seq, width)), one((seq, width)), one((width, width)),
            pl.BlockSpec((1, width, wide), lambda i: (i, 0, 0)),
            pl.BlockSpec((1, 2, width, wide // 2), lambda i: (i, 0, 0, 0)), col(1), one((8, width)),
        ],
        out_shape=[
            shape((seq, width), bf16), shape((seq, width), f32), shape((seq, width), bf16),
            shape((width, width), bf16), shape((ff // wide, width, wide), bf16),
            shape((ff // wide, 2, width, wide // 2), bf16),
            shape((1, ff), f32), shape((8, width), f32),
        ],
        scratch_shapes=[
            pltpu.VMEM((seq, width), bf16), pltpu.VMEM((width, seq), bf16),
            pltpu.VMEM((seq, width), bf16), pltpu.VMEM((width, seq), bf16),
            pltpu.VMEM((seq, width), f32), pltpu.VMEM((seq, width), f32), pltpu.VMEM((seq, width), f32),
            pltpu.VMEM((seq, wide), bf16), pltpu.VMEM((seq, wide), bf16), pltpu.VMEM((seq, width), bf16),
        ],
        compiler_params=pltpu.CompilerParams(vmem_limit_bytes=60 * MIB),
        cost_estimate=pl.CostEstimate(
            flops=12 * seq * width * ff, bytes_accessed=30 * seq * width, transcendentals=seq * ff
        ),
    )(ab, x, g, vec, w_out, w_up, w_down)


def gather_kernel(nblk, nrows, in_ref, out_ref, send_r, recv_r, send_b, recv_b):
    blk, row = lax.axis_index("blk"), lax.axis_index("rows")
    barrier = pltpu.get_barrier_semaphore()
    for step in range(1, nblk):
        pl.semaphore_signal(
            barrier, inc=1, device_id=(lax.rem(blk + step, nblk), row), device_id_type=MESH
        )

    def greet(step, unused):
        pl.semaphore_signal(
            barrier, inc=1, device_id=(blk, lax.rem(row + step, nrows)), device_id_type=MESH
        )
        return unused

    lax.fori_loop(1, nrows, greet, 0)
    pl.semaphore_wait(barrier, nblk + nrows - 2)
    out_ref[blk, row] = in_ref[...]

    def over_rows(step):
        other = lax.rem(row + step, nrows)
        return pltpu.make_async_remote_copy(
            src_ref=in_ref,
            dst_ref=out_ref.at[blk, row],
            send_sem=send_r.at[step],
            recv_sem=recv_r.at[step],
            device_id=(blk, other),
            device_id_type=MESH,
        )

    def over_blk(step):
        other = lax.rem(blk + step, nblk)
        return pltpu.make_async_remote_copy(
            src_ref=out_ref.at[blk],
            dst_ref=out_ref.at[blk],
            send_sem=send_b.at[step],
            recv_sem=recv_b.at[step],
            device_id=(other, row),
            device_id_type=MESH,
        )

    def start(step, unused):
        over_rows(step).start()
        return unused

    def finish(step, unused):
        over_rows(step).wait()
        return unused

    lax.fori_loop(1, nrows, start, 0)
    lax.fori_loop(1, nrows, finish, 0)
    for step in range(1, nblk):
        over_blk(step).start()
    for step in range(1, nblk):
        over_blk(step).wait()


def gather_all(vector, nblk, nrows):
    count = vector.shape[0] // LANES
    return pl.pallas_call(
        functools.partial(gather_kernel, nblk, nrows),
        out_shape=jax.ShapeDtypeStruct((nblk, nrows, count, LANES), f32),
        in_specs=[pl.BlockSpec(memory_space=pltpu.VMEM)],
        out_specs=pl.BlockSpec(memory_space=pltpu.VMEM),
        scratch_shapes=[
            pltpu.SemaphoreType.DMA((nrows,)),
            pltpu.SemaphoreType.DMA((nrows,)),
            pltpu.SemaphoreType.DMA((nblk,)),
            pltpu.SemaphoreType.DMA((nblk,)),
        ],
        compiler_params=pltpu.CompilerParams(collective_id=0, has_side_effects=True),
    )(vector.reshape(count, LANES))


class Place:
    def __init__(self):
        self.blk, self.row = lax.axis_index("blk"), lax.axis_index("rows")
        self.x, self.y = self.blk % 2, self.blk // 2
        self.core, self.z = self.row % 2, self.row // 2

    def along_blk(self, k):
        return (partner(self.blk, k), self.row)

    def along_rows(self, k):
        return (self.blk, partner(self.row, k))


class Sems:
    def __init__(self, send, recv):
        self.send, self.recv, self.used = send, recv, 0

    def take(self, count):
        self.used += count
        return self.used - count

    def copy(self, index, source, target, device):
        return remote(source, target, self.send.at[index], self.recv.at[index], *device)


def part(index, size, step):
    return pl.ds(pl.multiple_of(index * size, step), size)


class Piece:
    def __init__(self, place, sems, dims, bufs, whole=None, own=None, store=None):
        self.p, self.sems, self.base = place, sems, sems.take(self.SEMS)
        self.whole, self.own, self.store = whole, own, store
        self.b = types.SimpleNamespace(**bufs)
        self.nz, share, cols = dims
        self.hs, self.hc, self.hz = share // 2, cols // 2, self.nz // 2

    def start(self, stage):
        for copy in self.copies(stage):
            copy.start()

    def wait(self, stage):
        for copy in self.copies(stage):
            copy.wait()

    def run(self, stage, go_on=True):
        if stage:
            self.wait(stage - 1)
            self.add(stage)
        if stage < 5 and go_on:
            self.start(stage)


ROW_BUFS = ("core", "a1", "b1", "a2", "b2", "r3", "zr", "ag")
FAR_BUFS = ("core", "z1", "z2", "pr", "ag")


def shapes_of(names, shapes):
    return {name: pltpu.VMEM(shape, bf16) for name, shape in zip(names, shapes)}


class RowPiece(Piece):
    SEMS = 11

    @staticmethod
    def scratch(nz, share, cols):
        hs, hc = share // 2, cols // 2
        return shapes_of(
            ROW_BUFS,
            [
                (nz, share, cols), (nz // 2, share, hc), (nz // 2, hs, cols), (nz // 2, hs, hc), (nz // 2, hs, hc),
                (nz, hs, hc), (nz, hs, hc), (4, hs, hc),
            ],
        )

    def row(self, y):
        return part(y, self.hs, 16)

    def col(self, x):
        return part(x, self.hc, LANES)

    def copies(self, stage):
        p, at, b, copy = self.p, self.base, self.b, self.sems.copy
        low, high = slice(0, self.hz), slice(self.hz, self.nz)
        if stage == 0:
            return [copy(at, self.whole.at[:, 1 - p.core], b.core, p.along_rows(1))]
        if stage == 1:
            return [
                copy(at + 1, b.core.at[low, :, self.col(1 - p.x)], b.a1, p.along_blk(1)),
                copy(at + 2, b.core.at[high, self.row(1 - p.y), :], b.b1, p.along_blk(2)),
            ]
        if stage == 2:
            return [
                copy(at + 3, b.a1.at[:, self.row(1 - p.y), :], b.a2, p.along_blk(2)),
                copy(at + 4, b.b1.at[:, :, self.col(1 - p.x)], b.b2, p.along_blk(1)),
            ]
        if stage == 3:
            return [
                copy(at + 4 + k, b.r3.at[partner(p.z, k)], b.zr.at[p.z], p.along_rows(2 * k))
                for k in range(1, self.nz)
            ]
        return [copy(at + 7 + k, b.ag.at[p.blk], b.ag.at[p.blk], p.along_blk(k)) for k in range(1, 4)]

    def add(self, stage):
        p, b = self.p, self.b
        row, col = self.row(p.y), self.col(p.x)
        if stage == 1:
            b.core[...] = b.core[...] + self.own()
        if stage == 2:
            b.a1[...] = b.a1[...] + b.core[: self.hz, :, col]
            b.b1[...] = b.b1[...] + b.core[self.hz :, row, :]
        if stage == 3:
            b.r3[: self.hz] = b.a1[:, row, :] + b.a2[...]
            b.r3[self.hz :] = b.b1[:, :, col] + b.b2[...]
        if stage == 4:
            total = b.r3[p.z].astype(f32)
            for k in range(1, self.nz):
                total = total + b.zr[partner(p.z, k)].astype(f32)
            b.ag[p.blk] = total.astype(bf16)
        if stage == 5:
            for q in range(4):
                rows = slice(q // 2 * self.hs, (q // 2 + 1) * self.hs)
                self.store(rows, q % 2 * self.hc, b.ag[q])


class FarPiece(Piece):
    SEMS = 9

    @staticmethod
    def scratch(nz, share, cols):
        hs, hc = share // 2, cols // 2
        return shapes_of(
            FAR_BUFS,
            [(nz, share, cols), (nz // 2, share, cols), (share, cols), (4, hs, hc), (4, hs, hc)],
        )

    def quarter(self, blk):
        return (part(blk // 2, self.hs, 16), part(blk % 2, self.hc, LANES))

    def copies(self, stage):
        p, at, b, copy = self.p, self.base, self.b, self.sems.copy
        low, high = p.z % 2, p.z // 2
        if stage == 0:
            return [copy(at, self.whole.at[:, 1 - p.core], b.core, p.along_rows(1))]
        if stage == 1:
            return [
                copy(at + 1, b.core.at[1 - low], b.z1.at[0], p.along_rows(2)),
                copy(at + 2, b.core.at[3 - low], b.z1.at[1], p.along_rows(2)),
            ]
        if stage == 2:
            return [copy(at + 3, b.z1.at[1 - high], b.z2, p.along_rows(4))]
        if stage == 3:
            return [
                copy(at + 3 + k, b.z2.at[self.quarter(partner(p.blk, k))], b.pr.at[p.blk], p.along_blk(k))
                for k in range(1, 4)
            ]
        return [copy(at + 3 + k, b.ag.at[p.blk], b.ag.at[p.blk], p.along_blk(k)) for k in range(1, 4)]

    def add(self, stage):
        p, b = self.p, self.b
        low, high = p.z % 2, p.z // 2
        if stage == 1:
            b.core[...] = b.core[...] + self.own()
        if stage == 2:
            for i in range(2):
                b.z1[i] = b.z1[i] + b.core[2 * i + low]
        if stage == 3:
            b.z2[...] = b.z2[...] + b.z1[high]
        if stage == 4:
            rows, cols = self.quarter(p.blk)
            total = b.z2[rows, cols].astype(f32)
            for k in range(1, 4):
                total = total + b.pr[partner(p.blk, k)].astype(f32)
            b.ag[p.blk] = total.astype(bf16)
        if stage == 5:
            for q in range(4):
                rows = slice(q // 2 * self.hs, (q // 2 + 1) * self.hs)
                self.store(rows, q % 2 * self.hc, b.ag[q])


class ColPiece(Piece):
    SEMS = 12

    @staticmethod
    def scratch(nz, depth, cols):
        return shapes_of(
            ROW_BUFS[:6],
            [
                (2, 2, 2, depth, cols), (2, depth, cols), (2, depth, cols), (depth, cols), (depth, cols),
                (2, depth, cols),
            ],
        )

    @staticmethod
    def shared(nz, depth, cols):
        return shapes_of(("zr", "ag"), [(nz, 2, depth, cols), (4, 2, depth, cols)])

    def __init__(self, place, sems, dims, bufs, owner, **kinds):
        super().__init__(place, sems, dims, bufs, **kinds)
        self.owner = owner
        self.depth = dims[1]

    def copies(self, stage):
        p, at, b, copy = self.p, self.base, self.b, self.sems.copy
        if stage == 0:
            return [copy(at, self.whole.at[1 - p.core], b.core, p.along_rows(1))]
        if stage == 1:
            return [
                copy(at + 1, b.core.at[:, 1 - p.x, 0], b.a1, p.along_blk(1)),
                copy(at + 2, b.core.at[1 - p.y, :, 1], b.b1, p.along_blk(2)),
            ]
        if stage == 2:
            return [
                copy(at + 3, b.a1.at[1 - p.y], b.a2, p.along_blk(2)),
                copy(at + 4, b.b1.at[1 - p.x], b.b2, p.along_blk(1)),
            ]
        return [copy(at + 8 + k, b.ag.at[p.blk], b.ag.at[p.blk], p.along_blk(k)) for k in range(1, 4)]

    def over_z(self, k):
        device = (self.p.blk, 2 * self.owner + self.p.core)
        return self.sems.copy(self.base + 5 + k, self.b.r3, self.b.zr.at[self.p.z], device)

    def from_afar(self, k, what):
        @pl.when(self.p.z == self.owner ^ k)
        def far():
            what(self.over_z(k))

    def here(self, what):
        @pl.when(self.p.z == self.owner)
        def at_owner():
            what()

    def start(self, stage):
        if stage == 3:
            for k in range(1, 4):
                self.from_afar(k, lambda copy: copy.start())
        elif stage == 4:
            self.here(lambda: [copy.start() for copy in self.copies(4)] and None)
        else:
            super().start(stage)

    def wait(self, stage):
        if stage == 3:
            for k in range(1, 4):
                self.from_afar(k, lambda copy: copy.wait_send())
            self.here(lambda: [self.over_z(k).wait_recv() for k in range(1, 4)] and None)
        elif stage == 4:
            self.here(lambda: [copy.wait() for copy in self.copies(4)] and None)
        else:
            super().wait(stage)

    def add(self, stage):
        p, b = self.p, self.b
        if stage == 1:
            b.core[...] = b.core[...] + self.own()
        if stage == 2:
            b.a1[...] = b.a1[...] + b.core[:, p.x, 0]
            b.b1[...] = b.b1[...] + b.core[p.y, :, 1]
        if stage == 3:
            b.r3[0] = b.a1[p.y] + b.a2[...]
            b.r3[1] = b.b1[p.x] + b.b2[...]
        if stage == 4:
            def summed():
                total = b.r3[...].astype(f32)
                for k in range(1, 4):
                    total = total + b.zr[self.owner ^ k].astype(f32)
                b.ag[p.blk] = total.astype(bf16)
            self.here(summed)
        if stage == 5:
            def stored():
                for q in range(8):
                    self.store(slice(q * self.depth, (q + 1) * self.depth), b.ag[q // 2, q % 2])
            self.here(stored)


class Bag:
    def __init__(self):
        self.names, self.items = [], []

    def add(self, name, item):
        if isinstance(item, dict):
            for key, value in item.items():
                self.add(f"{name}.{key}", value)
        else:
            self.names.append(name)
            self.items.append(item)


def group(refs, name):
    return {key[len(name) + 1 :]: ref for key, ref in vars(refs).items() if key.startswith(name + ".")}


def only(shapes, names):
    return {name: shapes[name] for name in names if name in shapes}


class Plan:
    def __init__(self):
        self.actions = {}

    def at(self, point, *actions):
        self.actions.setdefault(point, []).extend(actions)

    def stages(self, piece, first, points):
        for number, point in enumerate(points):
            self.at(point, lambda number=first + number: piece.run(number))

    def run(self, point):
        for action in self.actions.get(point, []):
            action()

    def under(self, step, number, point):
        if point in self.actions:
            @pl.when(step == number)
            def actions():
                self.run(point)


EARLY, LATE = 64, 32


def write_lines(target, lines):
    target[...] = jnp.zeros_like(target)
    at = 0
    for line in lines:
        for k in range(line.shape[1] // LANES):
            target[at : at + 1, :] = line[:, k * LANES : (k + 1) * LANES]
            at += 1


FEED_POINTS = ((7, 11), (11, 16), (16,), ())
HANDED = {1: ("core",), 2: ("a1", "b1"), 3: ("r3",)}


def feed_move_kernel(names, *refs):
    r = types.SimpleNamespace(**dict(zip(names, refs)))
    step, last = pl.program_id(0), pl.num_programs(0) - 1
    place = Place()
    sems = Sems(r.send, r.recv)
    seq, width = r.x.shape
    wide = r.w_up.shape[1]
    nz, unused, share, cols = r.gu.shape[1:]
    depth, dcols = r.gd.shape[-2:]
    nrows = 2 * nz
    plan = Plan()

    ups, downs = [], []
    for i in range(4):
        side = i % 2
        ups.append(
            RowPiece(
                place, sems, (nz, share, cols), group(r, f"u{i}"), r.gu.at[side],
                lambda side=side: r.gu[side, :, place.core],
            )
        )
        bufs = group(r, f"d{i}")
        downs.append(
            ColPiece(
                place, sems, (nz, depth, dcols), bufs, i, whole=r.gd.at[side],
                own=lambda side=side: r.gd[side, place.core],
            )
        )
    for i, points in enumerate(FEED_POINTS):
        for kind, piece in (("up", ups[i]), ("down", downs[i])):
            plan.stages(piece, 1, points)
            if len(points) < 5:
                plan.at(20, lambda kind=kind, piece=piece, i=i, stage=len(points) + 1: hand_over(piece, stage, f"{kind}{i}"))

    def hand_over(piece, stage, name):
        piece.run(stage, False)
        for key in HANDED[stage]:
            getattr(r, f"{name}.{key}")[...] = getattr(piece.b, key)[...]

    gate_a, factor_m, shift_m, gate_m, b_down = vec_rows(r.vec, Vec.gate_a, Vec.factor_m, Vec.shift_m, Vec.gate_m, Vec.b_down)
    chunks = [slice(begin, begin + CHUNK) for begin in range(0, seq, CHUNK)]

    @pl.when(step == 0)
    def before():
        greet(place, 4, nrows)

        def enter(number, unused):
            rows = part(number, CHUNK, CHUNK)
            y = dot(r.ab[rows, :], r.w_out[...])
            r.y[rows, :] = y
            normed, unused = norm_rows(r.x[rows, :].astype(f32) + gate_a * y)
            hidden = normed * factor_m + shift_m
            r.h[rows, :] = hidden.astype(bf16)
            r.ht[:, rows] = hidden.T.astype(bf16)
            grad = gate_m * r.g[rows, :].astype(f32)
            r.dz[rows, :] = grad.astype(bf16)
            r.dzt[:, rows] = grad.T.astype(bf16)
            return 0

        lax.fori_loop(0, len(chunks), enter, 0)
        r.z[...] = jnp.zeros_like(r.z)
        r.dh[...] = jnp.zeros_like(r.dh)

    b_up = r.vec[pl.ds(Vec.b_up + step, 1), :]
    bias_sum = jnp.zeros((1, wide), f32)
    for number, rows in enumerate(chunks):
        for i in range(4):
            plan.under(step, i, 4 * i + number)
        act, du = feed_chunk(r.h[rows, :], r.dz[rows, :], r.w_up, b_up, r.w_down)
        r.act[rows, :] = act
        r.du[rows, :] = du
        bias_sum = bias_sum + jnp.sum(du.astype(f32), axis=0, keepdims=True)
        r.z[rows, :] += dot(act, r.w_down[...])
        r.dh[rows, :] += dot_nt(du, r.w_up[...])
    r.gb[pl.ds(step, 1), :] = bias_sum
    side = step % 2
    r.gu[side] = dot(r.ht[...], r.du[...]).astype(bf16).reshape(r.gu.shape[1:])
    down = dot(r.dzt[...], r.act[...]).astype(bf16)
    for core in range(2):
        half = down[:, core * dcols : (core + 1) * dcols]
        r.gd[side, core] = half.reshape(r.gd.shape[2:])
    for i in range(4):
        @pl.when(step == i)
        def sent():
            ups[i].run(0)
            downs[i].run(0)

    @pl.when(step == last)
    def after():
        plan.run(16)

        def leave(number, sums):
            rows = part(number, CHUNK, CHUNK)
            y = r.y[rows, :]
            middle = r.x[rows, :].astype(f32) + gate_a * y
            normed, inverse = norm_rows(middle)
            z = r.z[rows, :] + b_down
            r.result[rows, :] = (middle + gate_m * z).astype(bf16)
            grad = r.g[rows, :].astype(f32)
            dh = r.dh[rows, :]
            dx = grad + norm_back(dh * factor_m, normed, inverse)
            r.dx[rows, :] = dx
            dyb = (gate_a * dx).astype(bf16)
            r.dy[rows, :] = dyb
            r.datt[rows, :] = dot_nt(dyb, r.w_out[...]).astype(bf16)
            terms = (grad * z, dh, dh * normed, dx * y, r.dz[rows, :].astype(f32))
            return tuple(a + jnp.sum(b, axis=0, keepdims=True) for a, b in zip(sums, terms))

        sums = lax.fori_loop(0, len(chunks), leave, tuple(jnp.zeros((1, width), f32) for unused in range(5)))
        plan.run(18)
        r.g_out[...] = dot_tn(r.ab[...], r.dy[...]).astype(bf16)
        gain_m, scale_m, time = vec_rows(r.vec, Vec.gain_m, Vec.scale_m, Vec.step)
        dgate_m, dshift_m, along_m, dgate_a, grad_b_down = sums
        lines = [dgate_a, dshift_m, along_m * gain_m, dgate_m, along_m * (1.0 + scale_m), grad_b_down]
        lines += [r.gb[i : i + 1, :] for i in range(4)] + [time[:, :LANES]]
        write_lines(r.pack, lines)
        r.early[...] = r.pack[...].astype(bf16)
        plan.run(20)


def feed_move(ab, x, g, vec, w_out, w_up, w_down, nrows):
    seq, width = x.shape
    ff = w_up.shape[1]
    wide = width
    nz, share, depth, dcols = nrows // 2, width // nrows, width // 8, wide // 2
    once = pl.Buffered(buffer_count=1)
    fixed = lambda a: pl.BlockSpec(a.shape, lambda i: (0, 0), pipeline_mode=once)
    col = lambda r: pl.BlockSpec((r, wide), lambda i: (0, i))
    shape = jax.ShapeDtypeStruct
    ins, outs, scratch = Bag(), Bag(), Bag()
    for name, spec in (
        ("ab", fixed(ab)), ("x", fixed(x)), ("g", fixed(g)), ("vec", fixed(vec)), ("w_out", fixed(w_out)),
        ("w_up", col(width)), ("w_down", pl.BlockSpec((wide, width), lambda i: (i, 0))),
    ):
        ins.add(name, spec)
    for name, dims, kind in (
        ("result", (seq, width), bf16), ("dx", (seq, width), f32), ("datt", (seq, width), bf16),
        ("g_out", (width, width), bf16), ("early", (EARLY, LANES), bf16),
    ):
        outs.add(name, shape(dims, kind))
    row_bufs, col_bufs = RowPiece.scratch(nz, share, wide), ColPiece.scratch(nz, depth, dcols)
    for i, points in enumerate(FEED_POINTS):
        if len(points) < 5:
            for kind, bufs in (("up", row_bufs), ("down", col_bufs)):
                for key in HANDED[len(points) + 1]:
                    outs.add(f"{kind}{i}.{key}", shape(bufs[key].shape, bf16))
    for name in ("h", "dz", "act", "du", "dy"):
        scratch.add(name, pltpu.VMEM((seq, width), bf16))
    for name in ("ht", "dzt"):
        scratch.add(name, pltpu.VMEM((width, seq), bf16))
    for name in ("y", "z", "dh"):
        scratch.add(name, pltpu.VMEM((seq, width), f32))
    scratch.add("gb", pltpu.VMEM((8, wide), f32))
    scratch.add("pack", pltpu.VMEM((EARLY, LANES), f32))
    scratch.add("gu", pltpu.VMEM((2, nz, 2, share, wide), bf16))
    scratch.add("gd", pltpu.VMEM((2, 2, 2, 2, 2, depth, dcols), bf16))
    for i, points in enumerate(FEED_POINTS):
        kept = ROW_BUFS[: (1, 3, 6)[len(points)]]
        scratch.add(f"u{i}", only(row_bufs, kept))
        scratch.add(f"d{i}", only(col_bufs, kept))
    count = 4 * (RowPiece.SEMS + ColPiece.SEMS)
    scratch.add("send", pltpu.SemaphoreType.DMA((count,)))
    scratch.add("recv", pltpu.SemaphoreType.DMA((count,)))
    results = pl.pallas_call(
        functools.partial(feed_move_kernel, ins.names + outs.names + scratch.names),
        grid=(ff // wide,),
        in_specs=ins.items,
        out_specs=[pl.BlockSpec(o.shape, lambda i, n=len(o.shape): (0,) * n) for o in outs.items],
        out_shape=outs.items,
        scratch_shapes=scratch.items,
        compiler_params=pltpu.CompilerParams(collective_id=3, has_side_effects=True, vmem_limit_bytes=62 * MIB),
        cost_estimate=pl.CostEstimate(
            flops=12 * seq * width * ff, bytes_accessed=30 * seq * width, transcendentals=seq * ff
        ),
    )(ab, x, g, vec, w_out, w_up, w_down)
    return dict(zip(outs.names, results))


class Gather:
    def __init__(self, place, sems, source, target):
        self.p, self.sems, self.source, self.target = place, sems, source, target
        self.nblk, self.nrows = target.shape[:2]
        self.base = sems.take(self.nblk + self.nrows)

    def copies(self, stage):
        p = self.p
        if stage == 0:
            return [
                self.sems.copy(self.base + k, self.source, self.target.at[p.blk, p.row], p.along_rows(k))
                for k in range(1, self.nrows)
            ]
        return [
            self.sems.copy(self.base + self.nrows + k, self.target.at[p.blk], self.target.at[p.blk], p.along_blk(k))
            for k in range(1, self.nblk)
        ]

    def run(self, stage):
        if stage:
            for copy in self.copies(stage - 1):
                copy.wait()
        else:
            self.target[self.p.blk, self.p.row] = self.source[...]
        if stage < 2:
            for copy in self.copies(stage):
                copy.start()


class Return:
    def __init__(self, place, sems, source, target, local):
        self.p, self.sems, self.source, self.target, self.local = place, sems, source, target, local
        self.rows, self.nblk = target.shape[0], source.shape[0]
        self.base = sems.take(self.nblk)
        self.mine = jnp.minimum(place.blk, self.rows - 1)

    def copy(self, k):
        device = self.p.along_blk(k)
        return self.sems.copy(self.base + k, self.source.at[device[0]], self.target.at[self.mine], device)

    def own(self):
        return pltpu.make_async_copy(self.source.at[self.p.blk], self.target.at[self.mine], self.local)

    def start(self, ks):
        @pl.when(self.p.blk < self.rows)
        def sent():
            for k in ks:
                (self.copy(k) if k else self.own()).start()

    def finish(self):
        @pl.when(self.p.blk < self.rows)
        def left():
            self.own().wait()
            for k in range(1, self.nblk):
                self.copy(k).wait_send()

        for k in range(1, self.nblk):
            @pl.when(partner(self.p.blk, k) < self.rows)
            def arrived():
                self.copy(k).wait_recv()


def greet(place, nblk, nrows):
    barrier = pltpu.get_barrier_semaphore()
    for k in range(1, nblk):
        pl.semaphore_signal(barrier, inc=1, device_id=place.along_blk(k), device_id_type=MESH)
    for k in range(1, nrows):
        pl.semaphore_signal(barrier, inc=1, device_id=place.along_rows(k), device_id_type=MESH)
    pl.semaphore_wait(barrier, nblk + nrows - 2)


BEHIND_POINTS = ((8, 11), (8, 11), (6, 10, 13), (7, 10, 12, 15))
OUTER_POINTS = (5, 9, 11, 13, 15)
EARLY_POINTS = (8, 16)
RESULT_POINTS = (0, 0, 0, 0)
LATE_POINTS = ((9, 11, 13, 15, 16), (12, 13, 15, 17, 18), (12, 13, 15, 17, 19))


def behind_kernel(names, *refs):
    r = types.SimpleNamespace(**dict(zip(names, refs)))
    step, last = pl.program_id(0), pl.num_programs(0) - 1
    place = Place()
    sems = Sems(r.send, r.recv)
    nblk, stretch, width = r.x.shape
    nrows = r.early_g.shape[1]
    nz, unused, share, cols = r.gq.shape[1:]
    depth, dcols = getattr(r, "d.ag").shape[-2:]
    seq = nblk * stretch
    dims, ddims = (nz, share, cols), (nz, depth, dcols)

    def store_at(ref, begin):
        def store(rows, col, value):
            ref[rows, begin + col : begin + col + value.shape[1]] = value
        return store

    def store_qkv(j):
        def store(rows, col, value):
            for k in range(value.shape[1] // LANES):
                lane = col + k * LANES
                at = lane // (2 * LANES) * width + j * 2 * LANES + lane % (2 * LANES)
                r.share_qkv[rows, at : at + LANES] = value[:, k * LANES : (k + 1) * LANES]
        return store

    def store_down(rows, value):
        r.share_down[rows, :] = value

    shared = group(r, "d")
    carried = []
    for i, points in enumerate(FEED_POINTS):
        if len(points) < 5:
            up = RowPiece(
                place, sems, dims, dict(group(r, f"u{i}"), **group(r, f"up{i}")), store=store_at(r.share_up, i * cols)
            )
            down = ColPiece(
                place, sems, ddims, dict(shared, **group(r, f"d{i}"), **group(r, f"down{i}")), i, store=store_down
            )
            carried.append((len(points) + 1, up, down))
    outer = RowPiece(
        place, sems, dims, group(r, "o"), r.g_out, lambda: r.own_out[...], store_at(r.share_out, 0)
    )
    load = pltpu.make_async_copy(r.g_out.at[:, place.core], r.own_out, r.local.at[2])
    late_pieces = [
        kind(
            place, sems, dims, group(r, f"q{j}"), r.gq.at[j], lambda j=j: r.gq[j, :, place.core], store_qkv(j)
        )
        for j, kind in enumerate((RowPiece, RowPiece, RowPiece))
    ]
    results = Return(place, sems, r.result, r.tok_out, r.local.at[0])
    grads = Return(place, sems, r.gt, r.grad_out, r.local.at[1])
    early = Gather(place, sems, r.early_s, r.early_g)
    late = Gather(place, sems, r.late_b, r.late_g)

    def open_up():
        greet(place, nblk, nrows)
        load.start()
        for stage, up, down in carried:
            up.start(stage)
            down.start(stage)
        outer.run(0)
        r.share_down[...] = jnp.zeros_like(r.share_down)

    def start_early():
        r.early_s[...] = r.early[...]
        early.run(0)

    plan = Plan()
    plan.at(0, open_up)
    plan.at(1, start_early, load.wait)
    for (stage, up, down), points in zip(carried, BEHIND_POINTS):
        for piece in (up, down):
            plan.stages(piece, stage + 1, points)
    plan.stages(outer, 1, OUTER_POINTS)
    plan.stages(early, 1, EARLY_POINTS)
    for k, point in zip((3, 1, 2, 0), RESULT_POINTS):
        plan.at(point, lambda k=k: results.start([k]))
    for piece, points in zip(late_pieces, LATE_POINTS):
        plan.stages(piece, 1, points)

    for i in range(6):
        plan.under(step, i, 2 * i)
    side = step % 2 * LANES

    def store(rows, *grads):
        for i, grad in enumerate(grads):
            r.dqkv[rows, pl.ds(pl.multiple_of(2 * i * LANES + side, LANES), LANES)] = grad

    attend_back_pair(r, store)
    for i in range(6):
        plan.under(step, i, 2 * i + 1)

    @pl.when(step % 2 == 1)
    def projections():
        number = step // 2
        grad_w = dot(r.ht[...], r.dqkv[...]).astype(bf16)
        r.gq[number] = grad_w.reshape(r.gq.shape[1:])
        for j, piece in enumerate(late_pieces):
            @pl.when(number == j)
            def sent():
                piece.run(0)

        for rows in (slice(begin, begin + CHUNK) for begin in range(0, seq, CHUNK)):
            added = dot_nt(r.dqkv[rows, : 2 * LANES], r.wq[...])
            added = added + dot_nt(r.dqkv[rows, 2 * LANES : 4 * LANES], r.wk[...])
            added = added + dot_nt(r.dqkv[rows, 4 * LANES :], r.wv[...])

            @pl.when(number == 0)
            def fresh():
                r.dh[rows, :] = added

            @pl.when(number > 0)
            def more():
                r.dh[rows, :] += added

    @pl.when(step == last)
    def tail():
        factor, gain, scale = vec_rows(r.vec, Vec.factor_a, Vec.gain_a, Vec.scale_a)
        total = [jnp.zeros((1, width), f32) for unused in range(2)]

        def chunk(k):
            slot = partner(place.blk, k)
            rows = pl.ds(pl.multiple_of(slot * stretch, stretch), stretch)
            normed, inverse = norm_rows(r.x[slot].astype(f32))
            dh = r.dh[rows, :]
            r.gt[slot] = (r.dx[rows, :] + norm_back(dh * factor, normed, inverse)).astype(bf16)
            grads.start([k])
            total[0] = total[0] + jnp.sum(dh, axis=0, keepdims=True)
            total[1] = total[1] + jnp.sum(dh * normed, axis=0, keepdims=True)

        plan.run(12)
        chunk(3)
        plan.run(13)
        chunk(1)
        plan.run(14)
        chunk(2)
        chunk(0)
        write_lines(r.late_s, (total[0], total[1] * gain, total[1] * (1.0 + scale)))
        r.late_b[...] = r.late_s[...].astype(bf16)
        late.run(0)
        plan.run(15)
        plan.run(16)
        r.early_out[...] = r.early_g[...]
        late.run(1)
        plan.run(17)
        late.run(2)
        r.late_out[...] = r.late_g[...]
        plan.run(18)
        plan.run(19)
        results.finish()
        grads.finish()


def behind(q, k, v, grads, att, inv, eb, cosine, sine, w_qkv, hidden_t, x, dx, vec, early, handed, g_out, result,
           rows_dev, nrows):
    seq, width = q.shape
    nblk, stretch, unused = x.shape
    nz, share, cols, depth, dcols = nrows // 2, width // nrows, width, width // 8, width // 2
    pair = pl.BlockSpec((seq, LANES), lambda i: (0, i))
    once = pl.Buffered(buffer_count=1)
    fixed = lambda a: pl.BlockSpec(a.shape, lambda i: (0,) * len(a.shape), pipeline_mode=once)
    away = pl.BlockSpec(memory_space=pl.ANY)
    per = width // (2 * LANES)
    weight = lambda n: pl.BlockSpec((width, 2 * LANES), lambda i: (0, n * per + i // 2))
    shape = jax.ShapeDtypeStruct
    ins, args, outs, scratch = Bag(), [], Bag(), Bag()
    for name, spec, value in (
        ("q", pair, q), ("k", pair, k), ("v", pair, v), ("datt", pair, grads), ("att", pair, att), ("inv", pair, inv),
        ("eb", pl.BlockSpec((1, 2, seq, seq), lambda i: (i, 0, 0, 0)), eb), ("cos", fixed(cosine), cosine), ("sin", fixed(sine), sine),
        ("wq", weight(0), w_qkv), ("wk", weight(1), w_qkv), ("wv", weight(2), w_qkv),
        ("ht", fixed(hidden_t), hidden_t), ("x", fixed(x), x), ("dx", fixed(dx), dx), ("vec", fixed(vec), vec),
        ("early", fixed(early), early), *((name, fixed(value), value) for name, value in handed.items()),
        ("g_out", away, g_out), ("result", away, result),
    ):
        ins.add(name, spec)
        args.append(value)
    back = shape((rows_dev, stretch, width), bf16)
    late = (LATE, LANES)
    for name, value in (
        ("tok_out", back), ("grad_out", back), ("share_qkv", shape((share, 3 * width), bf16)),
        ("share_out", shape((share, cols), bf16)), ("share_up", shape((share, 4 * cols), bf16)),
        ("share_down", shape((8 * depth, dcols), bf16)),
        ("early_out", shape((nblk, nrows) + early.shape, bf16)), ("late_out", shape((nblk, nrows) + late, bf16)),
    ):
        outs.add(name, value)
    for name, dims, kind in (
        ("da", (2, seq, LANES), bf16), ("ds", (2, seq, seq), bf16),
        ("dqkv", (seq, 6 * LANES), bf16), ("dh", (seq, width), f32), ("gq", (3, nz, 2, share, cols), bf16),
        ("gt", (nblk, stretch, width), bf16), ("early_s", early.shape, bf16), ("late_s", late, f32),
        ("late_b", late, bf16), ("early_g", (nblk, nrows) + early.shape, bf16),
        ("late_g", (nblk, nrows) + late, bf16), ("own_out", (nz, share, cols), bf16),
    ):
        scratch.add(name, pltpu.VMEM(dims, kind))
    near, cross = RowPiece.scratch(nz, share, cols), ColPiece.scratch(nz, depth, dcols)
    for i, points in enumerate(FEED_POINTS):
        if len(points) < 5:
            kept = ROW_BUFS[(1, 3, 6)[len(points)] :]
            scratch.add(f"u{i}", only(near, kept))
            scratch.add(f"d{i}", only(cross, kept))
    scratch.add("d", ColPiece.shared(nz, depth, dcols))
    scratch.add("o", near)
    for j in range(3):
        scratch.add(f"q{j}", near)
    count = 8 * RowPiece.SEMS + 4 * ColPiece.SEMS + 2 * nblk + 2 * (nblk + nrows)
    scratch.add("send", pltpu.SemaphoreType.DMA((count,)))
    scratch.add("recv", pltpu.SemaphoreType.DMA((count,)))
    scratch.add("local", pltpu.SemaphoreType.DMA((3,)))
    results = pl.pallas_call(
        functools.partial(behind_kernel, ins.names + outs.names + scratch.names),
        grid=(width // LANES,),
        in_specs=ins.items,
        out_specs=[away, away] + [pl.BlockSpec(o.shape, lambda i, n=len(o.shape): (0,) * n) for o in outs.items[2:]],
        out_shape=outs.items,
        scratch_shapes=scratch.items,
        compiler_params=pltpu.CompilerParams(collective_id=2, has_side_effects=True, vmem_limit_bytes=62 * MIB),
        cost_estimate=pl.CostEstimate(
            flops=52 * seq * seq * width, bytes_accessed=40 * seq * width, transcendentals=H * seq * seq
        ),
    )(*args)
    return dict(zip(outs.names, results))


FETCH = ("tok", "grad", "early", "late", "table", "ada", "up", "qkv", "outer", "down")


def finish_kernel(names, *refs):
    r = types.SimpleNamespace(**dict(zip(names, refs)))
    row = lax.axis_index("rows")
    loads = {name: pltpu.make_async_copy(getattr(r, name + "_in"), getattr(r, name), r.local.at[i]) for i, name in enumerate(FETCH)}
    for load in loads.values():
        load.start()
    moves = []
    for i, (name, target) in enumerate((("tok", r.out), ("grad", r.grad_tokens))):
        loads[name].wait()
        moves.append(pltpu.make_async_copy(getattr(r, name), target, r.local.at[len(FETCH) + i]))
        moves[-1].start()
    for name in ("early", "late", "table", "ada"):
        loads[name].wait()
    rows_dev = r.out.shape[0]
    nblk, nrows = r.early.shape[:2]
    count = rows_dev * nrows
    width = r.out.shape[-1]
    per = width // LANES
    for b in range(rows_dev):
        r.early_s[b] = r.early[b].astype(f32)
        r.late_s[b] = r.late[b].astype(f32)
    r.mod[...] = jnp.zeros_like(r.mod)

    def of_all(ref, line):
        return [ref[b, :, line, :] for b in range(rows_dev)]

    for i in range(6 * per):
        blocks = of_all(r.late_s, i) if i < 2 * per else of_all(r.early_s, i - 2 * per)
        for b, block in enumerate(blocks):
            r.mod[b * nrows : (b + 1) * nrows, i * LANES : (i + 1) * LANES] = block
    total = jnp.sum(r.early_s[...], axis=(0, 1))
    late_total = jnp.sum(r.late_s[...], axis=(0, 1))

    ff = r.b_up.shape[0]
    r.gain_m[...] = total[4 * per : 5 * per]
    r.b_down[...] = total[5 * per : 6 * per]
    r.b_up[...] = total[6 * per : 6 * per + ff]
    r.gain_a[...] = late_total[2 * per : 3 * per]
    r.b_ada[: 2 * per, :] = late_total[: 2 * per]
    r.b_ada[2 * per :, :] = total[: 4 * per]
    mod = r.mod[...]
    mod_b = mod.astype(bf16)
    steps = r.steps
    steps[...] = jnp.full(steps.shape, -1.0, f32)
    for b, block in enumerate(of_all(r.early_s, 6 * per + ff)):
        steps[b * nrows : (b + 1) * nrows, :] = block
    entries = r.table.shape[0]
    hot = (steps[:, :entries] == lane_of((1, entries)).astype(f32)).astype(f32).astype(bf16)
    conds = dot(hot, r.table[...])
    r.act_t[...] = jnp.concatenate([silu(conds), jnp.zeros((LANES - conds.shape[0], conds.shape[1]), f32)]).T
    share = r.w_ada.shape[0]
    mine = r.act_t[pl.ds(pl.multiple_of(row * share, share), share), : conds.shape[0]]
    r.w_ada[...] = sum(dot(term, mod_b) for term in in_three(mine))
    grad_act = dot_nt(mod_b, r.ada[...])
    sigmoid = 1.0 / (1.0 + jnp.exp(-conds))
    grad_cond = grad_act * sigmoid * (1.0 + conds * (1.0 - sigmoid))
    r.grad_table[...] = sum(dot_tn(hot, term) for term in in_three(grad_cond))
    for name in ("up", "qkv", "outer", "down"):
        loads[name].wait()
    r.w_up[...] = r.up[...].astype(f32)
    r.w_qkv[...] = r.qkv[...].astype(f32)
    r.w_out[...] = r.outer[...].astype(f32)

    r.w_down[...] = r.down[...].astype(f32).T
    for move in moves:
        move.wait()


def finish(o, table, w_ada):
    rows_dev, stretch, width = o["tok_out"].shape
    nblk, nrows = o["early_out"].shape[:2]
    shape = jax.ShapeDtypeStruct
    away, near = pl.BlockSpec(memory_space=pl.ANY), pl.BlockSpec(memory_space=pltpu.VMEM)
    args, outs, scratch = [], Bag(), Bag()
    fetched = dict(
        tok=o["tok_out"], grad=o["grad_out"], early=o["early_out"], late=o["late_out"], table=table, ada=w_ada,
        up=o["share_up"], qkv=o["share_qkv"], outer=o["share_out"], down=o["share_down"],
    )
    for name in FETCH:
        args.append(fetched[name])
        scratch.add(name, pltpu.VMEM(fetched[name].shape, fetched[name].dtype))
    names = [name + "_in" for name in FETCH] + ["out", "grad_tokens"]
    six, share, per = 6 * width, width // nrows, width // LANES
    ff = o["share_up"].shape[1]
    for name, dims in (
        ("grad_table", table.shape), ("w_ada", (w_ada.shape[0] // nrows, six)), ("b_ada", (6 * per, LANES)),
        ("gain_a", (per, LANES)), ("w_qkv", (share, 3 * width)), ("w_out", (share, width)), ("gain_m", (per, LANES)),
        ("w_up", (share, ff)), ("b_up", (ff // LANES, LANES)), ("w_down", (ff // nrows, width)),
        ("b_down", (per, LANES)),
    ):
        outs.add(name, shape(dims, f32))
    lines = 32
    for name, dims in (
        ("early_s", (rows_dev, nrows, EARLY, LANES)), ("late_s", (rows_dev, nrows, LATE, LANES)), ("mod", (lines, six)),
        ("steps", (lines, LANES)), ("act_t", (LANES, LANES)),
    ):
        scratch.add(name, pltpu.VMEM(dims, f32))
    scratch.add("local", pltpu.SemaphoreType.DMA((2 + len(FETCH),)))
    moved = shape((rows_dev, stretch, width), bf16)
    return pl.pallas_call(
        functools.partial(finish_kernel, names + outs.names + scratch.names),
        in_specs=[away] * len(args),
        out_specs=[away, away] + [near] * len(outs.items),
        out_shape=[moved, moved] + outs.items,
        scratch_shapes=scratch.items,
        compiler_params=pltpu.CompilerParams(vmem_limit_bytes=62 * MIB),
    )(*args)


def rows_out(whole, rows, me, nblk):
    parts = [lax.dynamic_index_in_dim(whole, me, 0, keepdims=False)]
    for k in range(1, nblk):
        part = lax.dynamic_index_in_dim(whole, me ^ k, 0, keepdims=False)
        pairs = [(s, s ^ k) for s in range(nblk) if s < rows]
        parts.append(lax.ppermute(part, "blk", pairs))
    stacked = jnp.stack(parts)
    return jnp.take(stacked, jnp.arange(rows) ^ me, axis=0)


def pick(array, index, axis=0):
    return lax.dynamic_index_in_dim(array, index, axis, keepdims=False)


def xor_move(array, axis, size, k):
    return lax.ppermute(array, axis, [(s, s ^ k) for s in range(size)])


def halve(array, axis, bit, name, size, k):
    kept = pick(array, bit, axis).astype(f32)
    sent = pick(array, 1 - bit, axis)
    return (kept + xor_move(sent, name, size, k).astype(f32)).astype(bf16)


def reduce_weight(grad, blk, row, nblk, nrows):
    total, cols = grad.shape
    share = total // nrows
    nz = nrows // 2
    core, z = row % 2, row // 2
    x, y = blk % 2, blk // 2
    part = halve(grad.reshape(nz, 2, share, cols), 1, core, "rows", nrows, 1)
    part = part.reshape(nz, 2, share // 2, cols)
    front, back = part[: nz // 2], part[nz // 2 :]
    split = lambda a: jnp.stack([a[..., : cols // 2], a[..., cols // 2 :]])
    front = halve(split(front), 0, x, "blk", nblk, 1)
    back = halve(back, 1, y, "blk", nblk, 2)
    front = halve(front, 1, y, "blk", nblk, 2)
    back = halve(split(back), 0, x, "blk", nblk, 1)
    part = jnp.concatenate([front, back], axis=0)
    if nz <= 4:
        summed = pick(part, z).astype(f32)
        for k in range(1, nz):
            summed = summed + xor_move(pick(part, z ^ k), "rows", nrows, 2 * k).astype(f32)
        part = summed.astype(bf16)
    else:
        k = nz // 2
        while k:
            pairs = part.reshape((2, k) + part.shape[1:])
            part = halve(pairs, 0, (z // k) % 2, "rows", nrows, 2 * k)
            k //= 2
        part = part[0]
    quarters = [part] + [xor_move(part, "blk", nblk, k) for k in range(1, 4)]
    quarters = jnp.take(jnp.stack(quarters), jnp.arange(4) ^ blk, axis=0)
    ordered = quarters.reshape(2, 2, share // 2, cols // 2).transpose(0, 2, 1, 3)
    return ordered.reshape(share, cols).astype(f32)


def per_device(
    tokens, timesteps, lengths, time_table, w_ada, b_ada, gain_attn, w_qkv, w_out, gain_mlp, w_up, b_up,
    w_down, b_down, grad_out
):
    rows_dev, stretch, width = tokens.shape
    nblk, nrows = lax.axis_size("blk"), lax.axis_size("rows")
    blk, row = lax.axis_index("blk"), lax.axis_index("rows")
    seq = stretch * nblk

    x_blocks, g_blocks, hidden_t, q, k, v, cosine, sine, attended, inv, attended_b, eb, vec = ahead(
        tokens, grad_out, w_qkv, w_ada, lengths, timesteps, time_table, b_ada, gain_attn, gain_mlp, b_down, b_up, nblk
    )
    x_row = x_blocks.reshape(seq, width)

    ff = b_up.shape[0]
    fed = (attended_b, x_row, g_blocks.reshape(seq, width), vec, w_out, w_up, w_down)

    if (nblk, nrows) == (4, 8):
        f = feed_move(*fed, nrows)
        nz, share = nrows // 2, width // nrows
        o = behind(
            q, k, v, f["datt"], attended, inv, eb, cosine, sine, w_qkv, hidden_t, x_blocks, f["dx"], vec, f["early"],
            {name: value for name, value in f.items() if "." in name}, f["g_out"].reshape(nz, 2, share, width),
            f["result"].reshape(nblk, stretch, width), rows_dev, nrows,
        )
        out, grad_tokens, *rest = finish(o, time_table, w_ada)
        flat = (2, 3, 6, 8, 10)
        return (out, grad_tokens, *(value.reshape(-1) if i in flat else value for i, value in enumerate(rest)))

    shift_a, scale_a, gate_a, shift_m, scale_m, gate_m, factor_a, factor_m, gain_a, gain_m, step = vec[:11]
    result, grad_mid, grad_att, grad_w_out, grad_w_up, grad_w_down, gb_up, sums = feed(*fed)
    dgate_m, dshift_m, along_m, dgate_a, grad_b_down = (sums[i] for i in range(5))
    out = rows_out(result.reshape(nblk, stretch, width), rows_dev, blk, nblk)
    share_w_down = reduce_weight(grad_w_down.transpose(2, 0, 1, 3).reshape(width, ff).T, blk, row, nblk, nrows)
    share_w_up = reduce_weight(grad_w_up.transpose(1, 0, 2).reshape(width, ff), blk, row, nblk, nrows)
    share_w_out = reduce_weight(grad_w_out, blk, row, nblk, nrows)
    dq, dk, dv = attend_back(q, k, v, grad_att, attended, inv, eb, cosine, sine)
    grad_qkv = jnp.concatenate([dq, dk, dv], axis=-1)
    grad_w_qkv = dot(hidden_t, grad_qkv).astype(bf16)
    share_w_qkv = reduce_weight(grad_w_qkv, blk, row, nblk, nrows)
    grad_ha = dot_nt(grad_qkv, w_qkv)
    normed_a, inverse_a = norm_rows(x_row.astype(f32))
    along_a = jnp.sum(grad_ha * normed_a, axis=0)
    grad_in = (grad_mid + norm_back(grad_ha * factor_a, normed_a, inverse_a)).astype(bf16)
    grad_tokens = rows_out(grad_in.reshape(nblk, stretch, width), rows_dev, blk, nblk)
    count = 6 * width + ff + LANES
    packed = jnp.concatenate(
        [
            dgate_a, dshift_m, along_m * gain_m, dgate_m, along_m * (1.0 + scale_m), grad_b_down, gb_up[0],
            step[:LANES], jnp.sum(grad_ha, axis=0), along_a * gain_a, along_a * (1.0 + scale_a),
        ]
    )
    gathered = gather_all(packed, nblk, nrows).reshape(nblk, nrows, -1)
    early = gathered[:rows_dev].reshape(rows_dev * nrows, -1)
    dshift_a, dscale_a, part_gain_a = (early[:, count + i * width : count + (i + 1) * width] for i in range(3))

    table, ada_full = time_table.astype(f32), w_ada.astype(f32)
    grad_mod = jnp.concatenate([dshift_a, dscale_a, early[:, : 4 * width]], axis=-1)
    smalls = jnp.sum(early, axis=0)
    grad_gain_m, total_b_down = smalls[4 * width : 5 * width], smalls[5 * width : 6 * width]
    total_b_up = smalls[6 * width : 6 * width + ff]
    steps = early[:, 6 * width + ff].astype(jnp.int32)
    onehot = (steps[:, None] == jnp.arange(table.shape[0], dtype=jnp.int32)[None, :]).astype(f32)
    conds = jnp.dot(onehot, table, precision=highest)
    share = conds.shape[1] // nrows
    my_conds = lax.dynamic_slice_in_dim(conds, row * share, share, axis=1)
    grad_w_ada = jnp.dot(jax.nn.silu(my_conds).T, grad_mod, precision=highest)
    grad_cond_act = lax.dot_general(
        grad_mod, ada_full, (((1,), (1,)), ((), ())), precision=highest, preferred_element_type=f32
    )
    sigmoid = jax.nn.sigmoid(conds)
    grad_cond = grad_cond_act * sigmoid * (1.0 + conds * (1.0 - sigmoid))
    grad_table = jnp.dot(onehot.T, grad_cond, precision=highest)
    return (
        out,
        grad_tokens,
        grad_table,
        grad_w_ada,
        jnp.sum(grad_mod, axis=0),
        jnp.sum(part_gain_a, axis=0),
        share_w_qkv,
        share_w_out,
        grad_gain_m,
        share_w_up,
        total_b_up,
        share_w_down,
        total_b_down,
    )


def solution(mesh):
    whole, split = P(), P("rows", None)
    tokens = P("rows", "blk", None)
    return jax.shard_map(
        per_device,
        mesh=mesh,
        in_specs=(tokens, P("rows"), split) + (whole,) * 11 + (tokens,),
        out_specs=(
            tokens, tokens, whole, split, whole, whole, split, split, whole, split, whole, split, whole
        ),
        check_vma=False,
    )
```

time: 461 us -> 242 us (0.52)
  local copies, waits for them, and re-layouts: 88.8 us -> 0 us
  starting transfers between devices: 64.8 us -> 0 us
  Pallas kernels: 173 us -> 237 us
  waiting for transfers between devices: 58.4 us -> 0 us
  other arithmetic: 49.2 us -> 0 us
  matrix products: 17.1 us -> 0 us
    ppermute x50 -> x0, starting transfers between devices: 64.8 us -> none  [the longest x44 47.3 us: xor_move(): return lax.ppermute(array, axis, [(s, s ^ k) for s in range(size)])]
    pallas_call x4, Pallas kernels: 173 us -> 237 us  [the longest x1 111 us: behind(): pl.pallas_call(functools.partial(behind_kernel, ins.names + outs.names +...]
    ppermute x50 -> x0, waiting for transfers between devices: 58.4 us -> none  [the longest x44 58.4 us: xor_move(): return lax.ppermute(array, axis, [(s, s ^ k) for s in range(size)])]
    unnamed x95 -> x0, local copies, waits for them, and re-layouts: 33.7 us -> none
    convert_element_type x34 -> x0, other arithmetic: 23.8 us -> none  [the longest x20 15 us: halve(): return (kept + xor_move(sent, name, size, k).astype(f32)).astype(bf16)]
    dot_general x7 -> x0, matrix products: 17.1 us -> none  [the longest x1 6.63 us: dot(): return jnp.dot(a, b, preferred_element_type=f32)]
    dynamic_slice x4 -> x0, local copies, waits for them, and re-layouts: 16 us -> none  [the longest x2 13.6 us: pick(): return lax.dynamic_index_in_dim(array, index, axis, keepdims=False)]
    gather x6 -> x0, local copies, waits for them, and re-layouts: 11.9 us -> none  [the longest x2 6.16 us: rows_out(): return jnp.take(stacked, jnp.arange(rows) ^ me, axis=0)]
  transfers between devices with their start and end apart: 50 -> 0, of which waited for: 17 -> 0; matrix products, arithmetic and copies ran while one was open for 26% -> 0% of each run, Pallas kernels for 7% -> 0%
where the time goes in v4:
time: 242 us; the launch traced here: 238 us
  Pallas kernels  237 us (98%)
    pallas_call x1, Pallas kernels, behind(): pl.pallas_call(functools.partial(behind_kernel, ins.names + outs.names +...  111 us
    pallas_call x1, Pallas kernels, feed_move(): pl.pallas_call(functools.partial(feed_move_kernel, ins.names + outs.names...  73.8 us
    pallas_call x1, Pallas kernels, ahead(): pl.pallas_call(ahead_kernel, grid=(width // LANES,), in_specs=[away] * 4...  45.8 us
    pallas_call x1, Pallas kernels, finish(): pl.pallas_call(functools.partial(finish_kernel, names + outs.names + scra...  6 us

profile of v4, /device:TPU:0, one launch (start us, length us, event | category | flops | bytes accessed | tf_op | source)
XLA Modules:
  0.0 237.7 jit_solution(10879139744607894155)
XLA Ops:
  0.6 45.8 %shard_map.255 = (bf16[4,256,768]{2,1,0:T(8,128)(2,1)}, bf16[4,256,768]{2,1,0:T(8,128)(2,1)}, bf16[768,1024]{1,0:T(8,128)(2,1)}, bf16[1024,768]{1,0:T(8,128)(2,1...) custom-call(bf16[3,256,768]{2,1,0:T(8,128)(2,1)} %tok_ref.1, ...), custom_call_target="tpu_custom_call" | custom-call | flops 17716740096 | bytes 18874368 | tf_op jit(solution)/shard_map/pallas_call | solution.py:310
  46.5 73.8 %shard_map.256 = (bf16[1024,768]{1,0:T(8,128)(2,1)}, f32[1024,768]{1,0:T(8,128)}, bf16[1024,768]{1,0:T(8,128)(2,1)}, bf16[768,768]{1,0:T(8,128)(2,1)}, bf16[64,1...) custom-call(bf16[1024,768]{1,0:T(8,128)(2,1)} %get-tuple-element.65., ...), custom_call_target="tpu_custom_call" | custom-call | flops 28991029248 | bytes 23592960 | tf_op jit(solution)/shard_map/pallas_call | solution.py:1110
  120.4 111.1 %shard_map.257 = (bf16[3,256,768]{2,1,0:T(8,128)(2,1)}, bf16[3,256,768]{2,1,0:T(8,128)(2,1)}, bf16[96,2304]{1,0:T(8,128)(2,1)}, bf16[96,768]{1,0:T(8,128)(2,1)},...) custom-call(bf16[1024,768]{1,0:T(8,128)(2,1)} %get-tuple-element.62., ...), custom_call_target="tpu_custom_call" | custom-call | flops 41875931136 | bytes 31457280 | tf_op jit(solution)/shard_map/pallas_call | solution.py:1410
  231.5 6.0 %shard_map.258 = (bf16[3,256,768]{2,1,0:T(8,128)(2,1)}, bf16[3,256,768]{2,1,0:T(8,128)(2,1)}, f32[64,128]{1,0:T(8,128)}, f32[16,4608]{1,0:T(8,128)}, f32[36,128]...) custom-call(bf16[3,256,768]{2,1,0:T(8,128)(2,1)} %get-tuple-element., ...), custom_call_target="tpu_custom_call" | custom-call | tf_op jit(solution)/shard_map/pallas_call | solution.py:1527

commit v5 on v4

--- a/solution.py
+++ b/solution.py
@@ -1302,18 +1302,18 @@
             def sent():
                 piece.run(0)
 
-        for rows in (slice(begin, begin + CHUNK) for begin in range(0, seq, CHUNK)):
+        @pl.when(number == 0)
+        def fresh():
+            r.dh[...] = jnp.zeros_like(r.dh)
+
+        def onto(begin, unused):
+            rows = part(begin, CHUNK, CHUNK)
             added = dot_nt(r.dqkv[rows, : 2 * LANES], r.wq[...])
             added = added + dot_nt(r.dqkv[rows, 2 * LANES : 4 * LANES], r.wk[...])
-            added = added + dot_nt(r.dqkv[rows, 4 * LANES :], r.wv[...])
-
-            @pl.when(number == 0)
-            def fresh():
-                r.dh[rows, :] = added
-
-            @pl.when(number > 0)
-            def more():
-                r.dh[rows, :] += added
+            r.dh[rows, :] += added + dot_nt(r.dqkv[rows, 4 * LANES :], r.wv[...])
+            return unused
+
+        lax.fori_loop(0, seq // CHUNK, onto, 0)
 
     @pl.when(step == last)
     def tail():

time: 242 us -> 239 us (0.988)
  Pallas kernels: 237 us -> 234 us
where the time goes in v5:
time: 239 us; the launch traced here: 235 us
  Pallas kernels  234 us (98%)
    pallas_call x1, Pallas kernels, behind(): pl.pallas_call(functools.partial(behind_kernel, ins.names + outs.names +...  109 us
    pallas_call x1, Pallas kernels, feed_move(): pl.pallas_call(functools.partial(feed_move_kernel, ins.names + outs.names...  72.8 us
    pallas_call x1, Pallas kernels, ahead(): pl.pallas_call(ahead_kernel, grid=(width // LANES,), in_specs=[away] * 4...  45.8 us
    pallas_call x1, Pallas kernels, finish(): pl.pallas_call(functools.partial(finish_kernel, names + outs.names + scra...  6 us

profile of v5, /device:TPU:0, one launch (start us, length us, event | category | flops | bytes accessed | tf_op | source)
XLA Modules:
  0.0 234.8 jit_solution(5383730567135499590)
XLA Ops:
  0.6 45.8 %shard_map.255 = (bf16[4,256,768]{2,1,0:T(8,128)(2,1)}, bf16[4,256,768]{2,1,0:T(8,128)(2,1)}, bf16[768,1024]{1,0:T(8,128)(2,1)}, bf16[1024,768]{1,0:T(8,128)(2,1...) custom-call(bf16[3,256,768]{2,1,0:T(8,128)(2,1)} %tok_ref.1, ...), custom_call_target="tpu_custom_call" | custom-call | flops 17716740096 | bytes 18874368 | tf_op jit(solution)/shard_map/pallas_call | solution.py:310
  46.5 72.8 %shard_map.256 = (bf16[1024,768]{1,0:T(8,128)(2,1)}, f32[1024,768]{1,0:T(8,128)}, bf16[1024,768]{1,0:T(8,128)(2,1)}, bf16[768,768]{1,0:T(8,128)(2,1)}, bf16[64,1...) custom-call(bf16[1024,768]{1,0:T(8,128)(2,1)} %get-tuple-element.65., ...), custom_call_target="tpu_custom_call" | custom-call | flops 28991029248 | bytes 23592960 | tf_op jit(solution)/shard_map/pallas_call | solution.py:1110
  119.3 109.2 %shard_map.257 = (bf16[3,256,768]{2,1,0:T(8,128)(2,1)}, bf16[3,256,768]{2,1,0:T(8,128)(2,1)}, bf16[96,2304]{1,0:T(8,128)(2,1)}, bf16[96,768]{1,0:T(8,128)(2,1)},...) custom-call(bf16[1024,768]{1,0:T(8,128)(2,1)} %get-tuple-element.62., ...), custom_call_target="tpu_custom_call" | custom-call | flops 41875931136 | bytes 31457280 | tf_op jit(solution)/shard_map/pallas_call | solution.py:1410
  228.5 6.0 %shard_map.258 = (bf16[3,256,768]{2,1,0:T(8,128)(2,1)}, bf16[3,256,768]{2,1,0:T(8,128)(2,1)}, f32[64,128]{1,0:T(8,128)}, f32[16,4608]{1,0:T(8,128)}, f32[36,128]...) custom-call(bf16[3,256,768]{2,1,0:T(8,128)(2,1)} %get-tuple-element., ...), custom_call_target="tpu_custom_call" | custom-call | tf_op jit(solution)/shard_map/pallas_call | solution.py:1527

commit v6 on v5

--- a/solution.py
+++ b/solution.py
@@ -655,6 +655,13 @@
         for copy in self.copies(stage):
             copy.wait()
 
+    def take_own(self):
+        def onto(i, unused):
+            self.b.core[i] = self.b.core[i] + self.own(i)
+            return unused
+
+        lax.fori_loop(0, self.b.core.shape[0], onto, 0)
+
     def run(self, stage, go_on=True):
         if stage:
             self.wait(stage - 1)
@@ -717,7 +724,7 @@
         p, b = self.p, self.b
         row, col = self.row(p.y), self.col(p.x)
         if stage == 1:
-            b.core[...] = b.core[...] + self.own()
+            self.take_own()
         if stage == 2:
             b.a1[...] = b.a1[...] + b.core[: self.hz, :, col]
             b.b1[...] = b.b1[...] + b.core[self.hz :, row, :]
@@ -772,7 +779,7 @@
         p, b = self.p, self.b
         low, high = p.z % 2, p.z // 2
         if stage == 1:
-            b.core[...] = b.core[...] + self.own()
+            self.take_own()
         if stage == 2:
             for i in range(2):
                 b.z1[i] = b.z1[i] + b.core[2 * i + low]
@@ -864,7 +871,7 @@
     def add(self, stage):
         p, b = self.p, self.b
         if stage == 1:
-            b.core[...] = b.core[...] + self.own()
+            self.take_own()
         if stage == 2:
             b.a1[...] = b.a1[...] + b.core[:, p.x, 0]
             b.b1[...] = b.b1[...] + b.core[p.y, :, 1]
@@ -962,14 +969,14 @@
         ups.append(
             RowPiece(
                 place, sems, (nz, share, cols), group(r, f"u{i}"), r.gu.at[side],
-                lambda side=side: r.gu[side, :, place.core],
+                lambda i, side=side: r.gu[side, i, place.core],
             )
         )
         bufs = group(r, f"d{i}")
         downs.append(
             ColPiece(
                 place, sems, (nz, depth, dcols), bufs, i, whole=r.gd.at[side],
-                own=lambda side=side: r.gd[side, place.core],
+                own=lambda i, side=side: r.gd[side, place.core, i],
             )
         )
     for i, points in enumerate(FEED_POINTS):
@@ -1240,12 +1247,12 @@
             )
             carried.append((len(points) + 1, up, down))
     outer = RowPiece(
-        place, sems, dims, group(r, "o"), r.g_out, lambda: r.own_out[...], store_at(r.share_out, 0)
+        place, sems, dims, group(r, "o"), r.g_out, lambda i: r.own_out[i], store_at(r.share_out, 0)
     )
     load = pltpu.make_async_copy(r.g_out.at[:, place.core], r.own_out, r.local.at[2])
     late_pieces = [
         kind(
-            place, sems, dims, group(r, f"q{j}"), r.gq.at[j], lambda j=j: r.gq[j, :, place.core], store_qkv(j)
+            place, sems, dims, group(r, f"q{j}"), r.gq.at[j], lambda i, j=j: r.gq[j, i, place.core], store_qkv(j)
         )
         for j, kind in enumerate((RowPiece, RowPiece, RowPiece))
     ]

time: 239 us -> 239 us (level)
  no operation moved by 1% of the time
where the time goes in v6:
time: 239 us; the launch traced here: 235 us
  Pallas kernels  234 us (98%)
    pallas_call x1, Pallas kernels, behind(): pl.pallas_call(functools.partial(behind_kernel, ins.names + outs.names +...  109 us
    pallas_call x1, Pallas kernels, feed_move(): pl.pallas_call(functools.partial(feed_move_kernel, ins.names + outs.names...  72.8 us
    pallas_call x1, Pallas kernels, ahead(): pl.pallas_call(ahead_kernel, grid=(width // LANES,), in_specs=[away] * 4...  45.8 us
    pallas_call x1, Pallas kernels, finish(): pl.pallas_call(functools.partial(finish_kernel, names + outs.names + scra...  6 us

profile of v6, /device:TPU:0, one launch (start us, length us, event | category | flops | bytes accessed | tf_op | source)
XLA Modules:
  0.0 234.7 jit_solution(18054334816208168978)
XLA Ops:
  0.6 45.8 %shard_map.255 = (bf16[4,256,768]{2,1,0:T(8,128)(2,1)}, bf16[4,256,768]{2,1,0:T(8,128)(2,1)}, bf16[768,1024]{1,0:T(8,128)(2,1)}, bf16[1024,768]{1,0:T(8,128)(2,1...) custom-call(bf16[3,256,768]{2,1,0:T(8,128)(2,1)} %tok_ref.1, ...), custom_call_target="tpu_custom_call" | custom-call | flops 17716740096 | bytes 18874368 | tf_op jit(solution)/shard_map/pallas_call | solution.py:310
  46.5 72.8 %shard_map.256 = (bf16[1024,768]{1,0:T(8,128)(2,1)}, f32[1024,768]{1,0:T(8,128)}, bf16[1024,768]{1,0:T(8,128)(2,1)}, bf16[768,768]{1,0:T(8,128)(2,1)}, bf16[64,1...) custom-call(bf16[1024,768]{1,0:T(8,128)(2,1)} %get-tuple-element.65., ...), custom_call_target="tpu_custom_call" | custom-call | flops 28991029248 | bytes 23592960 | tf_op jit(solution)/shard_map/pallas_call | solution.py:1117
  119.3 109.2 %shard_map.257 = (bf16[3,256,768]{2,1,0:T(8,128)(2,1)}, bf16[3,256,768]{2,1,0:T(8,128)(2,1)}, bf16[96,2304]{1,0:T(8,128)(2,1)}, bf16[96,768]{1,0:T(8,128)(2,1)},...) custom-call(bf16[1024,768]{1,0:T(8,128)(2,1)} %get-tuple-element.62., ...), custom_call_target="tpu_custom_call" | custom-call | flops 41875931136 | bytes 31457280 | tf_op jit(solution)/shard_map/pallas_call | solution.py:1417
  228.5 6.0 %shard_map.258 = (bf16[3,256,768]{2,1,0:T(8,128)(2,1)}, bf16[3,256,768]{2,1,0:T(8,128)(2,1)}, f32[64,128]{1,0:T(8,128)}, f32[16,4608]{1,0:T(8,128)}, f32[36,128]...) custom-call(bf16[3,256,768]{2,1,0:T(8,128)(2,1)} %get-tuple-element., ...), custom_call_target="tpu_custom_call" | custom-call | tf_op jit(solution)/shard_map/pallas_call | solution.py:1534
